TPU v7x, 32 devices: a whole 2x2x4 slice. The times are simulated.
32 devices in a mesh: groups: 2 (over y), px: 16 (over z, x, core).
Axes of the slice: x: 2, y: 2, z: 4, core: 2. Of those that a mesh axis runs over, the one named last changes fastest.
Arguments:
- right_side: float32 [262144], P(('groups', 'px')), parts along dimension 0, may hold values from -36 to 36
- self_term: float32 [262144], P(('groups', 'px')), parts along dimension 0, may hold values from 1 to 4
- proj_tiles: float32 [4096, 64, 128], P(('groups', 'px')), parts along dimension 0, may hold values from -0.75 to 0.75
- owner_dev: int32 [4096, 1], P(('groups', 'px')), parts along dimension 0, may hold values from 0 to 15; in each aligned block of 128 rows (0 to 127, 128 to 255, ...) at most 16 rows name the same one
- cube_slot: int32 [4096], P(('groups', 'px')), parts along dimension 0, may hold values from 0 to 8191
- near_src: int32 [4096, 2], P(('groups', 'px')), parts along dimension 0, may hold values from 0 to 191
- near_tiles: float32 [4096, 64, 128], P(('groups', 'px')), parts along dimension 0, may hold values from -0.5 to 0.5
- kernel_hat: float32 [256, 256, 256], P(None, 'px'), may hold values from 0.2 to 2, as said below
Outputs:
- solution: float32 [262144], P(('groups', 'px')), parts along dimension 0
- residual: float32 [262144], P(('groups', 'px')), parts along dimension 0
There are 2 independent parts, one for each index of `groups`. A program takes and returns all parts, laid end to end along the dimension named above; an argument that names none is the same for every part. Nothing has to cross between parts.
Inputs may be any that keep to these rules, and one draw needn't show every extreme that they name: `owner_dev`: among the blocks of one device at most 16 have the same owner, and some device has 16 blocks of one owner. kernel_hat at frequency (k0, k1, k2) equals kernel_hat at ((-k0) mod 256, (-k1) mod 256, (-k2) mod 256).
All inputs are finite; a program needn't handle non-finite values.
Results may differ from a plain program's by a relative error of at most 0.0002.
Values sent between devices are 32-bit elements; how exact they have to be, the bound alone decides.
No kernel may reach another device: no remote copies, remote signals or barrier semaphores. Data moves between devices by JAX's collectives and lax.ppermute only.
A program may use at most 256 MiB of HBM per device.

v0:
```python
import jax
import jax.numpy as jnp
from jax import lax
from jax.sharding import PartitionSpec as P


def padded(cells, sides, width):
    for axis, dim in sides:
        count = lax.axis_size(axis)
        ends = count - 1
        head = lax.slice_in_dim(cells, 0, width, axis=dim)
        tail = lax.slice_in_dim(cells, cells.shape[dim] - width, cells.shape[dim], axis=dim)
        cells = jnp.concatenate(
            [
                lax.ppermute(tail, axis, [(i, (i + 1) % count) for i in range(ends)]),
                cells,
                lax.ppermute(head, axis, [((i + 1) % count, i) for i in range(ends)]),
            ],
            axis=dim,
        )
    return cells


def product(pattern, matrix, second):
    return jnp.einsum(pattern, matrix, second, precision=lax.Precision.HIGHEST)


def cube_layout(volume):
    planes = volume.shape[0]
    extent = volume.shape[1]
    shaped = volume.reshape(planes, extent // 8, 8, extent // 16, 16)
    return shaped.transpose(0, 1, 3, 2, 4).reshape(planes * (extent // 8) * (extent // 16), 128)


def grid_layout(cubed, planes, extent):
    shaped = cubed.reshape(planes, extent // 8, extent // 16, 8, 16)
    return shaped.transpose(0, 1, 3, 2, 4).reshape(planes, extent, extent)


def tables(extent):
    row_index = lax.broadcasted_iota(jnp.int32, (extent, extent), 0)
    col_index = lax.broadcasted_iota(jnp.int32, (extent, extent), 1)
    phase_angle = 2.0 * jnp.pi / extent * (row_index * col_index % extent).astype(jnp.float32)
    return (jnp.cos(phase_angle), jnp.sin(phase_angle))


def forward(real_in, imag_in, cosine_table, sine_table, pattern):
    real_out = product(pattern, real_in, cosine_table) + product(pattern, imag_in, sine_table)
    imag_out = product(pattern, imag_in, cosine_table) - product(pattern, real_in, sine_table)
    return (real_out, imag_out)


def inverse(real_in, imag_in, cosine_table, sine_table, pattern):
    real_out = product(pattern, real_in, cosine_table) - product(pattern, imag_in, sine_table)
    imag_out = product(pattern, imag_in, cosine_table) + product(pattern, real_in, sine_table)
    return (real_out, imag_out)


def convolve_even(charge_grid, kernel_local, cosine_table, sine_table, norm_scale):
    extent = charge_grid.shape[1]
    half_len = extent // 2
    cosine_half = cosine_table[:, :half_len]
    sine_half = sine_table[:, :half_len]
    parity = 1.0 - 2.0 * (jnp.arange(extent, dtype=jnp.int32) % 2).astype(jnp.float32)
    first_real = product("pjk,kl->pjl", charge_grid, cosine_half)
    first_imag = -product("pjk,kl->pjl", charge_grid, sine_half)
    nyquist = product("pjk,k->pj", charge_grid, parity)
    second_real, second_imag = forward(
        first_real, first_imag, cosine_table, sine_table, "pjl,jm->pml"
    )
    nyquist_real = product("pj,jm->pm", nyquist, cosine_table)
    nyquist_imag = -product("pj,jm->pm", nyquist, sine_table)
    arrived = (
        lax.all_to_all(second_real, "px", split_axis=1, concat_axis=0, tiled=True),
        lax.all_to_all(second_imag, "px", split_axis=1, concat_axis=0, tiled=True),
        lax.all_to_all(nyquist_real, "px", split_axis=1, concat_axis=0, tiled=True),
        lax.all_to_all(nyquist_imag, "px", split_axis=1, concat_axis=0, tiled=True),
    )
    third_real, third_imag = forward(
        arrived[0], arrived[1], cosine_table, sine_table, "jml,jn->nml"
    )
    edge_real, edge_imag = forward(arrived[2], arrived[3], cosine_table, sine_table, "jm,jn->nm")
    kernel_main = kernel_local[:, :, :half_len]
    kernel_edge = kernel_local[:, :, half_len]
    fourth_real, fourth_imag = inverse(
        third_real * kernel_main, third_imag * kernel_main, cosine_table, sine_table, "nml,nj->jml"
    )
    edge_back_real, edge_back_imag = inverse(
        edge_real * kernel_edge, edge_imag * kernel_edge, cosine_table, sine_table, "nm,nj->jm"
    )
    returned = (
        lax.all_to_all(fourth_real, "px", split_axis=0, concat_axis=1, tiled=True),
        lax.all_to_all(fourth_imag, "px", split_axis=0, concat_axis=1, tiled=True),
        lax.all_to_all(edge_back_real, "px", split_axis=0, concat_axis=1, tiled=True),
        lax.all_to_all(edge_back_imag, "px", split_axis=0, concat_axis=1, tiled=True),
    )
    fifth_real, fifth_imag = inverse(
        returned[0], returned[1], cosine_table, sine_table, "pml,mj->pjl"
    )
    edge_final = product("pm,mj->pj", returned[2], cosine_table) - product(
        "pm,mj->pj", returned[3], sine_table
    )
    doubling = jnp.where(jnp.arange(half_len) == 0, 1.0, 2.0).astype(jnp.float32)
    result = product("pjl,kl->pjk", fifth_real, cosine_half * doubling[None, :])
    result = result - product("pjl,kl->pjk", fifth_imag, sine_half * doubling[None, :])
    result = result + edge_final[:, :, None] * parity[None, None, :]
    return result * norm_scale


def on_device(
    right_side, self_term, proj_tiles, owner_dev, cube_slot, near_src, near_tiles, kernel_hat
):
    members = lax.axis_size("px")
    blocks = proj_tiles.shape[0]
    extent = kernel_hat.shape[0]
    planes = extent // members
    capacity = max(2, 2 * blocks // members)
    slot_count = members * capacity
    rim_width = blocks // 4
    cube_count = planes * (extent // 8) * (extent // 16)
    owners = owner_dev[:, 0]
    same_owner = owners[:, None] == owners[None, :]
    earlier = lax.broadcasted_iota(jnp.int32, (blocks, blocks), 1) < lax.broadcasted_iota(
        jnp.int32, (blocks, blocks), 0
    )
    position = jnp.sum((same_owner & earlier).astype(jnp.int32), axis=1)
    send_slot = owners * capacity + position
    slot_table = send_slot[:, None] == jnp.arange(slot_count, dtype=jnp.int32)[None, :]
    send_onehot = slot_table.astype(jnp.float32)
    send_ids = jnp.max(jnp.where(slot_table, cube_slot[:, None], -1), axis=0)
    arrived_ids = lax.all_to_all(send_ids, "px", split_axis=0, concat_axis=0, tiled=True)
    recv_onehot = (jnp.arange(cube_count, dtype=jnp.int32)[:, None] == arrived_ids[None, :]).astype(
        jnp.float32
    )
    cosine_table, sine_table = tables(extent)
    norm_scale = 1.0 / float(extent) ** 3
    self_local = self_term.reshape(blocks, 64)

    def operator(values):
        charges = product("bpc,bp->bc", proj_tiles, values)
        outgoing = product("bs,bc->sc", send_onehot, charges)
        incoming = lax.all_to_all(outgoing, "px", split_axis=0, concat_axis=0, tiled=True)
        cubed = product("ks,sc->kc", recv_onehot, incoming)
        charge_grid = grid_layout(cubed, planes, extent)
        far_grid = convolve_even(charge_grid, kernel_hat, cosine_table, sine_table, norm_scale)
        reply = product("ks,kc->sc", recv_onehot, cube_layout(far_grid))
        returned = lax.all_to_all(reply, "px", split_axis=0, concat_axis=0, tiled=True)
        picked = product("bs,sc->bc", send_onehot, returned)
        far_part = product("bpc,bc->bp", proj_tiles, picked)
        extended = padded(values, (("px", 0),), rim_width)
        sources = extended[near_src].reshape(blocks, near_tiles.shape[2])
        near_part = product("bpj,bj->bp", near_tiles, sources)
        return self_local * values + near_part + far_part

    rhs_blocks = right_side.reshape(blocks, 64)
    initial_norm = jnp.sqrt(lax.psum(jnp.sum(rhs_blocks * rhs_blocks), "px"))
    basis_one = rhs_blocks / initial_norm
    image_one = operator(basis_one)
    diag_one = lax.psum(jnp.sum(basis_one * image_one), "px")
    rest_one = image_one - diag_one * basis_one
    sub_one = jnp.sqrt(lax.psum(jnp.sum(rest_one * rest_one), "px"))
    basis_two = rest_one / sub_one
    image_two = operator(basis_two)
    upper_two = lax.psum(jnp.sum(basis_one * image_two), "px")
    rest_middle = image_two - upper_two * basis_one
    diag_two = lax.psum(jnp.sum(basis_two * rest_middle), "px")
    rest_two = rest_middle - diag_two * basis_two
    sub_two_sq = lax.psum(jnp.sum(rest_two * rest_two), "px")
    gram_one = diag_one * diag_one + sub_one * sub_one
    gram_cross = diag_one * upper_two + sub_one * diag_two
    gram_two = upper_two * upper_two + diag_two * diag_two + sub_two_sq
    determinant = gram_one * gram_two - gram_cross * gram_cross
    weight_one = initial_norm * (diag_one * gram_two - upper_two * gram_cross) / determinant
    weight_two = initial_norm * (upper_two * gram_one - diag_one * gram_cross) / determinant
    solution = weight_one * basis_one + weight_two * basis_two
    residual = rhs_blocks - weight_one * image_one - weight_two * image_two
    return (solution.reshape(blocks * 64), residual.reshape(blocks * 64))


def solution(mesh):
    return jax.shard_map(
        on_device,
        mesh=mesh,
        in_specs=(
            P(("groups", "px")),
            P(("groups", "px")),
            P(("groups", "px"), None, None),
            P(("groups", "px"), None),
            P(("groups", "px")),
            P(("groups", "px"), None),
            P(("groups", "px"), None, None),
            P(None, "px", None),
        ),
        out_specs=(P(("groups", "px")), P(("groups", "px"))),
        check_vma=False,
    )
```

profile of v0, /device:TPU:0, one launch (start us, length us, event | category | flops | bytes accessed | tf_op | source)
XLA Modules:
  0.0 1180.0 jit_solution(6323953302737870807)
XLA Ops:
  3.7 7.4 all-to-all-start
  13.2 34.5 %psum.42 = f32[]{:T(128)} all-reduce(f32[]{:T(128)} %multiply_reduce_fusion.5), channel_id=1, replica_groups=mesh['groups'=2,'px'=16] {'px'}, use_global_device_ids=true, to_apply=%region_1.2 | all-reduce | flops 1 | bytes 8 | tf_op jit(solution)/shard_map/psum | solution.py:156
  66.5 17.3 %convolution_bitcast_fusion.1 = f32[16,32,8,16,16]{4,3,2,1,0:T(8,128)} fusion(f32[8,16,256,1,1]{2,1,0,4,3:T(8,128)S(1)} %bitcast.403, s32[256]{0:T(256)S(1)} %eq.110, s32[16,32,16]{2,1,0:T(8,128)S(1)} %multiply_add_fusion), kind=kOutput, calls=%fused_computation.3 | convolution fusion | flops 3223322624 | bytes 4359168 | tf_op jit(solution)/shard_map/ks,sc->kc/dot_general | solution.py:25
  83.7 23.5 %reshape.176 = f32[16,256,256]{2,1,0:T(8,128)} reshape(f32[16,32,8,16,16]{4,3,2,1,0:T(8,128)} %convolution_bitcast_fusion.1) | data formatting | bytes 8388608 | tf_op jit(solution)/shard_map/reshape | solution.py:37
  134.0 6.5 all-to-all-start.6
  147.5 6.2 all-to-all-start.3
  163.5 31.3 %all-to-all-done.3 = f32[16,256,128]{2,0,1:T(8,128)} async-done(((f32[16,256,128]{2,0,1:T(8,128)}), f32[16,256,128]{2,0,1:T(8,128)}, u32[]{:S(2)}, u32[]{:S(2)}) %all-to-all-start.3) | async-done | bytes 2097184 | tf_op jit(solution)/shard_map/all_to_all | solution.py:75
  194.8 11.4 all-to-all-start.2
  233.7 13.5 %all-to-all-done.2 = f32[16,256,128]{2,0,1:T(8,128)} async-done(((f32[16,256,128]{2,0,1:T(8,128)}), f32[16,256,128]{2,0,1:T(8,128)}, u32[]{:S(2)}, u32[]{:S(2)}) %all-to-all-start.2) | async-done | bytes 2097184 | tf_op jit(solution)/shard_map/all_to_all | solution.py:74
  247.2 11.2 all-to-all-start.9
  276.0 6.0 all-to-all-start.8
  289.7 6.1 all-to-all-start.5
  305.9 31.1 %all-to-all-done.5 = f32[256,16,128]{2,1,0:T(8,128)} async-done(((f32[256,16,128]{2,1,0:T(8,128)}), f32[256,16,128]{2,1,0:T(8,128)}, u32[]{:S(2)}, u32[]{:S(2)}) %all-to-all-start.5) | async-done | bytes 2097184 | tf_op jit(solution)/shard_map/all_to_all | solution.py:93
  337.0 11.3 all-to-all-start.4
  370.2 19.2 %all-to-all-done.4 = f32[256,16,128]{2,1,0:T(8,128)} async-done(((f32[256,16,128]{2,1,0:T(8,128)}), f32[256,16,128]{2,1,0:T(8,128)}, u32[]{:S(2)}, u32[]{:S(2)}) %all-to-all-start.4) | async-done | bytes 2097184 | tf_op jit(solution)/shard_map/all_to_all | solution.py:92
  406.1 19.4 %reshape.177 = f32[16,32,8,16,16]{4,3,2,1,0:T(8,128)} reshape(f32[16,256,256]{2,1,0:T(8,128)} %add_multiply_fusion.1) | data formatting | bytes 8388608 | tf_op jit(solution)/shard_map/reshape | solution.py:31
  425.5 29.9 %copy.268 = f32[16,32,16,8,16]{4,3,2,1,0:T(8,128)} copy(f32[16,32,16,8,16]{4,2,3,1,0:T(8,128)} %bitcast.380) | data formatting | bytes 8388608 | tf_op jit(solution)/shard_map/transpose | solution.py:32
  455.4 21.4 %reshape.235 = f32[8192,128,1]{1,0,2:T(8,128)} reshape(f32[16,32,16,8,16]{4,3,2,1,0:T(8,128)} %copy.268) | data formatting | bytes 8388608 | tf_op jit(solution)/shard_map/reshape | solution.py:32
  476.8 7.4 fusion.444
  484.2 25.9 %all-to-all-start.10 = ((f32[16,16,128]{2,1,0:T(8,128)}), f32[16,16,128]{2,1,0:T(8,128)S(1)}, u32[]{:S(2)}, u32[]{:S(2)}) async-start(f32[16,16,128]{2,1,0:T(8,128)} %fusion.444), calls=%async_computation.10 | async-start | bytes 262144 | tf_op jit(solution)/shard_map/all_to_all | solution.py:147
  510.1 8.3 fusion.441
  518.7 8.3 fusion.445
  527.6 34.6 %psum.43 = f32[]{:T(128)} all-reduce(f32[]{:T(128)} %get-tuple-element.4), channel_id=1, replica_groups=mesh['groups'=2,'px'=16] {'px'}, use_global_device_ids=true, to_apply=%region_5.6 | all-reduce | flops 1 | bytes 8 | tf_op jit(solution)/shard_map/psum | solution.py:159
  563.4 30.1 %psum.44 = f32[]{:T(128)} all-reduce(f32[]{:T(128)} %multiply_reduce_fusion.3), channel_id=1, replica_groups=mesh['groups'=2,'px'=16] {'px'}, use_global_device_ids=true, to_apply=%region_7.8 | all-reduce | flops 1 | bytes 8 | tf_op jit(solution)/shard_map/psum | solution.py:161
  600.5 10.5 all_to_all.347
  611.2 17.3 %convolution_bitcast_fusion = f32[16,32,8,16,16]{4,3,2,1,0:T(8,128)} fusion(f32[8,16,256,1,1]{2,1,0,4,3:T(8,128)S(1)} %bitcast.402, s32[256]{0:T(256)S(1)} %eq.110, s32[16,32,16]{2,1,0:T(8,128)S(1)} %multiply_add_fusion), kind=kOutput, calls=%fused_computation.2 | convolution fusion | flops 3223322624 | bytes 4359168 | tf_op jit(solution)/shard_map/ks,sc->kc/dot_general | solution.py:25
  628.5 23.9 %reshape.180 = f32[16,256,256]{2,1,0:T(8,128)} reshape(f32[16,32,8,16,16]{4,3,2,1,0:T(8,128)} %convolution_bitcast_fusion) | data formatting | bytes 8388608 | tf_op jit(solution)/shard_map/reshape | solution.py:37
  681.5 6.1 all-to-all-start.16
  695.3 6.1 all-to-all-start.13
  711.4 31.1 %all-to-all-done.13 = f32[16,256,128]{2,0,1:T(8,128)} async-done(((f32[16,256,128]{2,0,1:T(8,128)}), f32[16,256,128]{2,0,1:T(8,128)}, u32[]{:S(2)}, u32[]{:S(2)}) %all-to-all-start.13) | async-done | bytes 2097184 | tf_op jit(solution)/shard_map/all_to_all | solution.py:75
  742.5 11.7 all-to-all-start.12
  774.9 20.0 %all-to-all-done.12 = f32[16,256,128]{2,0,1:T(8,128)} async-done(((f32[16,256,128]{2,0,1:T(8,128)}), f32[16,256,128]{2,0,1:T(8,128)}, u32[]{:S(2)}, u32[]{:S(2)}) %all-to-all-start.12) | async-done | bytes 2097184 | tf_op jit(solution)/shard_map/all_to_all | solution.py:74
  794.9 11.2 all-to-all-start.19
  823.9 6.0 all-to-all-start.18
  837.0 6.1 all-to-all-start.15
  851.4 32.8 %all-to-all-done.15 = f32[256,16,128]{2,1,0:T(8,128)} async-done(((f32[256,16,128]{2,1,0:T(8,128)}), f32[256,16,128]{2,1,0:T(8,128)}, u32[]{:S(2)}, u32[]{:S(2)}) %all-to-all-start.15) | async-done | bytes 2097184 | tf_op jit(solution)/shard_map/all_to_all | solution.py:93
  884.3 11.3 all-to-all-start.14
  915.8 20.9 %all-to-all-done.14 = f32[256,16,128]{2,1,0:T(8,128)} async-done(((f32[256,16,128]{2,1,0:T(8,128)}), f32[256,16,128]{2,1,0:T(8,128)}, u32[]{:S(2)}, u32[]{:S(2)}) %all-to-all-start.14) | async-done | bytes 2097184 | tf_op jit(solution)/shard_map/all_to_all | solution.py:92
  953.2 19.4 %reshape.181 = f32[16,32,8,16,16]{4,3,2,1,0:T(8,128)} reshape(f32[16,256,256]{2,1,0:T(8,128)} %add_multiply_fusion) | data formatting | bytes 8388608 | tf_op jit(solution)/shard_map/reshape | solution.py:31
  972.6 29.9 %copy.302 = f32[16,32,16,8,16]{4,3,2,1,0:T(8,128)} copy(f32[16,32,16,8,16]{4,2,3,1,0:T(8,128)} %bitcast.381) | data formatting | bytes 8388608 | tf_op jit(solution)/shard_map/transpose | solution.py:32
  1002.5 21.5 %reshape.261 = f32[8192,128,1]{1,0,2:T(8,128)} reshape(f32[16,32,16,8,16]{4,3,2,1,0:T(8,128)} %copy.302) | data formatting | bytes 8388608 | tf_op jit(solution)/shard_map/reshape | solution.py:32
  1024.1 6.3 fusion.449
  1030.4 24.6 %all-to-all-start.20 = ((f32[16,16,128]{2,1,0:T(8,128)}), f32[16,16,128]{2,1,0:T(8,128)S(1)}, u32[]{:S(2)}, u32[]{:S(2)}) async-start(f32[16,16,128]{2,1,0:T(8,128)} %fusion.449), calls=%async_computation.20 | async-start | bytes 262144 | tf_op jit(solution)/shard_map/all_to_all | solution.py:147
  1055.0 8.3 fusion.446
  1063.6 8.3 fusion.450
  1072.6 34.6 %psum.45 = f32[]{:T(128)} all-reduce(f32[]{:T(128)} %get-tuple-element.2), channel_id=1, replica_groups=mesh['groups'=2,'px'=16] {'px'}, use_global_device_ids=true, to_apply=%region_9.10 | all-reduce | flops 1 | bytes 8 | tf_op jit(solution)/shard_map/psum | solution.py:164
  1109.6 30.1 %psum.46 = f32[]{:T(128)} all-reduce(f32[]{:T(128)} %multiply_reduce_fusion.1), channel_id=1, replica_groups=mesh['groups'=2,'px'=16] {'px'}, use_global_device_ids=true, to_apply=%region_11.12 | all-reduce | flops 1 | bytes 8 | tf_op jit(solution)/shard_map/psum | solution.py:166
  1146.3 30.0 %psum.47 = f32[]{:T(128)} all-reduce(f32[]{:T(128)} %multiply_reduce_fusion), channel_id=1, replica_groups=mesh['groups'=2,'px'=16] {'px'}, use_global_device_ids=true, to_apply=%region_13.14 | all-reduce | flops 1 | bytes 8 | tf_op jit(solution)/shard_map/psum | solution.py:168
  (249 shorter events, 317.5 us)
Async XLA Ops:
  3.7 51.1 %all-to-all-start = ((s32[16,16,1]{1,2,0:T(1,128)}), s32[16,16,1]{1,2,0:T(1,128)S(1)}, u32[]{:S(2)}, u32[]{:S(2)}) async-start(s32[16,16,1]{1,2,0:T(1,128)} %bitcast.6), calls=%async_computation | async-start | bytes 16384 | tf_op jit(solution)/shard_map/all_to_all | solution.py:131
  54.8 11.6 all-to-all-start.1
  115.1 18.9 %all-to-all-start.7 = ((f32[16,1,256]{2,1,0:T(1,128)}), f32[16,1,256]{2,1,0:T(1,128)S(1)}, u32[]{:S(2)}, u32[]{:S(2)}) async-start(f32[16,1,256]{2,1,0:T(1,128)} %reshape.279), calls=%async_computation.7 | async-start | bytes 32768 | tf_op jit(solution)/shard_map/all_to_all | solution.py:77
  124.1 4.2 copy-start.3
  124.1 4.2 copy-start
  134.0 13.5 %all-to-all-start.6 = ((f32[16,1,256]{2,1,0:T(1,128)}), f32[16,1,256]{2,1,0:T(1,128)S(1)}, u32[]{:S(2)}, u32[]{:S(2)}) async-start(f32[16,1,256]{2,1,0:T(1,128)} %reshape.277), calls=%async_computation.6 | async-start | bytes 32768 | tf_op jit(solution)/shard_map/all_to_all | solution.py:76
  147.5 47.3 %all-to-all-start.3 = ((f32[16,256,128]{2,0,1:T(8,128)}), f32[16,256,128]{2,0,1:T(8,128)}, u32[]{:S(2)}, u32[]{:S(2)}) async-start(f32[16,256,128]{2,0,1:T(8,128)} %copy.241), calls=%async_computation.3 | async-start | bytes 4194304 | tf_op jit(solution)/shard_map/all_to_all | solution.py:75
  194.8 52.4 %all-to-all-start.2 = ((f32[16,256,128]{2,0,1:T(8,128)}), f32[16,256,128]{2,0,1:T(8,128)}, u32[]{:S(2)}, u32[]{:S(2)}) async-start(f32[16,256,128]{2,0,1:T(8,128)} %copy.236), calls=%async_computation.2 | async-start | bytes 4194304 | tf_op jit(solution)/shard_map/all_to_all | solution.py:74
  206.2 3.2 copy-start.18
  227.8 1.3 copy-start.11
  247.2 28.8 %all-to-all-start.9 = ((f32[16,1,256]{2,1,0:T(1,128)}), f32[16,1,256]{2,1,0:T(1,128)S(1)}, u32[]{:S(2)}, u32[]{:S(2)}) async-start(f32[16,1,256]{2,1,0:T(1,128)} %reshape.283), calls=%async_computation.9 | async-start | bytes 32768 | tf_op jit(solution)/shard_map/all_to_all | solution.py:95
  260.3 2.9 copy-start.14
  263.1 3.6 copy-start.12
  266.7 4.9 copy-start.6
  276.0 13.7 %all-to-all-start.8 = ((f32[16,1,256]{2,1,0:T(1,128)}), f32[16,1,256]{2,1,0:T(1,128)S(1)}, u32[]{:S(2)}, u32[]{:S(2)}) async-start(f32[16,1,256]{2,1,0:T(1,128)} %reshape.281), calls=%async_computation.8 | async-start | bytes 32768 | tf_op jit(solution)/shard_map/all_to_all | solution.py:94
  289.7 47.2 %all-to-all-start.5 = ((f32[256,16,128]{2,1,0:T(8,128)}), f32[256,16,128]{2,1,0:T(8,128)}, u32[]{:S(2)}, u32[]{:S(2)}) async-start(f32[256,16,128]{2,1,0:T(8,128)} %copy.254), calls=%async_computation.5 | async-start | bytes 4194304 | tf_op jit(solution)/shard_map/all_to_all | solution.py:93
  295.8 4.6 copy-start.7
  305.9 46.2 %copy-start.21 = (s32[128,2]{0,1:T(2,128)S(1)}, s32[128,2]{0,1:T(2,128)}, u32[]{:S(2)}) copy-start(s32[128,2]{0,1:T(2,128)} %param.13) | copy-start | bytes 3076
  305.9 46.5 %copy-start.20 = (f32[8192]{0:T(1024)S(1)}, f32[8192]{0:T(1024)}, u32[]{:S(2)}) copy-start(f32[8192]{0:T(1024)} %param.9) | copy-start | bytes 98308
  337.0 52.4 %all-to-all-start.4 = ((f32[256,16,128]{2,1,0:T(8,128)}), f32[256,16,128]{2,1,0:T(8,128)}, u32[]{:S(2)}, u32[]{:S(2)}) async-start(f32[256,16,128]{2,1,0:T(8,128)} %copy.249), calls=%async_computation.4 | async-start | bytes 4194304 | tf_op jit(solution)/shard_map/all_to_all | solution.py:92
  348.2 6.8 collective-permute-start
  350.5 4.5 collective-permute-start.1
  394.5 2.9 copy-start.17
  397.4 3.4 copy-start.13
  484.2 34.2 %all-to-all-start.10 = ((f32[16,16,128]{2,1,0:T(8,128)}), f32[16,16,128]{2,1,0:T(8,128)S(1)}, u32[]{:S(2)}, u32[]{:S(2)}) async-start(f32[16,16,128]{2,1,0:T(8,128)} %fusion.444), calls=%async_computation.10 | async-start | bytes 262144 | tf_op jit(solution)/shard_map/all_to_all | solution.py:147
  652.4 5.9 copy-start.1
  669.9 11.7 all-to-all-start.17
  681.5 13.7 %all-to-all-start.16 = ((f32[16,1,256]{2,1,0:T(1,128)}), f32[16,1,256]{2,1,0:T(1,128)S(1)}, u32[]{:S(2)}, u32[]{:S(2)}) async-start(f32[16,1,256]{2,1,0:T(1,128)} %reshape.285), calls=%async_computation.16 | async-start | bytes 32768 | tf_op jit(solution)/shard_map/all_to_all | solution.py:76
  695.3 47.2 %all-to-all-start.13 = ((f32[16,256,128]{2,0,1:T(8,128)}), f32[16,256,128]{2,0,1:T(8,128)}, u32[]{:S(2)}, u32[]{:S(2)}) async-start(f32[16,256,128]{2,0,1:T(8,128)} %copy.277), calls=%async_computation.13 | async-start | bytes 4194304 | tf_op jit(solution)/shard_map/all_to_all | solution.py:75
  701.3 4.6 copy-start.2
  742.5 52.4 %all-to-all-start.12 = ((f32[16,256,128]{2,0,1:T(8,128)}), f32[16,256,128]{2,0,1:T(8,128)}, u32[]{:S(2)}, u32[]{:S(2)}) async-start(f32[16,256,128]{2,0,1:T(8,128)} %copy.272), calls=%async_computation.12 | async-start | bytes 4194304 | tf_op jit(solution)/shard_map/all_to_all | solution.py:74
  769.2 1.3 copy-start.9
  794.9 29.0 %all-to-all-start.19 = ((f32[16,1,256]{2,1,0:T(1,128)}), f32[16,1,256]{2,1,0:T(1,128)S(1)}, u32[]{:S(2)}, u32[]{:S(2)}) async-start(f32[16,1,256]{2,1,0:T(1,128)} %reshape.291), calls=%async_computation.19 | async-start | bytes 32768 | tf_op jit(solution)/shard_map/all_to_all | solution.py:95
  808.0 2.9 copy-start.15
  810.9 3.6 copy-start.10
  814.4 4.9 copy-start.4
  819.3 10.6 copy-start.8
  823.9 13.1 %all-to-all-start.18 = ((f32[16,1,256]{2,1,0:T(1,128)}), f32[16,1,256]{2,1,0:T(1,128)S(1)}, u32[]{:S(2)}, u32[]{:S(2)}) async-start(f32[16,1,256]{2,1,0:T(1,128)} %reshape.289), calls=%async_computation.18 | async-start | bytes 32768 | tf_op jit(solution)/shard_map/all_to_all | solution.py:94
  837.0 47.2 %all-to-all-start.15 = ((f32[256,16,128]{2,1,0:T(8,128)}), f32[256,16,128]{2,1,0:T(8,128)}, u32[]{:S(2)}, u32[]{:S(2)}) async-start(f32[256,16,128]{2,1,0:T(8,128)} %copy.289), calls=%async_computation.15 | async-start | bytes 4194304 | tf_op jit(solution)/shard_map/all_to_all | solution.py:93
  843.1 2.9 copy-start.5
  884.3 52.4 %all-to-all-start.14 = ((f32[256,16,128]{2,1,0:T(8,128)}), f32[256,16,128]{2,1,0:T(8,128)}, u32[]{:S(2)}, u32[]{:S(2)}) async-start(f32[256,16,128]{2,1,0:T(8,128)} %copy.284), calls=%async_computation.14 | async-start | bytes 4194304 | tf_op jit(solution)/shard_map/all_to_all | solution.py:92
  895.5 5.0 collective-permute-start.2
  897.8 4.2 collective-permute-start.3
  941.3 3.1 copy-start.16
  1002.5 21.5 %copy-start.19 = (pred[256,8192]{1,0:T(8,128)(4,1)S(1)}, pred[256,8192]{1,0:T(8,128)(4,1)}, u32[]{:S(2)}) copy-start(pred[256,8192]{1,0:T(8,128)(4,1)} %iota_compare_fusion) | copy-start | bytes 6291460
  1030.4 33.0 %all-to-all-start.20 = ((f32[16,16,128]{2,1,0:T(8,128)}), f32[16,16,128]{2,1,0:T(8,128)S(1)}, u32[]{:S(2)}, u32[]{:S(2)}) async-start(f32[16,16,128]{2,1,0:T(8,128)} %fusion.449), calls=%async_computation.20 | async-start | bytes 262144 | tf_op jit(solution)/shard_map/all_to_all | solution.py:147
where the time goes:
time: 1190 us; the launch traced here: 1180 us
  matrix products  296 us (25%)
  local copies, waits for them, and re-layouts  247 us (21%)
  waiting for transfers between devices  206 us (17%)
  blocking collectives  204 us (17%)
  starting transfers between devices  193 us (16%)
  other arithmetic  20.1 us (2%)
  between operations  12.7 us (1%)
    dot_general x78, matrix products, product(): return jnp.einsum(pattern, matrix, second, precision=lax.Precision.HIGHEST)  293 us
    all_to_all x2, waiting for transfers between devices, convolve_even(): lax.all_to_all(fourth_imag, 'px', split_axis=0, concat_axis=1, tiled=True)  63.9 us
    all_to_all x2, waiting for transfers between devices, convolve_even(): lax.all_to_all(second_imag, 'px', split_axis=1, concat_axis=0, tiled=True)  62.4 us
    transpose x2, local copies, waits for them, and re-layouts, cube_layout(): shaped.transpose(0, 1, 3, 2, 4)  59.9 us
    all_to_all x2, starting transfers between devices, operator(): lax.all_to_all(reply, 'px', split_axis=0, concat_axis=0, tiled=True)  50.6 us
    reshape x2, local copies, waits for them, and re-layouts, grid_layout(): return shaped.transpose(0, 1, 3, 2, 4).reshape(planes, extent, extent)  47.4 us
    reshape x2, local copies, waits for them, and re-layouts, cube_layout(): shaped.transpose(0, 1, 3, 2, 4)  42.9 us
    all_to_all x2, waiting for transfers between devices, convolve_even(): lax.all_to_all(fourth_real, 'px', split_axis=0, concat_axis=1, tiled=True)  40.1 us
  transfers between devices with their start and end apart: 24, of which 10 were waited for; matrix products, arithmetic and copies ran while one was open for 20% of the time, Pallas kernels for 0%

commit v1 on v0

v1 whole, which is shorter than its diff:
```python
import functools
import jax
import jax.numpy as jnp
import numpy as np
from jax import lax
from jax.experimental import pallas as pl
from jax.experimental.pallas import tpu as pltpu
from jax.sharding import PartitionSpec as P

LANES = 128
CUBE_ROWS = 8
CUBE_COLS = 16


def split(value):
    high = value.astype(jnp.bfloat16)
    low = (value - high.astype(jnp.float32)).astype(jnp.bfloat16)
    return high, low


def split_table(table):
    if isinstance(table, np.ndarray):
        table = table.astype(np.float32)
        high = table.astype(jnp.bfloat16)
        return jnp.asarray(high), jnp.asarray((table - high.astype(np.float32)).astype(jnp.bfloat16))
    high = lax.reduce_precision(table, 8, 7)
    return high.astype(jnp.bfloat16), (table - high).astype(jnp.bfloat16)


def dot_in(left, right):
    return jnp.dot(left, right, preferred_element_type=jnp.float32)


def dot_three(left, right):
    left_high, left_low = left
    right_high, right_low = right
    return dot_in(left_high, right_high) + (
        dot_in(left_low, right_high) + dot_in(left_high, right_low)
    )


def partner_steps(members):
    steps = [1 << i for i in range(members.bit_length() - 1)]
    return steps[2:] + steps[1:2] + steps[:1]


def exchange(value, step):
    members = lax.axis_size("px")
    return lax.ppermute(value, "px", [(i, i ^ step) for i in range(members)])


def gather_pieces(piece):
    pieces = piece
    for step in partner_steps(lax.axis_size("px")):
        pieces = jnp.concatenate([pieces, exchange(pieces, step)], axis=0)
    return pieces


def scatter_pieces(pieces):
    for step in reversed(partner_steps(lax.axis_size("px"))):
        half = pieces.shape[0] // 2
        pieces = pieces[:half] + exchange(pieces[half:], step)
    return pieces


def total(value):
    for step in reversed(partner_steps(lax.axis_size("px"))):
        value = value + exchange(value, step)
    return value


def angle_tables(numerator, extent):
    angle = (2.0 * jnp.pi / extent) * (numerator % extent).astype(jnp.float32)
    return jnp.cos(angle), jnp.sin(angle)


def butterfly16(real, imag, sign):
    def four(a, b, c, d):
        (ar, ai), (br, bi), (cr, ci), (dr, di) = a, b, c, d
        sr, si, tr, ti = ar + cr, ai + ci, ar - cr, ai - ci
        ur, ui, vr, vi = br + dr, bi + di, br - dr, bi - di
        wr, wi = (-vi, vr) if sign > 0 else (vi, -vr)
        return (sr + ur, si + ui), (tr + wr, ti + wi), (sr - ur, si - ui), (tr - wr, ti - wi)

    def turned(value, power):
        power %= 16
        if power == 0:
            return value
        r, i = value
        cosine = float(np.cos(2 * np.pi * power / 16))
        sine = sign * float(np.sin(2 * np.pi * power / 16))
        if power == 4:
            return (-i, r) if sign > 0 else (i, -r)
        return (r * cosine - i * sine, r * sine + i * cosine)

    points = list(zip(real, imag))
    inner = [four(*(points[4 * j1 + j0] for j1 in range(4))) for j0 in range(4)]
    out = [None] * 16
    for b1 in range(4):
        column = [turned(inner[j0][b1], j0 * b1) for j0 in range(4)]
        for b0, value in enumerate(four(*column)):
            out[b1 + 4 * b0] = value
    return [v[0] for v in out], [v[1] for v in out]


def spectral_kernel(
    parts,
    extent,
    chunk,
    rows_ref,
    charge_ref,
    onehot_ref,
    cube_high,
    cube_low,
    back_high,
    back_low,
    turn_high,
    turn_low,
    plane_high,
    plane_low,
    unplane_high,
    unplane_low,
    line_high,
    line_low,
    unline_high,
    unline_low,
    twist_ref,
    filter_ref,
    out_ref,
    *scratch,
):
    grid = scratch[: 2 * parts]
    rows = scratch[2 * parts :]
    count = charge_ref.shape[0]
    width = parts * LANES
    kept = filter_ref.shape[1]
    slabs = extent // CUBE_COLS

    def clear(i, _):
        for ref in grid:
            ref[pl.ds(i * 64, 64), :] = jnp.zeros((64, LANES), jnp.float32)
        return 0

    lax.fori_loop(0, slabs * extent // 64, clear, 0)

    def turns(start):
        picked = onehot_ref[pl.ds(start, chunk), :]
        both = dot_in(picked, turn_high[...]) + dot_in(picked, turn_low[...])
        return both[:, :width], both[:, width:]

    def spread(step, _):
        start = pl.multiple_of(step * chunk, chunk)
        values = split(charge_ref[pl.ds(start, chunk), :])
        both = dot_three(values, (cube_high[...], cube_low[...]))
        real, imag = both[:, :width], both[:, width:]
        cosine, sine = turns(start)
        turned = (real * cosine + imag * sine, imag * cosine - real * sine)
        for part in range(2):
            for half in range(parts):
                rows[part * parts + half][...] = turned[part][:, half * LANES : (half + 1) * LANES]

        def add(i, _):
            row = rows_ref[start + i]
            for ref, source in zip(grid, rows):
                ref[pl.ds(row, 1), :] += source[pl.ds(i, 1), :]
            return 0

        lax.fori_loop(0, chunk, add, 0, unroll=8)
        return 0

    lax.fori_loop(0, count // chunk, spread, 0)

    def across(sign):
        def body(i, _):
            start = pl.multiple_of(i * 8, 8)
            for half in range(parts):
                places = [pl.ds(start + slab * extent, 8) for slab in range(slabs)]
                real = [grid[half][place, :] for place in places]
                imag = [grid[parts + half][place, :] for place in places]
                real, imag = butterfly16(real, imag, sign)
                for place, r, j in zip(places, real, imag):
                    grid[half][place, :] = r
                    grid[parts + half][place, :] = j
            return 0

        lax.fori_loop(0, extent // 8, body, 0)

    across(-1)

    def middle(b, _):
        place = pl.ds(pl.multiple_of(b * extent, extent), extent)
        stacked = jnp.concatenate(
            [
                jnp.concatenate([grid[part * parts + half][place, :] for half in range(parts)], axis=1)
                for part in range(2)
            ],
            axis=0,
        )
        planes = dot_three((plane_high[...], plane_low[...]), split(stacked))
        real, imag = planes[:kept], planes[kept:]
        twist_cos, twist_sin = twist_ref[b, 0:1, :], twist_ref[b, 1:2, :]
        twisted = (real * twist_cos + imag * twist_sin, imag * twist_cos - real * twist_sin)
        back = ([], [])
        for half in range(parts):
            cut = slice(half * LANES, (half + 1) * LANES)
            line = jnp.concatenate([twisted[0][:, cut], twisted[1][:, cut]], axis=1)
            full = dot_three(split(line), (line_high[...], line_low[...]))
            scale = filter_ref[b, :, cut]
            full = full * jnp.concatenate([scale, scale], axis=1)
            full = dot_three(split(full), (unline_high[...], unline_low[...]))
            back[0].append(full[:, :LANES])
            back[1].append(full[:, LANES:])
        real, imag = (jnp.concatenate(values, axis=1) for values in back)
        stacked = jnp.concatenate(
            [real * twist_cos - imag * twist_sin, imag * twist_cos + real * twist_sin], axis=0
        )
        planes = dot_three((unplane_high[...], unplane_low[...]), split(stacked))
        for part in range(2):
            for half in range(parts):
                grid[part * parts + half][place, :] = planes[
                    part * extent : (part + 1) * extent, half * LANES : (half + 1) * LANES
                ]
        return 0

    lax.fori_loop(0, slabs, middle, 0)
    across(1)

    def collect(step, _):
        start = pl.multiple_of(step * chunk, chunk)

        def take(i, _):
            row = rows_ref[start + i]
            for ref, source in zip(rows, grid):
                ref[pl.ds(i, 1), :] = source[pl.ds(row, 1), :]
            return 0

        lax.fori_loop(0, chunk, take, 0, unroll=8)
        cosine, sine = turns(start)
        real = jnp.concatenate([rows[half][...] for half in range(parts)], axis=1)
        imag = jnp.concatenate([rows[parts + half][...] for half in range(parts)], axis=1)
        both = jnp.concatenate([real * cosine - imag * sine, imag * cosine + real * sine], axis=1)
        out_ref[pl.ds(start, chunk), :] = dot_three(split(both), (back_high[...], back_low[...]))
        return 0

    lax.fori_loop(0, count // chunk, collect, 0)


def spectral_tables(kernel_local):
    members = lax.axis_size("px")
    extent = kernel_local.shape[0]
    slab = kernel_local.shape[1]
    padded_slab = max(LANES // CUBE_COLS, slab)
    width = padded_slab * CUBE_COLS
    first = lax.axis_index("px") * slab
    column = jnp.arange(width, dtype=jnp.int32)
    k1 = first + column // CUBE_COLS
    real_slab = (column // CUBE_COLS < slab).astype(jnp.float32)
    point = jnp.arange(CUBE_ROWS * CUBE_COLS, dtype=jnp.int32)
    cosine, sine = angle_tables((point // CUBE_COLS)[:, None] * k1[None, :], extent)
    same = (point[:, None] % CUBE_COLS == column[None, :] % CUBE_COLS) * real_slab[None, :]
    cube = jnp.concatenate([cosine * same, -sine * same], axis=1)
    turn_row = jnp.arange(extent // CUBE_ROWS, dtype=jnp.int32) * CUBE_ROWS
    cosine, sine = angle_tables(turn_row[:, None] * k1[None, :], extent)
    turn = jnp.concatenate([cosine, sine], axis=1)
    kept = -(-(extent // 2 + 1) // 8) * 8
    n0 = np.arange(extent)
    k0 = np.arange(kept)
    angle = 2.0 * np.pi / extent * (k0[:, None] * n0[None, :] % extent)
    cosine, sine = np.cos(angle), np.sin(angle)
    plane = np.block([[cosine, sine], [-sine, cosine]])
    unplane = np.block([[cosine.T, -sine.T], [sine.T, cosine.T]])
    inside = LANES // CUBE_COLS
    small = np.arange(CUBE_COLS)
    angle = 2.0 * np.pi / CUBE_COLS * (small[:, None] * small[None, :] % CUBE_COLS)
    cosine = np.kron(np.eye(inside), np.cos(angle))
    sine = np.kron(np.eye(inside), np.sin(angle))
    line = np.block([[cosine, -sine], [sine, cosine]])
    unline = np.block([[cosine, sine], [-sine, cosine]])
    lane = np.arange(width) % CUBE_COLS
    angle = 2.0 * np.pi / extent * (small[:, None] * lane[None, :])
    twist = np.stack([np.cos(angle), np.sin(angle)], axis=1)
    weight = np.where((k0 == 0) | (k0 == extent // 2), 1.0, 2.0) * (k0 <= extent // 2)
    weight = weight / float(extent) ** 3
    filters = kernel_local[:kept] * jnp.asarray(weight, jnp.float32)[:, None, None]
    filters = jnp.pad(filters, ((0, 0), (0, padded_slab - slab), (0, 0)))
    filters = filters.reshape(kept, padded_slab, extent // CUBE_COLS, CUBE_COLS)
    filters = filters.transpose(3, 0, 1, 2).reshape(CUBE_COLS, kept, width)
    tables = []
    for table in (cube, cube.T, turn, plane, unplane, line, unline):
        tables.extend(split_table(table))
    return tables + [jnp.asarray(twist, jnp.float32), filters]


def spectral(cubes, extent, charges, tables):
    count = charges.shape[0]
    width = tables[-1].shape[2]
    parts = width // LANES
    slabs = extent // CUBE_COLS
    per_plane = (extent // CUBE_ROWS) * slabs
    rows = (cubes % slabs) * extent + cubes // per_plane
    turn_index = cubes // slabs % (extent // CUBE_ROWS)
    onehot = (
        turn_index[:, None] == jnp.arange(extent // CUBE_ROWS, dtype=jnp.int32)[None, :]
    ).astype(jnp.bfloat16)
    chunk = 512
    whole = pl.BlockSpec(memory_space=pltpu.VMEM)
    return pl.pallas_call(
        functools.partial(spectral_kernel, parts, extent, chunk),
        out_shape=jax.ShapeDtypeStruct((count, LANES), jnp.float32),
        in_specs=[pl.BlockSpec(memory_space=pltpu.SMEM)] + [whole] * (2 + len(tables)),
        out_specs=whole,
        scratch_shapes=[pltpu.VMEM((slabs * extent, LANES), jnp.float32)] * (2 * parts)
        + [pltpu.VMEM((chunk, LANES), jnp.float32)] * (2 * parts),
        compiler_params=pltpu.CompilerParams(vmem_limit_bytes=48 * 1024 * 1024),
        name="spectral",
    )(rows, charges, onehot, *tables)


def halo(cells, width):
    count = lax.axis_size("px")
    ends = count - 1
    return jnp.concatenate(
        [
            lax.ppermute(cells[-width:], "px", [(i, i + 1) for i in range(ends)]),
            cells,
            lax.ppermute(cells[:width], "px", [(i + 1, i) for i in range(ends)]),
        ],
        axis=0,
    )


def on_device(
    right_side, self_term, proj_tiles, owner_dev, cube_slot, near_src, near_tiles, kernel_hat
):
    members = lax.axis_size("px")
    blocks = proj_tiles.shape[0]
    extent = kernel_hat.shape[0]
    cubes_dev = extent // members * (extent // CUBE_ROWS) * (extent // CUBE_COLS)
    self_local = self_term.reshape(blocks, 64)
    cubes = owner_dev[:, 0] * cubes_dev + cube_slot
    tables = spectral_tables(kernel_hat)
    all_cubes = gather_pieces(cubes.reshape(1, blocks)).reshape(members * blocks)

    def operator(values):
        charges = jnp.sum(proj_tiles * values[:, :, None], axis=1)
        gathered = gather_pieces(charges)
        picked = scatter_pieces(spectral(all_cubes, extent, gathered, tables))
        sources = halo(values, blocks // 4)[near_src].reshape(blocks, near_tiles.shape[2])
        return (
            self_local * values
            + jnp.sum(near_tiles * sources[:, None, :], axis=2)
            + jnp.sum(proj_tiles * picked[:, None, :], axis=2)
        )

    rhs = right_side.reshape(blocks, 64)
    first = operator(rhs)
    sums = total(
        jnp.stack([jnp.sum(rhs * rhs), jnp.sum(rhs * first), jnp.sum(first * first)]).reshape(1, 3)
    )
    second = operator(first)
    initial_norm = jnp.sqrt(sums[0, 0])
    diag_one = sums[0, 1] / sums[0, 0]
    gram_one = sums[0, 2] / sums[0, 0]
    scale = jnp.sqrt(gram_one)
    basis_one = rhs / initial_norm
    image_one = first / initial_norm
    basis_two = (image_one - diag_one * basis_one) / scale
    image_two = (second / initial_norm - diag_one * image_one) / scale
    sums = total(
        jnp.stack(
            [
                jnp.sum(basis_one * image_two),
                jnp.sum(image_one * image_two),
                jnp.sum(image_two * image_two),
            ]
        ).reshape(1, 3)
    )
    upper_two, gram_cross, gram_two = sums[0, 0], sums[0, 1], sums[0, 2]
    determinant = gram_one * gram_two - gram_cross * gram_cross
    weight_one = initial_norm * (diag_one * gram_two - upper_two * gram_cross) / determinant
    weight_two = initial_norm * (upper_two * gram_one - diag_one * gram_cross) / determinant
    answer = weight_one * basis_one + weight_two * basis_two
    residual = rhs - weight_one * image_one - weight_two * image_two
    return (answer.reshape(blocks * 64), residual.reshape(blocks * 64))


def solution(mesh):
    return jax.shard_map(
        on_device,
        mesh=mesh,
        in_specs=(
            P(("groups", "px")),
            P(("groups", "px")),
            P(("groups", "px"), None, None),
            P(("groups", "px"), None),
            P(("groups", "px")),
            P(("groups", "px"), None),
            P(("groups", "px"), None, None),
            P(None, "px", None),
        ),
        out_specs=(P(("groups", "px")), P(("groups", "px"))),
        check_vma=False,
    )
```

time: 1190 us -> 291 us (0.24)
  matrix products: 296 us -> 0 us
  local copies, waits for them, and re-layouts: 247 us -> 25.6 us
  blocking collectives: 204 us -> 0 us
  waiting for transfers between devices: 206 us -> 49.9 us
  starting transfers between devices: 193 us -> 42 us
  Pallas kernels: 0 us -> 123 us
  other arithmetic: 20.1 us -> 39.4 us
    dot_general x78 -> x0, matrix products: 293 us -> none  [product(): return jnp.einsum(pattern, matrix, second, precision=lax.Precision.HIGHEST)]
    all_to_all x20 -> x0, waiting for transfers between devices: 205 us -> none  [the longest x2 63.9 us: convolve_even(): lax.all_to_all(fourth_imag, 'px', split_axis=0, concat_axis=1, tiled=True)]
    psum x6 -> x0, blocking collectives: 194 us -> none  [the longest x1 34.6 us: on_device(): diag_one = lax.psum(jnp.sum(basis_one * image_one), 'px')]
    all_to_all x20 -> x0, starting transfers between devices: 186 us -> none  [the longest x2 50.6 us: operator(): lax.all_to_all(reply, 'px', split_axis=0, concat_axis=0, tiled=True)]
    reshape x11 -> x2, local copies, waits for them, and re-layouts: 132 us -> 5.86 us  [the longest x1 5.02 us: spectral_tables(): filters = filters.transpose(3, 0, 1, 2).reshape(CUBE_COLS, kept, width)]
    pallas_call x0 -> x2, Pallas kernels: none -> 123 us  [spectral(): pl.pallas_call(functools.partial(spectral_kernel, parts, extent, chunk),...]
    transpose x2 -> x0, local copies, waits for them, and re-layouts: 59.9 us -> none  [cube_layout(): shaped.transpose(0, 1, 3, 2, 4)]
    ppermute x4 -> x32, waiting for transfers between devices: 1.52 us -> 49.9 us  [the longest x28 49.9 us: exchange(): return lax.ppermute(value, 'px', [(i, i ^ step) for i in range(members)])]
  transfers between devices with their start and end apart: 24 -> 32, of which waited for: 10 -> 18; matrix products, arithmetic and copies ran while one was open for 20% -> 14% of each run, Pallas kernels for 0% -> 0%
where the time goes in v1:
time: 291 us; the launch traced here: 290 us
  Pallas kernels  123 us (42%)
  waiting for transfers between devices  49.9 us (17%)
  starting transfers between devices  42 us (14%)
  other arithmetic  39.4 us (14%)
  local copies, waits for them, and re-layouts  25.6 us (9%)
  between operations  9.83 us (3%)
    pallas_call x2, Pallas kernels, spectral(): pl.pallas_call(functools.partial(spectral_kernel, parts, extent, chunk),...  123 us
    ppermute x28, waiting for transfers between devices, exchange(): return lax.ppermute(value, 'px', [(i, i ^ step) for i in range(members)])  49.9 us
    ppermute x28, starting transfers between devices, exchange(): return lax.ppermute(value, 'px', [(i, i ^ step) for i in range(members)])  35.4 us
    unnamed x73, local copies, waits for them, and re-layouts  10.4 us
    add x8, other arithmetic, total(): value = value + exchange(value, step)  7.9 us
    reduce_sum x2, other arithmetic, operator(): jnp.sum(near_tiles * sources[:, None, :], axis=2)  6.7 us
  transfers between devices with their start and end apart: 32, of which 18 were waited for; matrix products, arithmetic and copies ran while one was open for 14% of the time, Pallas kernels for 0%

profile of v1, /device:TPU:0, one launch (start us, length us, event | category | flops | bytes accessed | tf_op | source)
XLA Modules:
  0.0 289.8 jit_solution(6232247696520309278)
XLA Ops:
  1.5 3.0 %multiply_reduce_fusion.4 = f32[128,128]{1,0:T(8,128)S(1)} fusion(f32[128,64,128]{2,1,0:T(8,128)} %param.20, f32[128,64]{1,0:T(8,128)S(1)} %reshape.200), kind=kLoop, calls=%fused_computation.6 | loop fusion | flops 2080768 | bytes 4292608 | tf_op jit(solution)/shard_map/reduce_sum | solution.py:345
  4.5 3.1 %collective-permute-start.6 = (f32[128,128]{1,0:T(8,128)S(1)}, f32[128,128]{1,0:T(8,128)S(1)}, u32[]{:S(2)}, u32[]{:S(2)}) collective-permute-start(f32[128,128]{1,0:T(8,128)S(1)} %multiply_reduce_fusion.4), channel_id=1, source_target_pairs={{0,4},{1,5},{2,6},{3,7},{4,0},{5,1},{6,2},{7,3},{8,12},{9,13},{10,... | collective-permute-start | bytes 196616 | tf_op jit(solution)/shard_map/ppermute | solution.py:49
  7.8 3.3 %copy.36 = f32[136,16,256]{0,2,1:T(8,128)} copy(f32[136,16,256]{2,1,0:T(8,128)S(1)} %slice-done) | data formatting | bytes 4456448
  11.3 4.6 %broadcast_multiply_fusion = f32[136,16,256]{0,2,1:T(8,128)} fusion(f32[136,16,256]{0,2,1:T(8,128)} %copy.36, f32[136]{0:T(256)S(1)} %copy-done.28), kind=kLoop, calls=%fused_computation.8 | loop fusion | flops 557056 | bytes 4456992 | tf_op jit(solution)/shard_map/mul | solution.py:284
  16.5 3.1 %collective-permute-start.3 = (s32[2,128]{1,0:T(2,128)S(1)}, s32[2,128]{1,0:T(2,128)S(1)}, u32[]{:S(2)}, u32[]{:S(2)}) collective-permute-start(s32[2,128]{1,0:T(2,128)S(1)} %pad_add_fusion.2), channel_id=1, source_target_pairs={{0,8},{1,9},{2,10},{3,11},{4,12},{5,13},{6,14},{7,15},{8,0},{9,1},... | collective-permute-start | bytes 3080 | tf_op jit(solution)/shard_map/ppermute | solution.py:49
  19.7 1.5 collective-permute-done.3
  21.2 1.9 collective-permute-start.4
  23.1 2.7 collective-permute-start.7
  25.8 4.6 %collective-permute-done.7 = f32[256,128]{1,0:T(8,128)S(1)} collective-permute-done((f32[256,128]{1,0:T(8,128)S(1)}, f32[256,128]{1,0:T(8,128)S(1)}, u32[]{:S(2)}, u32[]{:S(2)}) %collective-permute-start.7) | collective-permute-done | bytes 131104 | tf_op jit(solution)/shard_map/ppermute | solution.py:49
  31.5 5.0 %copy.30.filter_ref = f32[16,136,256]{2,1,0:T(8,128)} copy(f32[16,136,256]{1,0,2:T(8,128)} %bitcast.64) | data formatting | bytes 4456448 | tf_op jit(solution)/shard_map/reshape | solution.py:287
  45.7 61.5 %spectral.2 = f32[2048,128]{1,0:T(8,128)S(1)} custom-call(s32[2048]{0:T(1024)S(1)} %get-tuple-element.23.rows_ref, f32[2048,128]{1,0:T(8,128)S(1)} %constant_dynamic-update-slice_fusion.charge_ref, bf16[2048,32]{1,0:T(8,128)(2,1)S(1)} %fusion.onehot_ref, bf16[128,512]{1,0:T(8,128)(2,1)S(1)} %copy.28.cube_high, bf16[128,512]{1,0:T(8,128)(2,1)S(1)} %copy.29.cube_low, ...), custom_call_target="tpu_custom_call" | custom-call | tf_op jit(solution)/shard_map/spectral/pallas_call | solution.py:307
  107.8 1.5 collective-permute-done.10
  111.0 2.0 collective-permute-start
  113.6 1.5 collective-permute-start.1
  115.4 2.9 collective-permute-done.11
  119.2 1.7 collective-permute-start.12
  121.9 6.1 %collective-permute-done.12 = f32[256,128]{1,0:T(8,128)S(1)} collective-permute-done((f32[256,128]{1,0:T(8,128)S(1)}, f32[256,128]{1,0:T(8,128)S(1)}, u32[]{:S(2)}, u32[]{:S(2)}) %collective-permute-start.12) | collective-permute-done | bytes 131104 | tf_op jit(solution)/shard_map/ppermute | solution.py:49
  128.1 3.4 %multiply_reduce_fusion.5 = f32[128,64]{1,0:T(8,128)S(1)} fusion(f32[128,64,128]{2,1,0:T(8,128)} %param.24, f32[128,128]{1,0:T(8,128)S(1)} %mul.254), kind=kLoop, calls=%fused_computation.7 | loop fusion | flops 2088960 | bytes 4292608 | tf_op jit(solution)/shard_map/reduce_sum | solution.py:351
  134.2 1.6 multiply_reduce_fusion.1
  137.1 3.1 %collective-permute-done.20 = f32[128,128]{1,0:T(8,128)S(1)} collective-permute-done((f32[128,128]{1,0:T(8,128)S(1)}, f32[128,128]{1,0:T(8,128)S(1)}, u32[]{:S(2)}, u32[]{:S(2)}) %collective-permute-start.20) | collective-permute-done | bytes 65568 | tf_op jit(solution)/shard_map/ppermute | solution.py:49
  140.2 2.1 collective-permute-start.21
  142.3 5.2 %collective-permute-done.21 = f32[256,128]{1,0:T(8,128)S(1)} collective-permute-done((f32[256,128]{1,0:T(8,128)S(1)}, f32[256,128]{1,0:T(8,128)S(1)}, u32[]{:S(2)}, u32[]{:S(2)}) %collective-permute-start.21) | collective-permute-done | bytes 131104 | tf_op jit(solution)/shard_map/ppermute | solution.py:49
  147.5 1.4 collective-permute-start.22
  148.9 5.1 %collective-permute-done.22 = f32[512,128]{1,0:T(8,128)S(1)} collective-permute-done((f32[512,128]{1,0:T(8,128)S(1)}, f32[512,128]{1,0:T(8,128)S(1)}, u32[]{:S(2)}, u32[]{:S(2)}) %collective-permute-start.22) | collective-permute-done | bytes 262176 | tf_op jit(solution)/shard_map/ppermute | solution.py:49
  154.8 1.5 reduce_sum.118
  156.3 1.5 reduce_sum.121
  159.1 61.6 %spectral.3 = f32[2048,128]{1,0:T(8,128)S(1)} custom-call(s32[2048]{0:T(1024)S(1)} %get-tuple-element.23.rows_ref, f32[2048,128]{1,0:T(8,128)S(1)} %constant_dynamic-update-slice_fusion.5.charge_ref, bf16[2048,32]{1,0:T(8,128)(2,1)S(1)} %fusion.onehot_ref, bf16[128,512]{1,0:T(8,128)(2,1)S(1)} %copy.28.cube_high, bf16[128,512]{1,0:T(8,128)(2,1)S(1)} %copy.29.cube_low, ...), custom_call_target="tpu_custom_call" | custom-call | tf_op jit(solution)/shard_map/spectral/pallas_call | solution.py:307
  221.3 1.9 collective-permute-start.18
  225.3 2.0 maximum_bitcast_fusion
  227.3 2.0 collective-permute-start.14
  229.4 1.7 collective-permute-start.25
  231.1 2.0 fusion.30
  234.1 4.0 %collective-permute-done.15 = f32[1,3]{1,0:T(1,128)S(1)} collective-permute-done((f32[1,3]{1,0:T(1,128)S(1)}, f32[1,3]{1,0:T(1,128)S(1)}, u32[]{:S(2)}, u32[]{:S(2)}) %collective-permute-start.15) | collective-permute-done | bytes 44 | tf_op jit(solution)/shard_map/ppermute | solution.py:49
  238.2 2.0 fusion.32
  240.2 2.1 collective-permute-start.16
  242.3 2.4 collective-permute-done.16
  246.0 2.2 collective-permute-done.17
  248.2 2.3 collective-permute-start.26
  255.6 1.9 collective-permute-start.27
  257.5 3.3 %multiply_reduce_fusion.2 = f32[128,64]{1,0:T(8,128)S(1)} fusion(f32[128,64,128]{2,1,0:T(8,128)} %param.24, f32[128,128]{1,0:T(8,128)S(1)} %mul.288), kind=kLoop, calls=%fused_computation.4 | loop fusion | flops 2088960 | bytes 4292608 | tf_op jit(solution)/shard_map/reduce_sum | solution.py:351
  261.0 3.3 %multiply_reduce_fusion = f32[128,64]{1,0:T(8,128)S(1)} fusion(f32[128,64,128]{2,1,0:T(8,128)} %param.20, f32[128,128]{1,0:T(8,128)S(1)} %slice_add_fusion.6), kind=kLoop, calls=%fused_computation.2 | loop fusion | flops 2088960 | bytes 4292608 | tf_op jit(solution)/shard_map/reduce_sum | solution.py:352
  265.1 1.9 maximum_bitcast_fusion.1
  268.1 1.9 fusion.29
  271.0 2.6 collective-permute-done.29
  273.6 1.9 fusion.31
  275.5 1.9 collective-permute-start.30
  277.4 2.5 collective-permute-done.30
  280.7 2.7 collective-permute-done.31
  (179 shorter events, 35.0 us)
Async XLA Ops:
  4.5 18.5 %collective-permute-start.6 = (f32[128,128]{1,0:T(8,128)S(1)}, f32[128,128]{1,0:T(8,128)S(1)}, u32[]{:S(2)}, u32[]{:S(2)}) collective-permute-start(f32[128,128]{1,0:T(8,128)S(1)} %multiply_reduce_fusion.4), channel_id=1, source_target_pairs={{0,4},{1,5},{2,6},{3,7},{4,0},{5,1},{6,2},{7,3},{8,12},{9,13},{10,... | collective-permute-start | bytes 196616 | tf_op jit(solution)/shard_map/ppermute | solution.py:49
  7.6 8.9 %collective-permute-start.2 = (s32[1,128]{1,0:T(1,128)S(1)}, s32[1,128]{1,0:T(1,128)S(1)}, u32[]{:S(2)}, u32[]{:S(2)}) collective-permute-start(s32[1,128]{1,0:T(1,128)S(1)} %fusion.23), channel_id=1, source_target_pairs={{0,4},{1,5},{2,6},{3,7},{4,0},{5,1},{6,2},{7,3},{8,12},{9,13},{10,... | collective-permute-start | bytes 1544 | tf_op jit(solution)/shard_map/ppermute | solution.py:49
  16.5 4.6 %collective-permute-start.3 = (s32[2,128]{1,0:T(2,128)S(1)}, s32[2,128]{1,0:T(2,128)S(1)}, u32[]{:S(2)}, u32[]{:S(2)}) collective-permute-start(s32[2,128]{1,0:T(2,128)S(1)} %pad_add_fusion.2), channel_id=1, source_target_pairs={{0,8},{1,9},{2,10},{3,11},{4,12},{5,13},{6,14},{7,15},{8,0},{9,1},... | collective-permute-start | bytes 3080 | tf_op jit(solution)/shard_map/ppermute | solution.py:49
  21.2 4.6 %collective-permute-start.4 = (s32[4,128]{1,0:T(4,128)S(1)}, s32[4,128]{1,0:T(4,128)S(1)}, u32[]{:S(2)}, u32[]{:S(2)}) collective-permute-start(s32[4,128]{1,0:T(4,128)S(1)} %pad_add_fusion.1), channel_id=1, source_target_pairs={{0,2},{1,3},{2,0},{3,1},{4,6},{5,7},{6,4},{7,5},{8,10},{9,11},{10,... | collective-permute-start | bytes 6152 | tf_op jit(solution)/shard_map/ppermute | solution.py:49
  23.0 15.8 %copy-start.17 = (f32[128,128]{1,0:T(8,128)}, f32[128,128]{1,0:T(8,128)S(1)}, u32[]{:S(2)}) copy-start(f32[128,128]{1,0:T(8,128)S(1)} %collective-permute-done.6) | copy-start | bytes 196612
  23.1 7.3 %collective-permute-start.7 = (f32[256,128]{1,0:T(8,128)S(1)}, f32[256,128]{1,0:T(8,128)S(1)}, u32[]{:S(2)}, u32[]{:S(2)}) collective-permute-start(f32[256,128]{1,0:T(8,128)S(1)} %pad_maximum_fusion.5), channel_id=1, source_target_pairs={{0,8},{1,9},{2,10},{3,11},{4,12},{5,13},{6,14},{7,15},{8,0},{9,1},... | collective-permute-start | bytes 393224 | tf_op jit(solution)/shard_map/ppermute | solution.py:49
  25.7 10.7 %collective-permute-start.5 = (s32[8,128]{1,0:T(8,128)S(1)}, s32[8,128]{1,0:T(8,128)S(1)}, u32[]{:S(2)}, u32[]{:S(2)}) collective-permute-start(s32[8,128]{1,0:T(8,128)S(1)} %pad_add_fusion), channel_id=1, source_target_pairs={{0,1},{1,0},{2,3},{3,2},{4,5},{5,4},{6,7},{7,6},{8,9},{9,8},{10,11... | collective-permute-start | bytes 12296 | tf_op jit(solution)/shard_map/ppermute | solution.py:49
  31.1 6.7 %collective-permute-start.8 = (f32[512,128]{1,0:T(8,128)}, f32[512,128]{1,0:T(8,128)}, u32[]{:S(2)}, u32[]{:S(2)}) collective-permute-start(f32[512,128]{1,0:T(8,128)} %pad_maximum_fusion.2), channel_id=1, source_target_pairs={{0,2},{1,3},{2,0},{3,1},{4,6},{5,7},{6,4},{7,5},{8,10},{9,11},{10,... | collective-permute-start | bytes 786440 | tf_op jit(solution)/shard_map/ppermute | solution.py:49
  31.4 10.7 %copy-start = (bf16[512,272]{1,0:T(8,128)(2,1)S(1)}, bf16[512,272]{1,0:T(8,128)(2,1)}, u32[]{:S(2)}) copy-start(bf16[512,272]{1,0:T(8,128)(2,1)} %constant.169.clone.unplane_high) | copy-start | bytes 835588
  38.8 3.2 %collective-permute-start.9 = (f32[1024,128]{1,0:T(8,128)S(1)}, f32[1024,128]{1,0:T(8,128)S(1)}, u32[]{:S(2)}, u32[]{:S(2)}) collective-permute-start(f32[1024,128]{1,0:T(8,128)S(1)} %pad_maximum_fusion), channel_id=1, source_target_pairs={{0,1},{1,0},{2,3},{3,2},{4,5},{5,4},{6,7},{7,6},{8,9},{9,8},{10,11... | collective-permute-start | bytes 1572872 | tf_op jit(solution)/shard_map/ppermute | solution.py:49
  45.7 64.5 %copy-start.20 = (f32[8192]{0:T(1024)S(1)}, f32[8192]{0:T(1024)}, u32[]{:S(2)}) copy-start(f32[8192]{0:T(1024)} %param.18) | copy-start | bytes 98308
  45.7 69.4 %copy-start.29 = (s32[128,2]{0,1:T(2,128)S(1)}, s32[128,2]{0,1:T(2,128)}, u32[]{:S(2)}) copy-start(s32[128,2]{0,1:T(2,128)} %param.23) | copy-start | bytes 3076
  107.2 13.7 %copy-start.24 = (f32[8192]{0:T(1024)S(1)}, f32[8192]{0:T(1024)}, u32[]{:S(2)}) copy-start(f32[8192]{0:T(1024)} %param.19) | copy-start | bytes 98308
  107.2 13.8 %copy-start.16 = (f32[128,64]{1,0:T(8,128)S(1)}, f32[128,64]{1,0:T(8,128)}, u32[]{:S(2)}) copy-start(f32[128,64]{1,0:T(8,128)} %copy-done.15) | copy-start | bytes 98308
  107.3 2.1 collective-permute-start.10
  109.5 8.8 %collective-permute-start.11 = (f32[512,128]{1,0:T(8,128)S(1)}, f32[512,128]{1,0:T(8,128)}, u32[]{:S(2)}, u32[]{:S(2)}) collective-permute-start(f32[512,128]{1,0:T(8,128)S(1)} %slice.141), channel_id=1, source_target_pairs={{0,2},{1,3},{2,0},{3,1},{4,6},{5,7},{6,4},{7,5},{8,10},{9,11},{10,... | collective-permute-start | bytes 786440 | tf_op jit(solution)/shard_map/ppermute | solution.py:49
  111.0 10.0 %collective-permute-start = (f32[32,64]{1,0:T(8,128)}, f32[32,64]{1,0:T(8,128)S(1)}, u32[]{:S(2)}, u32[]{:S(2)}) collective-permute-start(f32[32,64]{1,0:T(8,128)} %slice.106), channel_id=1, source_target_pairs={{0,1},{1,2},{2,3},{3,4},{4,5},{5,6},{6,7},{7,8},{8,9},{9,10},{10,1... | collective-permute-start | bytes 24584 | tf_op jit(solution)/shard_map/ppermute | solution.py:324
  113.6 7.4 %collective-permute-start.1 = (f32[32,64]{1,0:T(8,128)}, f32[32,64]{1,0:T(8,128)S(1)}, u32[]{:S(2)}, u32[]{:S(2)}) collective-permute-start(f32[32,64]{1,0:T(8,128)} %slice.108), channel_id=1, source_target_pairs={{1,0},{2,1},{3,2},{4,3},{5,4},{6,5},{7,6},{8,7},{9,8},{10,9},{11,1... | collective-permute-start | bytes 24584 | tf_op jit(solution)/shard_map/ppermute | solution.py:326
  119.2 8.7 %collective-permute-start.12 = (f32[256,128]{1,0:T(8,128)S(1)}, f32[256,128]{1,0:T(8,128)S(1)}, u32[]{:S(2)}, u32[]{:S(2)}) collective-permute-start(f32[256,128]{1,0:T(8,128)S(1)} %slice.143), channel_id=1, source_target_pairs={{0,8},{1,9},{2,10},{3,11},{4,12},{5,13},{6,14},{7,15},{8,0},{9,1},... | collective-permute-start | bytes 393224 | tf_op jit(solution)/shard_map/ppermute | solution.py:49
  128.0 4.3 %collective-permute-start.13 = (f32[128,128]{1,0:T(8,128)S(1)}, f32[128,128]{1,0:T(8,128)S(1)}, u32[]{:S(2)}, u32[]{:S(2)}) collective-permute-start(f32[128,128]{1,0:T(8,128)S(1)} %slice.145), channel_id=1, source_target_pairs={{0,4},{1,5},{2,6},{3,7},{4,0},{5,1},{6,2},{7,3},{8,12},{9,13},{10,... | collective-permute-start | bytes 196616 | tf_op jit(solution)/shard_map/ppermute | solution.py:49
  134.1 19.8 %copy-start.18 = (f32[128,64]{1,0:T(8,128)}, f32[128,64]{1,0:T(8,128)S(1)}, u32[]{:S(2)}) copy-start(f32[128,64]{1,0:T(8,128)S(1)} %add_add_fusion) | copy-start | bytes 98308
  134.2 24.9 %copy-start.5 = (bf16[256,256]{1,0:T(8,128)(2,1)S(1)}, bf16[256,256]{1,0:T(8,128)(2,1)}, u32[]{:S(2)}) copy-start(bf16[256,256]{1,0:T(8,128)(2,1)} %constant.171.clone.line_high) | copy-start | bytes 393220
  134.2 24.9 %copy-start.7 = (bf16[256,256]{1,0:T(8,128)(2,1)S(1)}, bf16[256,256]{1,0:T(8,128)(2,1)}, u32[]{:S(2)}) copy-start(bf16[256,256]{1,0:T(8,128)(2,1)} %constant.172.clone.line_low) | copy-start | bytes 393220
  134.2 24.9 %copy-start.9 = (bf16[256,256]{1,0:T(8,128)(2,1)S(1)}, bf16[256,256]{1,0:T(8,128)(2,1)}, u32[]{:S(2)}) copy-start(bf16[256,256]{1,0:T(8,128)(2,1)} %constant.173.clone.unline_high) | copy-start | bytes 393220
  134.2 24.9 %copy-start.11 = (bf16[256,256]{1,0:T(8,128)(2,1)S(1)}, bf16[256,256]{1,0:T(8,128)(2,1)}, u32[]{:S(2)}) copy-start(bf16[256,256]{1,0:T(8,128)(2,1)} %constant.174.clone.unline_low) | copy-start | bytes 393220
  135.8 4.3 %collective-permute-start.20 = (f32[128,128]{1,0:T(8,128)S(1)}, f32[128,128]{1,0:T(8,128)S(1)}, u32[]{:S(2)}, u32[]{:S(2)}) collective-permute-start(f32[128,128]{1,0:T(8,128)S(1)} %multiply_reduce_fusion.1), channel_id=1, source_target_pairs={{0,4},{1,5},{2,6},{3,7},{4,0},{5,1},{6,2},{7,3},{8,12},{9,13},{10,... | collective-permute-start | bytes 196616 | tf_op jit(solution)/shard_map/ppermute | solution.py:49
  140.2 7.3 %collective-permute-start.21 = (f32[256,128]{1,0:T(8,128)S(1)}, f32[256,128]{1,0:T(8,128)S(1)}, u32[]{:S(2)}, u32[]{:S(2)}) collective-permute-start(f32[256,128]{1,0:T(8,128)S(1)} %pad_maximum_fusion.6), channel_id=1, source_target_pairs={{0,8},{1,9},{2,10},{3,11},{4,12},{5,13},{6,14},{7,15},{8,0},{9,1},... | collective-permute-start | bytes 393224 | tf_op jit(solution)/shard_map/ppermute | solution.py:49
  147.5 6.4 %collective-permute-start.22 = (f32[512,128]{1,0:T(8,128)S(1)}, f32[512,128]{1,0:T(8,128)S(1)}, u32[]{:S(2)}, u32[]{:S(2)}) collective-permute-start(f32[512,128]{1,0:T(8,128)S(1)} %pad_maximum_fusion.4), channel_id=1, source_target_pairs={{0,2},{1,3},{2,0},{3,1},{4,6},{5,7},{6,4},{7,5},{8,10},{9,11},{10,... | collective-permute-start | bytes 786440 | tf_op jit(solution)/shard_map/ppermute | solution.py:49
  154.8 3.1 %collective-permute-start.23 = (f32[1024,128]{1,0:T(8,128)}, f32[1024,128]{1,0:T(8,128)}, u32[]{:S(2)}, u32[]{:S(2)}) collective-permute-start(f32[1024,128]{1,0:T(8,128)} %pad_maximum_fusion.1), channel_id=1, source_target_pairs={{0,1},{1,0},{2,3},{3,2},{4,5},{5,4},{6,7},{7,6},{8,9},{9,8},{10,11... | collective-permute-start | bytes 1572872 | tf_op jit(solution)/shard_map/ppermute | solution.py:49
  159.1 62.2 %copy-start.19 = (f32[128,64]{1,0:T(8,128)S(1)}, f32[128,64]{1,0:T(8,128)}, u32[]{:S(2)}) copy-start(f32[128,64]{1,0:T(8,128)} %copy-done.18) | copy-start | bytes 98308
  159.1 65.5 %copy-start.21 = (f32[8192]{0:T(1024)S(1)}, f32[8192]{0:T(1024)}, u32[]{:S(2)}) copy-start(f32[8192]{0:T(1024)} %param.18) | copy-start | bytes 98308
  159.1 65.5 %copy-start.25 = (f32[8192]{0:T(1024)S(1)}, f32[8192]{0:T(1024)}, u32[]{:S(2)}) copy-start(f32[8192]{0:T(1024)} %param.19) | copy-start | bytes 98308
  159.1 65.5 %copy-start.26 = (f32[8192]{0:T(1024)S(1)}, f32[8192]{0:T(1024)}, u32[]{:S(2)}) copy-start(f32[8192]{0:T(1024)} %reduce_sum.118) | copy-start | bytes 98308
  159.1 65.5 %copy-start.27 = (f32[8192]{0:T(1024)S(1)}, f32[8192]{0:T(1024)}, u32[]{:S(2)}) copy-start(f32[8192]{0:T(1024)} %reduce_sum.121) | copy-start | bytes 98308
  220.7 8.6 %collective-permute-start.24 = (f32[1024,128]{1,0:T(8,128)S(1)}, f32[1024,128]{1,0:T(8,128)S(1)}, u32[]{:S(2)}, u32[]{:S(2)}) collective-permute-start(f32[1024,128]{1,0:T(8,128)S(1)} %slice.149), channel_id=1, source_target_pairs={{0,1},{1,0},{2,3},{3,2},{4,5},{5,4},{6,7},{7,6},{8,9},{9,8},{10,11... | collective-permute-start | bytes 1572872 | tf_op jit(solution)/shard_map/ppermute | solution.py:49
  221.3 33.2 %collective-permute-start.18 = (f32[32,64]{1,0:T(8,128)S(1)}, f32[32,64]{1,0:T(8,128)S(1)}, u32[]{:S(2)}, u32[]{:S(2)}) collective-permute-start(f32[32,64]{1,0:T(8,128)S(1)} %get-tuple-element.16), channel_id=1, source_target_pairs={{0,1},{1,2},{2,3},{3,4},{4,5},{5,6},{6,7},{7,8},{8,9},{9,10},{10,1... | collective-permute-start | bytes 24584 | tf_op jit(solution)/shard_map/ppermute | solution.py:324
  223.2 31.3 %collective-permute-start.19 = (f32[32,64]{1,0:T(8,128)S(1)}, f32[32,64]{1,0:T(8,128)S(1)}, u32[]{:S(2)}, u32[]{:S(2)}) collective-permute-start(f32[32,64]{1,0:T(8,128)S(1)} %get-tuple-element.17), channel_id=1, source_target_pairs={{1,0},{2,1},{3,2},{4,3},{5,4},{6,5},{7,6},{8,7},{9,8},{10,9},{11,1... | collective-permute-start | bytes 24584 | tf_op jit(solution)/shard_map/ppermute | solution.py:326
  227.3 3.8 %collective-permute-start.14 = (f32[1,3]{1,0:T(1,128)S(1)}, f32[1,3]{1,0:T(1,128)S(1)}, u32[]{:S(2)}, u32[]{:S(2)}) collective-permute-start(f32[1,3]{1,0:T(1,128)S(1)} %maximum_bitcast_fusion), channel_id=1, source_target_pairs={{0,1},{1,0},{2,3},{3,2},{4,5},{5,4},{6,7},{7,6},{8,9},{9,8},{10,11... | collective-permute-start | bytes 44 | tf_op jit(solution)/shard_map/ppermute | solution.py:49
  229.4 18.8 %collective-permute-start.25 = (f32[512,128]{1,0:T(8,128)S(1)}, f32[512,128]{1,0:T(8,128)S(1)}, u32[]{:S(2)}, u32[]{:S(2)}) collective-permute-start(f32[512,128]{1,0:T(8,128)S(1)} %slice.151), channel_id=1, source_target_pairs={{0,2},{1,3},{2,0},{3,1},{4,6},{5,7},{6,4},{7,5},{8,10},{9,11},{10,... | collective-permute-start | bytes 786440 | tf_op jit(solution)/shard_map/ppermute | solution.py:49
  233.2 5.0 %collective-permute-start.15 = (f32[1,3]{1,0:T(1,128)S(1)}, f32[1,3]{1,0:T(1,128)S(1)}, u32[]{:S(2)}, u32[]{:S(2)}) collective-permute-start(f32[1,3]{1,0:T(1,128)S(1)} %fusion.30), channel_id=1, source_target_pairs={{0,2},{1,3},{2,0},{3,1},{4,6},{5,7},{6,4},{7,5},{8,10},{9,11},{10,... | collective-permute-start | bytes 44 | tf_op jit(solution)/shard_map/ppermute | solution.py:49
  240.2 4.4 %collective-permute-start.16 = (f32[1,3]{1,0:T(1,128)S(1)}, f32[1,3]{1,0:T(1,128)S(1)}, u32[]{:S(2)}, u32[]{:S(2)}) collective-permute-start(f32[1,3]{1,0:T(1,128)S(1)} %fusion.32), channel_id=1, source_target_pairs={{0,8},{1,9},{2,10},{3,11},{4,12},{5,13},{6,14},{7,15},{8,0},{9,1},... | collective-permute-start | bytes 44 | tf_op jit(solution)/shard_map/ppermute | solution.py:49
  244.6 3.5 %collective-permute-start.17 = (f32[1,3]{1,0:T(1,128)S(1)}, f32[1,3]{1,0:T(1,128)S(1)}, u32[]{:S(2)}, u32[]{:S(2)}) collective-permute-start(f32[1,3]{1,0:T(1,128)S(1)} %add.213), channel_id=1, source_target_pairs={{0,4},{1,5},{2,6},{3,7},{4,0},{5,1},{6,2},{7,3},{8,12},{9,13},{10,... | collective-permute-start | bytes 44 | tf_op jit(solution)/shard_map/ppermute | solution.py:49
  248.2 7.3 %collective-permute-start.26 = (f32[256,128]{1,0:T(8,128)S(1)}, f32[256,128]{1,0:T(8,128)S(1)}, u32[]{:S(2)}, u32[]{:S(2)}) collective-permute-start(f32[256,128]{1,0:T(8,128)S(1)} %slice.153), channel_id=1, source_target_pairs={{0,8},{1,9},{2,10},{3,11},{4,12},{5,13},{6,14},{7,15},{8,0},{9,1},... | collective-permute-start | bytes 393224 | tf_op jit(solution)/shard_map/ppermute | solution.py:49
  255.6 5.3 %collective-permute-start.27 = (f32[128,128]{1,0:T(8,128)S(1)}, f32[128,128]{1,0:T(8,128)S(1)}, u32[]{:S(2)}, u32[]{:S(2)}) collective-permute-start(f32[128,128]{1,0:T(8,128)S(1)} %slice.155), channel_id=1, source_target_pairs={{0,4},{1,5},{2,6},{3,7},{4,0},{5,1},{6,2},{7,3},{8,12},{9,13},{10,... | collective-permute-start | bytes 196616 | tf_op jit(solution)/shard_map/ppermute | solution.py:49
  267.0 1.1 collective-permute-start.28
  270.0 3.5 %collective-permute-start.29 = (f32[1,3]{1,0:T(1,128)S(1)}, f32[1,3]{1,0:T(1,128)S(1)}, u32[]{:S(2)}, u32[]{:S(2)}) collective-permute-start(f32[1,3]{1,0:T(1,128)S(1)} %fusion.29), channel_id=1, source_target_pairs={{0,2},{1,3},{2,0},{3,1},{4,6},{5,7},{6,4},{7,5},{8,10},{9,11},{10,... | collective-permute-start | bytes 44 | tf_op jit(solution)/shard_map/ppermute | solution.py:49
  275.5 4.4 %collective-permute-start.30 = (f32[1,3]{1,0:T(1,128)S(1)}, f32[1,3]{1,0:T(1,128)S(1)}, u32[]{:S(2)}, u32[]{:S(2)}) collective-permute-start(f32[1,3]{1,0:T(1,128)S(1)} %fusion.31), channel_id=1, source_target_pairs={{0,8},{1,9},{2,10},{3,11},{4,12},{5,13},{6,14},{7,15},{8,0},{9,1},... | collective-permute-start | bytes 44 | tf_op jit(solution)/shard_map/ppermute | solution.py:49
  279.9 3.5 %collective-permute-start.31 = (f32[1,3]{1,0:T(1,128)S(1)}, f32[1,3]{1,0:T(1,128)S(1)}, u32[]{:S(2)}, u32[]{:S(2)}) collective-permute-start(f32[1,3]{1,0:T(1,128)S(1)} %add.225), channel_id=1, source_target_pairs={{0,4},{1,5},{2,6},{3,7},{4,0},{5,1},{6,2},{7,3},{8,12},{9,13},{10,... | collective-permute-start | bytes 44 | tf_op jit(solution)/shard_map/ppermute | solution.py:49
  (17 other events, 97.8 us)

commit v2 on v1

v2 whole, which is shorter than its diff:
```python
import functools
import jax
import jax.numpy as jnp
import numpy as np
from jax import lax
from jax.experimental import pallas as pl
from jax.experimental.pallas import tpu as pltpu
from jax.sharding import PartitionSpec as P

LANES = 128
CUBE_ROWS = 8
CUBE_COLS = 16


def split(value):
    high = value.astype(jnp.bfloat16)
    low = (value - high.astype(jnp.float32)).astype(jnp.bfloat16)
    return high, low


def split_table(table):
    if isinstance(table, np.ndarray):
        table = table.astype(np.float32)
        high = table.astype(jnp.bfloat16)
        return jnp.asarray(high), jnp.asarray((table - high.astype(np.float32)).astype(jnp.bfloat16))
    high = lax.reduce_precision(table, 8, 7)
    return high.astype(jnp.bfloat16), (table - high).astype(jnp.bfloat16)


def dot_in(left, right):
    return jnp.dot(left, right, preferred_element_type=jnp.float32)


def dot_three(left, right):
    left_high, left_low = left
    right_high, right_low = right
    return dot_in(
        jnp.concatenate([left_high, left_low, left_high], axis=1),
        jnp.concatenate([right_high, right_high, right_low], axis=0),
    )


def partner_steps(members):
    return [1 << i for i in reversed(range(members.bit_length() - 1))]


def exchange(value, step):
    members = lax.axis_size("px")
    return lax.ppermute(value, "px", [(i, i ^ step) for i in range(members)])


def gather_pieces(piece, beside):
    steps = partner_steps(lax.axis_size("px"))
    pieces = piece[None]
    for step in steps[:-1]:
        pieces = jnp.concatenate([pieces, exchange(pieces, step)], axis=0)
    pieces, beside = lax.optimization_barrier((pieces, beside))
    return (pieces, exchange(pieces, steps[-1])), beside


def scatter_pieces(kept, sent):
    steps = list(reversed(partner_steps(lax.axis_size("px"))))
    pieces = kept + exchange(sent, steps[0])
    for step in steps[1:]:
        half = pieces.shape[0] // 2
        pieces = pieces[:half] + exchange(pieces[half:], step)
    return pieces


def total(value):
    for step in reversed(partner_steps(lax.axis_size("px"))):
        value = value + exchange(value, step)
    return value


def angle_tables(numerator, extent):
    angle = (2.0 * jnp.pi / extent) * (numerator % extent).astype(jnp.float32)
    return jnp.cos(angle), jnp.sin(angle)


def butterfly16(real, imag, sign):
    def four(a, b, c, d):
        (ar, ai), (br, bi), (cr, ci), (dr, di) = a, b, c, d
        sr, si, tr, ti = ar + cr, ai + ci, ar - cr, ai - ci
        ur, ui, vr, vi = br + dr, bi + di, br - dr, bi - di
        wr, wi = (-vi, vr) if sign > 0 else (vi, -vr)
        return (sr + ur, si + ui), (tr + wr, ti + wi), (sr - ur, si - ui), (tr - wr, ti - wi)

    def turned(value, power):
        power %= 16
        if power == 0:
            return value
        r, i = value
        cosine = float(np.cos(2 * np.pi * power / 16))
        sine = sign * float(np.sin(2 * np.pi * power / 16))
        if power == 4:
            return (-i, r) if sign > 0 else (i, -r)
        return (r * cosine - i * sine, r * sine + i * cosine)

    points = list(zip(real, imag))
    inner = [four(*(points[4 * j1 + j0] for j1 in range(4))) for j0 in range(4)]
    out = [None] * 16
    for b1 in range(4):
        column = [turned(inner[j0][b1], j0 * b1) for j0 in range(4)]
        for b0, value in enumerate(four(*column)):
            out[b1 + 4 * b0] = value
    return [v[0] for v in out], [v[1] for v in out]


def spectral_kernel(
    parts,
    extent,
    chunk,
    rows_ref,
    near_ref,
    distant_ref,
    onehot_ref,
    cube_high,
    cube_low,
    back_high,
    back_low,
    turn_high,
    turn_low,
    even_high,
    even_low,
    odd_high,
    odd_low,
    uneven_high,
    uneven_low,
    unodd_high,
    unodd_low,
    line_high,
    line_low,
    unline_high,
    unline_low,
    twist_ref,
    filter_ref,
    kept_ref,
    sent_ref,
    *scratch,
):
    grid = scratch[: 2 * parts]
    twin = scratch[2 * parts : 4 * parts]
    rows = scratch[4 * parts :]
    half_count = kept_ref.shape[0]
    pieces = near_ref.shape[0]
    blocks = half_count // pieces
    width = parts * LANES
    evens, odds = even_high.shape[0] // 2, odd_high.shape[0] // 2
    slabs = extent // CUBE_COLS

    def clear(i, _):
        for ref in grid + twin:
            ref[pl.ds(i * 64, 64), :] = jnp.zeros((64, LANES), jnp.float32)
        return 0

    lax.fori_loop(0, slabs * extent // 64, clear, 0)

    def turns(start):
        picked = onehot_ref[pl.ds(start, chunk), :]
        both = dot_in(picked, turn_high[...]) + dot_in(picked, turn_low[...])
        return both[:, :width], both[:, width:]

    def spread(source_ref, offset, step, _):
        start = pl.multiple_of(offset + step * chunk, chunk)
        taken = source_ref[pl.ds(step * (chunk // blocks), chunk // blocks), :blocks, :]
        values = split(taken.reshape(chunk, LANES))
        both = dot_three(values, (cube_high[...], cube_low[...]))
        real, imag = both[:, :width], both[:, width:]
        cosine, sine = turns(start)
        turned = (real * cosine + imag * sine, imag * cosine - real * sine)
        for part in range(2):
            for half in range(parts):
                rows[part * parts + half][...] = turned[part][:, half * LANES : (half + 1) * LANES]

        def add(i, _):
            for refs, place in ((grid, i), (twin, i + chunk // 2)):
                row = rows_ref[start + place]
                for ref, source in zip(refs, rows):
                    ref[pl.ds(row, 1), :] += source[pl.ds(place, 1), :]
            return 0

        lax.fori_loop(0, chunk // 2, add, 0, unroll=8)
        return 0

    for index, source_ref in enumerate((near_ref, distant_ref)):
        body = functools.partial(spread, source_ref, index * half_count)
        lax.fori_loop(0, half_count // chunk, body, 0)

    def across(sign):
        def body(i, _):
            start = pl.multiple_of(i * 8, 8)
            for half in range(parts):
                places = [pl.ds(start + slab * extent, 8) for slab in range(slabs)]
                real = [grid[half][place, :] for place in places]
                imag = [grid[parts + half][place, :] for place in places]
                if sign < 0:
                    real = [r + twin[half][place, :] for r, place in zip(real, places)]
                    imag = [r + twin[parts + half][place, :] for r, place in zip(imag, places)]
                real, imag = butterfly16(real, imag, sign)
                for place, r, j in zip(places, real, imag):
                    grid[half][place, :] = r
                    grid[parts + half][place, :] = j
            return 0

        lax.fori_loop(0, extent // 8, body, 0)

    across(-1)

    def middle(b, _):
        low = pl.ds(pl.multiple_of(b * extent, extent), extent // 2)
        high = pl.ds(pl.multiple_of(b * extent + extent // 2, extent // 2), extent // 2)

        def joined(place):
            return jnp.concatenate(
                [
                    jnp.concatenate(
                        [grid[part * parts + half][place, :] for half in range(parts)], axis=1
                    )
                    for part in range(2)
                ],
                axis=0,
            )

        first, last = joined(low), joined(high)
        even = dot_three((even_high[...], even_low[...]), split(first + last))
        odd = dot_three((odd_high[...], odd_low[...]), split(first - last))
        real = jnp.concatenate([even[:evens], odd[:odds]], axis=0)
        imag = jnp.concatenate([even[evens:], odd[odds:]], axis=0)
        twist_cos, twist_sin = twist_ref[b, 0:1, :], twist_ref[b, 1:2, :]
        twisted = (real * twist_cos + imag * twist_sin, imag * twist_cos - real * twist_sin)
        back = ([], [])
        for half in range(parts):
            cut = slice(half * LANES, (half + 1) * LANES)
            line = jnp.concatenate([twisted[0][:, cut], twisted[1][:, cut]], axis=1)
            full = dot_three(split(line), (line_high[...], line_low[...]))
            scale = filter_ref[b, :, cut]
            full = full * jnp.concatenate([scale, scale], axis=1)
            full = dot_three(split(full), (unline_high[...], unline_low[...]))
            back[0].append(full[:, :LANES])
            back[1].append(full[:, LANES:])
        real, imag = (jnp.concatenate(values, axis=1) for values in back)
        real, imag = real * twist_cos - imag * twist_sin, imag * twist_cos + real * twist_sin
        even = jnp.concatenate([real[:evens], imag[:evens]], axis=0)
        odd = jnp.concatenate([real[evens:], imag[evens:]], axis=0)
        even = dot_three((uneven_high[...], uneven_low[...]), split(even))
        odd = dot_three((unodd_high[...], unodd_low[...]), split(odd))
        for place, planes in ((low, even + odd), (high, even - odd)):
            for part in range(2):
                for half in range(parts):
                    grid[part * parts + half][place, :] = planes[
                        part * (extent // 2) : (part + 1) * (extent // 2),
                        half * LANES : (half + 1) * LANES,
                    ]
        return 0

    lax.fori_loop(0, slabs, middle, 0, unroll=4)
    across(1)

    def collect(out_ref, offset, step, _):
        start = pl.multiple_of(offset + step * chunk, chunk)

        def take(i, _):
            row = rows_ref[start + i]
            for ref, source in zip(rows, grid):
                ref[pl.ds(i, 1), :] = source[pl.ds(row, 1), :]
            return 0

        lax.fori_loop(0, chunk, take, 0, unroll=8)
        cosine, sine = turns(start)
        real = jnp.concatenate([rows[half][...] for half in range(parts)], axis=1)
        imag = jnp.concatenate([rows[parts + half][...] for half in range(parts)], axis=1)
        both = jnp.concatenate([real * cosine - imag * sine, imag * cosine + real * sine], axis=1)
        out_ref[pl.ds(pl.multiple_of(step * chunk, chunk), chunk), :] = dot_three(split(both), (back_high[...], back_low[...]))
        return 0

    for index, out_ref in enumerate((kept_ref, sent_ref)):
        body = functools.partial(collect, out_ref, index * half_count)
        lax.fori_loop(0, half_count // chunk, body, 0)


def spectral_tables(kernel_local):
    members = lax.axis_size("px")
    extent = kernel_local.shape[0]
    slab = kernel_local.shape[1]
    padded_slab = max(LANES // CUBE_COLS, slab)
    width = padded_slab * CUBE_COLS
    first = lax.axis_index("px") * slab
    column = jnp.arange(width, dtype=jnp.int32)
    k1 = first + column // CUBE_COLS
    real_slab = (column // CUBE_COLS < slab).astype(jnp.float32)
    point = jnp.arange(CUBE_ROWS * CUBE_COLS, dtype=jnp.int32)
    cosine, sine = angle_tables((point // CUBE_COLS)[:, None] * k1[None, :], extent)
    same = (point[:, None] % CUBE_COLS == column[None, :] % CUBE_COLS) * real_slab[None, :]
    cube = jnp.concatenate([cosine * same, -sine * same], axis=1)
    turn_row = jnp.arange(extent // CUBE_ROWS, dtype=jnp.int32) * CUBE_ROWS
    cosine, sine = angle_tables(turn_row[:, None] * k1[None, :], extent)
    turn = jnp.concatenate([cosine, sine], axis=1)
    half = extent // 2
    n0 = np.arange(half)
    k0_even = np.arange(0, -(-(half // 2 + 1) // 8) * 16, 2)
    k0_odd = np.arange(1, half, 2)
    k0 = np.concatenate([k0_even, k0_odd])
    planes = []
    for k0_part in (k0_even, k0_odd):
        angle = 2.0 * np.pi / extent * (k0_part[:, None] * n0[None, :] % extent)
        cosine, sine = np.cos(angle), np.sin(angle)
        planes.append(np.block([[cosine, sine], [-sine, cosine]]))
    inside = LANES // CUBE_COLS
    small = np.arange(CUBE_COLS)
    angle = 2.0 * np.pi / CUBE_COLS * (small[:, None] * small[None, :] % CUBE_COLS)
    cosine = np.kron(np.eye(inside), np.cos(angle))
    sine = np.kron(np.eye(inside), np.sin(angle))
    line = np.block([[cosine, -sine], [sine, cosine]])
    unline = np.block([[cosine, sine], [-sine, cosine]])
    lane = np.arange(width) % CUBE_COLS
    angle = 2.0 * np.pi / extent * (small[:, None] * lane[None, :])
    twist = np.stack([np.cos(angle), np.sin(angle)], axis=1)
    weight = np.where((k0 == 0) | (k0 == half), 1.0, 2.0) * (k0 <= half)
    weight = weight / float(extent) ** 3
    filters = jnp.concatenate(
        [kernel_local[: k0_even[-1] + 1 : 2], kernel_local[1:half:2]], axis=0
    )
    filters = filters * jnp.asarray(weight, jnp.float32)[:, None, None]
    filters = jnp.pad(filters, ((0, 0), (0, padded_slab - slab), (0, 0)))
    filters = filters.reshape(len(k0), padded_slab, extent // CUBE_COLS, CUBE_COLS)
    filters = filters.transpose(3, 0, 1, 2).reshape(CUBE_COLS, len(k0), width)
    tables = []
    for table in (cube, cube.T, turn, *planes, *(plane.T for plane in planes), line, unline):
        tables.extend(split_table(table))
    return tables + [jnp.asarray(twist, jnp.float32), filters]


def cube_places(cubes, extent):
    slabs = extent // CUBE_COLS
    turns = extent // CUBE_ROWS
    rows = (cubes % slabs) * extent + cubes // (turns * slabs)
    turn_index = cubes // slabs % turns
    onehot = turn_index[:, None] == jnp.arange(turns, dtype=jnp.int32)[None, :]
    return rows, onehot.astype(jnp.bfloat16)


def spectral(places, extent, blocks, gathered, tables):
    half_count = gathered[0].shape[0] * blocks
    parts = tables[-1].shape[2] // LANES
    slabs = extent // CUBE_COLS
    chunk = min(512, half_count)
    whole = pl.BlockSpec(memory_space=pltpu.VMEM)
    out = jax.ShapeDtypeStruct((half_count, LANES), jnp.float32)
    return pl.pallas_call(
        functools.partial(spectral_kernel, parts, extent, chunk),
        out_shape=(out, out),
        in_specs=[pl.BlockSpec(memory_space=pltpu.SMEM)] + [whole] * (3 + len(tables)),
        out_specs=(whole, whole),
        scratch_shapes=[pltpu.VMEM((slabs * extent, LANES), jnp.float32)] * (4 * parts)
        + [pltpu.VMEM((chunk, LANES), jnp.float32)] * (2 * parts),
        compiler_params=pltpu.CompilerParams(vmem_limit_bytes=56 * 1024 * 1024),
        name="spectral",
    )(places[0], *gathered, places[1], *tables)


NOTE_ROWS = 8
STEP_BLOCKS = 16
RIM_PART = 4


def sum_row(*values):
    lane = lax.broadcasted_iota(jnp.int32, (1, LANES), 1)
    row = jnp.zeros((1, LANES), jnp.float32)
    for index, value in enumerate(values):
        row = jnp.where(lane == index, value, row)
    return row


def put_edges(out_ref, values):
    step, steps = pl.program_id(0), pl.num_programs(0)
    panels = values.shape[1]
    below = out_ref.shape[0] - steps * STEP_BLOCKS // RIM_PART

    for first, lanes in ((0, slice(0, panels)), (steps - steps // RIM_PART, slice(panels, 2 * panels))):

        @pl.when((step >= first) & (step < first + steps // RIM_PART))
        def _():
            row = pl.multiple_of(below + (step - first) * STEP_BLOCKS, 8)
            out_ref[pl.ds(row, STEP_BLOCKS), lanes] = values


def project_kernel(proj_ref, values_ref, note_ref, out_ref):
    step = pl.program_id(0)
    charges = jnp.sum(proj_ref[...] * values_ref[...][:, :, None], axis=1)
    out_ref[pl.ds(pl.multiple_of(step * STEP_BLOCKS, STEP_BLOCKS), STEP_BLOCKS), :] = charges

    put_edges(out_ref, values_ref[...])

    @pl.when(step == pl.num_programs(0) - 1)
    def _():
        blocks = pl.num_programs(0) * STEP_BLOCKS
        out_ref[blocks : blocks + NOTE_ROWS, :] = jnp.broadcast_to(
            note_ref[...], (NOTE_ROWS, LANES)
        )


def complete_kernel(proj_ref, picked_ref, base_ref, rhs_ref, image_ref, out_ref):
    step = pl.program_id(0)
    tiles = proj_ref[...]
    image = base_ref[...] + jnp.sum(tiles * picked_ref[...][:, None, :], axis=2)
    image_ref[...] = image
    charges = jnp.sum(tiles * image[:, :, None], axis=1)
    out_ref[pl.ds(pl.multiple_of(step * STEP_BLOCKS, STEP_BLOCKS), STEP_BLOCKS), :] = charges
    put_edges(out_ref, image)
    blocks = pl.num_programs(0) * STEP_BLOCKS
    rhs = rhs_ref[...]
    row = sum_row(jnp.sum(rhs * rhs), jnp.sum(rhs * image), jnp.sum(image * image))

    @pl.when(step == 0)
    def _():
        out_ref[blocks : blocks + NOTE_ROWS, :] = jnp.zeros((NOTE_ROWS, LANES), jnp.float32)

    out_ref[blocks : blocks + 1, :] += row


def vector_scalars(sums):
    norm_sq, mixed, image_sq = sums[0:1, 0:1], sums[0:1, 1:2], sums[0:1, 2:3]
    gram_one = image_sq / norm_sq
    return jnp.sqrt(norm_sq), mixed / norm_sq, gram_one, jnp.sqrt(gram_one)


def close_kernel(proj_ref, picked_ref, base_ref, rhs_ref, first_ref, sums_ref, image_ref, out_ref):
    step = pl.program_id(0)
    second = base_ref[...] + jnp.sum(proj_ref[...] * picked_ref[...][:, None, :], axis=2)
    initial_norm, diag_one, _, scale = vector_scalars(sums_ref[...])
    basis_one = rhs_ref[...] / initial_norm
    image_one = first_ref[...] / initial_norm
    image_two = (second / initial_norm - diag_one * image_one) / scale
    image_ref[...] = image_two
    row = sum_row(
        jnp.sum(basis_one * image_two),
        jnp.sum(image_one * image_two),
        jnp.sum(image_two * image_two),
    )

    @pl.when(step == 0)
    def _():
        out_ref[...] = jnp.zeros((NOTE_ROWS, LANES), jnp.float32)

    out_ref[0:1, :] += row


def finish_kernel(rhs_ref, first_ref, image_ref, sums_ref, last_ref, answer_ref, residual_ref, rows_ref):
    initial_norm, diag_one, gram_one, scale = vector_scalars(sums_ref[...])
    last = last_ref[...]
    upper_two, gram_cross, gram_two = last[0:1, 0:1], last[0:1, 1:2], last[0:1, 2:3]
    rhs = rhs_ref[...]
    basis_one = rhs / initial_norm
    image_one = first_ref[...] / initial_norm
    basis_two = (image_one - diag_one * basis_one) / scale
    determinant = gram_one * gram_two - gram_cross * gram_cross
    weight_one = initial_norm * (diag_one * gram_two - upper_two * gram_cross) / determinant
    weight_two = initial_norm * (upper_two * gram_one - diag_one * gram_cross) / determinant
    half = rhs.shape[0] // 2
    for out_ref, value in (
        (answer_ref, weight_one * basis_one + weight_two * basis_two),
        (residual_ref, rhs - weight_one * image_one - weight_two * image_ref[...]),
    ):
        rows_ref[...] = value
        out_ref[...] = jnp.concatenate(
            [rows_ref[pl.ds(side, half, stride=2), :] for side in range(2)], axis=1
        )


def local_call(kernel, name, proj_tiles, rows, whole, outs):
    blocks, panels, points = proj_tiles.shape

    def cut(width):
        return pl.BlockSpec((STEP_BLOCKS, width), lambda i: (i, 0))

    def uncut(shape):
        return pl.BlockSpec(shape, lambda i: (0, 0))

    out_specs = [cut(out[1]) if out[0] == blocks else uncut(out) for out in outs]
    return pl.pallas_call(
        kernel,
        grid=(blocks // STEP_BLOCKS,),
        out_shape=[jax.ShapeDtypeStruct(out, jnp.float32) for out in outs],
        in_specs=[pl.BlockSpec((STEP_BLOCKS, panels, points), lambda i: (i, 0, 0))]
        + [cut(row.shape[1]) for row in rows]
        + [uncut(value.shape) for value in whole],
        out_specs=out_specs,
        cost_estimate=pl.CostEstimate(
            flops=4 * proj_tiles.size, bytes_accessed=4 * proj_tiles.size, transcendentals=0
        ),
        compiler_params=pltpu.CompilerParams(vmem_limit_bytes=16 * 1024 * 1024),
        name=name,
    )(proj_tiles, *rows, *whole)


def piece_place(device):
    steps = partner_steps(lax.axis_size("px"))[:-1]
    away = lax.axis_index("px") ^ device
    return sum((away // step % 2) << place for place, step in enumerate(steps))


def halo(cells, distant):
    me, members = lax.axis_index("px"), lax.axis_size("px")
    width = cells.shape[0] // RIM_PART
    panels = cells.shape[1]
    sides = []
    for device, lane, present in ((me - 1, panels, me > 0), (me + 1, 0, me < members - 1)):
        place = jnp.where(present, piece_place(device), 0)
        start = (place, distant.shape[1] - width, lane)
        edge = lax.dynamic_slice(distant, start, (1, width, panels))[0]
        sides.append(jnp.where(present, edge, 0.0))
    return jnp.concatenate([sides[0], cells, sides[1]], axis=0)


def on_device(
    right_side, self_term, proj_tiles, owner_dev, cube_slot, near_src, near_tiles, kernel_hat
):
    members = lax.axis_size("px")
    blocks = proj_tiles.shape[0]
    extent = kernel_hat.shape[0]
    cubes_dev = extent // members * (extent // CUBE_ROWS) * (extent // CUBE_COLS)
    self_local = self_term.reshape(blocks, 64)
    cubes = owner_dev[:, 0] * cubes_dev + cube_slot
    tables = spectral_tables(kernel_hat)

    rhs = right_side.reshape(blocks, 64)
    note_shape = (blocks + NOTE_ROWS + blocks // RIM_PART, LANES)

    def base_of(values, gathered):
        sources = halo(values, gathered[1])[near_src].reshape(blocks, near_tiles.shape[2])
        return self_local * values + jnp.sum(near_tiles * sources[:, None, :], axis=2)

    def far(places, gathered):
        return scatter_pieces(*spectral(places, extent, blocks, gathered, tables))

    note = jnp.pad(cubes.astype(jnp.float32)[None, :], ((0, 0), (0, LANES - blocks)))
    (payload,) = local_call(project_kernel, "project", proj_tiles, [rhs], [note], [note_shape])
    gathered, tables = gather_pieces(payload, tables)
    base = base_of(rhs, gathered)
    all_cubes = jnp.concatenate([half[:, blocks, :blocks] for half in gathered], axis=0)
    places = cube_places(all_cubes.astype(jnp.int32).reshape(members * blocks), extent)
    first, payload = local_call(
        complete_kernel,
        "complete",
        proj_tiles,
        [far(places, gathered), base, rhs],
        [],
        [(blocks, 64), note_shape],
    )
    gathered, _ = gather_pieces(payload, ())
    base = base_of(first, gathered)
    sums = sum(jnp.sum(half[:, blocks, :], axis=0, keepdims=True) for half in gathered)
    image, last = local_call(
        close_kernel,
        "close",
        proj_tiles,
        [far(places, gathered), base, rhs, first],
        [sums],
        [(blocks, 64), (NOTE_ROWS, LANES)],
    )
    last = total(last)
    out = jax.ShapeDtypeStruct((blocks // 2, 128), jnp.float32)
    answer, residual = pl.pallas_call(
        finish_kernel,
        out_shape=(out, out),
        scratch_shapes=[pltpu.VMEM((blocks, 64), jnp.float32)],
        name="finish",
    )(rhs, first, image, sums, last)
    return (answer.reshape(blocks * 64), residual.reshape(blocks * 64))


def solution(mesh):
    return jax.shard_map(
        on_device,
        mesh=mesh,
        in_specs=(
            P(("groups", "px")),
            P(("groups", "px")),
            P(("groups", "px"), None, None),
            P(("groups", "px"), None),
            P(("groups", "px")),
            P(("groups", "px"), None),
            P(("groups", "px"), None, None),
            P(None, "px", None),
        ),
        out_specs=(P(("groups", "px")), P(("groups", "px"))),
        check_vma=False,
    )
```

time: 291 us -> 231 us (0.79)
  Pallas kernels: 123 us -> 103 us
  other arithmetic: 39.4 us -> 21.5 us
  starting transfers between devices: 42 us -> 26.1 us
  between operations: 9.83 us -> 1 us
  waiting for transfers between devices: 49.9 us -> 55.5 us
  local copies, waits for them, and re-layouts: 25.6 us -> 22.4 us
    pallas_call x2, Pallas kernels: 123 us -> 92.1 us  [spectral(): pl.pallas_call(functools.partial(spectral_kernel, parts, extent, chunk),...]
    pallas_call x0 -> x4, Pallas kernels: none -> 11.4 us  [the longest x3 9.46 us: local_call(): pl.pallas_call(kernel, grid=(blocks // STEP_BLOCKS,), out_shape=[jax.Shap...]
    ppermute x28 -> x20, starting transfers between devices: 35.4 us -> 26.1 us  [exchange(): return lax.ppermute(value, 'px', [(i, i ^ step) for i in range(members)])]
    reduce_sum x8 -> x4, other arithmetic: 17.2 us -> 8.28 us  [the longest x2 6.71 us: base_of(): jnp.sum(near_tiles * sources[:, None, :], axis=2)]
    add x8 -> x4, other arithmetic: 7.9 us -> 0.61 us  [total(): value = value + exchange(value, step)]
    ppermute x4 -> x0, starting transfers between devices: 6.66 us -> none  [the longest x2 3.91 us: halo(): lax.ppermute(cells[-width:], 'px', [(i, i + 1) for i in range(ends)])]
    optimization_barrier x0 -> x4, local copies, waits for them, and re-layouts: none -> 6.64 us  [gather_pieces(): pieces, beside = lax.optimization_barrier((pieces, beside))]
    ppermute x28 -> x20, waiting for transfers between devices: 49.9 us -> 55.5 us  [exchange(): return lax.ppermute(value, 'px', [(i, i ^ step) for i in range(members)])]
  transfers between devices with their start and end apart: 32 -> 20, of which waited for: 18 -> 16; matrix products, arithmetic and copies ran while one was open for 14% -> 14% of each run, Pallas kernels for 0% -> 0%
where the time goes in v2:
time: 231 us; the launch traced here: 230 us
  Pallas kernels  103 us (45%)
  waiting for transfers between devices  55.5 us (24%)
  starting transfers between devices  26.1 us (11%)
  local copies, waits for them, and re-layouts  22.4 us (10%)
  other arithmetic  21.5 us (9%)
    pallas_call x2, Pallas kernels, spectral(): pl.pallas_call(functools.partial(spectral_kernel, parts, extent, chunk),...  92.1 us
    ppermute x20, waiting for transfers between devices, exchange(): return lax.ppermute(value, 'px', [(i, i ^ step) for i in range(members)])  55.5 us
    ppermute x20, starting transfers between devices, exchange(): return lax.ppermute(value, 'px', [(i, i ^ step) for i in range(members)])  26.1 us
    pallas_call x3, Pallas kernels, local_call(): pl.pallas_call(kernel, grid=(blocks // STEP_BLOCKS,), out_shape=[jax.Shap...  9.46 us
    unnamed x32, local copies, waits for them, and re-layouts  7.38 us
    reduce_sum x2, other arithmetic, base_of(): jnp.sum(near_tiles * sources[:, None, :], axis=2)  6.71 us
    optimization_barrier x4, local copies, waits for them, and re-layouts, gather_pieces(): pieces, beside = lax.optimization_barrier((pieces, beside))  6.64 us
  transfers between devices with their start and end apart: 20, of which 16 were waited for; matrix products, arithmetic and copies ran while one was open for 14% of the time, Pallas kernels for 0%

profile of v2, /device:TPU:0, one launch (start us, length us, event | category | flops | bytes accessed | tf_op | source)
XLA Modules:
  0.0 230.0 jit_solution(10960961869912201265)
XLA Ops:
  2.2 2.2 copy-done
  4.4 1.9 project.1
  6.3 4.1 %collective-permute-start = (f32[1,168,128]{2,0,1:T(1,128)S(1)}, f32[1,168,128]{2,0,1:T(1,128)S(1)}, u32[]{:S(2)}, u32[]{:S(2)}) collective-permute-start(f32[1,168,128]{2,0,1:T(1,128)S(1)} %bitcast.45), channel_id=1, source_target_pairs={{0,8},{1,9},{2,10},{3,11},{4,12},{5,13},{6,14},{7,15},{8,0},{9,1},... | collective-permute-start | bytes 258056 | tf_op jit(solution)/shard_map/ppermute | solution.py:49
  10.4 1.1 slice.55
  11.5 1.8 copy.45
  13.4 1.8 copy.44
  15.2 2.7 %fusion = f32[16,136,16,16]{1,0,3,2:T(8,128)S(1)} fusion(f32[64,16,16,16]{0,3,2,1:T(8,128)S(1)} %bitcast.54, f32[72,16,16,16]{0,3,2,1:T(8,128)} %bitcast.55, f32[136]{0:T(256)S(1)} %copy-done.13), kind=kLoop, calls=%fused_computation.3 | loop fusion | flops 1114112 | bytes 4456992 | tf_op jit(solution)/shard_map/transpose | solution.py:327
  18.0 4.4 %copy.34 = f32[16,136,16,16]{1,3,2,0:T(8,128)} copy(f32[16,136,16,16]{1,0,3,2:T(8,128)S(1)} %fusion) | data formatting | bytes 4456448 | tf_op jit(solution)/shard_map/transpose | solution.py:327
  23.2 1.6 collective-permute-start.1
  25.0 4.0 %collective-permute-done.1 = f32[2,168,128]{2,0,1:T(2,128)S(1)} collective-permute-done((f32[2,168,128]{2,0,1:T(2,128)S(1)}, f32[2,168,128]{2,0,1:T(2,128)S(1)}, u32[]{:S(2)}, u32[]{:S(2)}) %collective-permute-start.1) | collective-permute-done | bytes 172064 | tf_op jit(solution)/shard_map/ppermute | solution.py:49
  29.3 1.6 collective-permute-start.2
  32.3 5.7 %collective-permute-done.2 = f32[4,168,128]{2,0,1:T(4,128)S(1)} collective-permute-done((f32[4,168,128]{2,0,1:T(4,128)S(1)}, f32[4,168,128]{2,0,1:T(4,128)S(1)}, u32[]{:S(2)}, u32[]{:S(2)}) %collective-permute-start.2) | collective-permute-done | bytes 344096 | tf_op jit(solution)/shard_map/ppermute | solution.py:49
  40.1 4.9 %copy.39.filter_ref = f32[16,136,256]{2,1,0:T(8,128)} copy(f32[16,136,256]{1,2,0:T(8,128)} %bitcast.53) | data formatting | bytes 4456448 | tf_op jit(solution)/shard_map/optimization_barrier | solution.py:57
  45.7 1.1 fusion.1.onehot_ref
  46.8 46.0 %spectral.2 = (f32[1024,128]{1,0:T(8,128)}, f32[1024,128]{1,0:T(8,128)}) custom-call(s32[2048]{0:T(1024)} %get-tuple-element.75.rows_ref, f32[8,168,128]{2,1,0:T(8,128)} %copy-done.8, f32[8,168,128]{2,1,0:T(8,128)} %copy-done.10, bf16[2048,32]{1,0:T(8,128)(2,1)} %fusion.1.onehot_ref, bf16[128,512]{1,0:T(8,128)(2,1)} %copy.37.cube_high, ...), custom_call_target="tpu_custom_call" | custom-call | tf_op jit(solution)/shard_map/spectral/pallas_call | solution.py:350
  93.6 1.5 collective-permute-done.4
  95.1 1.1 add.208
  96.3 1.6 collective-permute-start.5
  99.6 5.3 %collective-permute-done.5 = f32[512,128]{1,0:T(8,128)S(1)} collective-permute-done((f32[512,128]{1,0:T(8,128)S(1)}, f32[512,128]{1,0:T(8,128)S(1)}, u32[]{:S(2)}, u32[]{:S(2)}) %collective-permute-start.5) | collective-permute-done | bytes 262176 | tf_op jit(solution)/shard_map/ppermute | solution.py:49
  105.0 1.6 collective-permute-start.6
  106.6 3.4 %multiply_reduce_fusion.1 = f32[128,64]{1,0:T(8,128)S(1)} fusion(f32[128,64,128]{2,1,0:T(8,128)} %param.28, f32[128,128]{1,0:T(8,128)S(1)} %mul.144), kind=kLoop, calls=%fused_computation.5 | loop fusion | flops 2088960 | bytes 4292608 | tf_op jit(solution)/shard_map/reduce_sum | solution.py:532
  110.9 4.3 %collective-permute-done.7 = f32[128,128]{1,0:T(8,128)S(1)} collective-permute-done((f32[128,128]{1,0:T(8,128)S(1)}, f32[128,128]{1,0:T(8,128)S(1)}, u32[]{:S(2)}, u32[]{:S(2)}) %collective-permute-start.7) | collective-permute-done | bytes 65568 | tf_op jit(solution)/shard_map/ppermute | solution.py:49
  115.3 4.1 %complete.1 = (f32[128,64]{1,0:T(8,128)S(1)}, f32[168,128]{1,0:T(8,128)S(1)}) custom-call(f32[128,64,128]{2,1,0:T(8,128)S(1)} %copy-done.1, f32[128,128]{1,0:T(8,128)S(1)} %slice_add_fusion.5.picked_ref, f32[128,64]{1,0:T(8,128)S(1)} %multiply_add_fusion.1.base_ref, f32[128,64]{1,0:T(8,128)S(1)} %reshape.151.values_ref.rhs_ref), custom_call_target="tpu_custom_call" | custom-call | flops 4194304 | bytes 4194304 | tf_op jit(solution)/shard_map/complete/pallas_call | solution.py:481
  119.4 1.0 collective-permute-start.8
  120.4 4.5 %collective-permute-done.8 = f32[1,168,128]{2,1,0:T(8,128)S(1)} collective-permute-done((f32[1,168,128]{2,1,0:T(8,128)S(1)}, f32[1,168,128]{2,1,0:T(8,128)S(1)}, u32[]{:S(2)}, u32[]{:S(2)}) %collective-permute-start.8) | collective-permute-done | bytes 86048 | tf_op jit(solution)/shard_map/ppermute | solution.py:49
  124.9 2.6 %collective-permute-start.9 = (f32[2,168,128]{2,1,0:T(8,128)S(1)}, f32[2,168,128]{2,1,0:T(8,128)S(1)}, u32[]{:S(2)}, u32[]{:S(2)}) collective-permute-start(f32[2,168,128]{2,1,0:T(8,128)S(1)} %pad_maximum_fusion.6), channel_id=1, source_target_pairs={{0,4},{1,5},{2,6},{3,7},{4,0},{5,1},{6,2},{7,3},{8,12},{9,13},{10,... | collective-permute-start | bytes 516104 | tf_op jit(solution)/shard_map/ppermute | solution.py:49
  127.5 3.4 %collective-permute-done.9 = f32[2,168,128]{2,1,0:T(8,128)S(1)} collective-permute-done((f32[2,168,128]{2,1,0:T(8,128)S(1)}, f32[2,168,128]{2,1,0:T(8,128)S(1)}, u32[]{:S(2)}, u32[]{:S(2)}) %collective-permute-start.9) | collective-permute-done | bytes 172064 | tf_op jit(solution)/shard_map/ppermute | solution.py:49
  130.9 1.5 collective-permute-start.10
  132.4 5.8 %collective-permute-done.10 = f32[4,168,128]{2,1,0:T(8,128)S(1)} collective-permute-done((f32[4,168,128]{2,1,0:T(8,128)S(1)}, f32[4,168,128]{2,1,0:T(8,128)S(1)}, u32[]{:S(2)}, u32[]{:S(2)}) %collective-permute-start.10) | collective-permute-done | bytes 344096 | tf_op jit(solution)/shard_map/ppermute | solution.py:49
  138.4 2.1 collective-permute-done.11.distant_ref
  141.3 46.1 %spectral.3 = (f32[1024,128]{1,0:T(8,128)}, f32[1024,128]{1,0:T(8,128)}) custom-call(s32[2048]{0:T(1024)} %get-tuple-element.75.rows_ref, f32[8,168,128]{2,1,0:T(8,128)} %copy-done.7, f32[8,168,128]{2,1,0:T(8,128)} %copy-done.11, bf16[2048,32]{1,0:T(8,128)(2,1)} %fusion.1.onehot_ref, bf16[128,512]{1,0:T(8,128)(2,1)} %copy.37.cube_high, ...), custom_call_target="tpu_custom_call" | custom-call | tf_op jit(solution)/shard_map/spectral/pallas_call | solution.py:350
  190.1 1.3 add.227
  191.4 1.5 collective-permute-start.13
  192.9 3.4 %multiply_reduce_fusion = f32[128,64]{1,0:T(8,128)S(1)} fusion(f32[128,64,128]{2,1,0:T(8,128)} %param.28, f32[128,128]{1,0:T(8,128)S(1)} %mul.148), kind=kLoop, calls=%fused_computation.4 | loop fusion | flops 2088960 | bytes 4292608 | tf_op jit(solution)/shard_map/reduce_sum | solution.py:532
  196.2 3.7 %collective-permute-done.13 = f32[512,128]{1,0:T(8,128)S(1)} collective-permute-done((f32[512,128]{1,0:T(8,128)S(1)}, f32[512,128]{1,0:T(8,128)S(1)}, u32[]{:S(2)}, u32[]{:S(2)}) %collective-permute-start.13) | collective-permute-done | bytes 262176 | tf_op jit(solution)/shard_map/ppermute | solution.py:49
  200.0 2.1 collective-permute-start.14
  202.9 2.4 %collective-permute-done.14 = f32[256,128]{1,0:T(8,128)S(1)} collective-permute-done((f32[256,128]{1,0:T(8,128)S(1)}, f32[256,128]{1,0:T(8,128)S(1)}, u32[]{:S(2)}, u32[]{:S(2)}) %collective-permute-start.14) | collective-permute-done | bytes 131104 | tf_op jit(solution)/shard_map/ppermute | solution.py:49
  205.3 1.0 collective-permute-start.15
  206.3 4.2 %collective-permute-done.15 = f32[128,128]{1,0:T(8,128)S(1)} collective-permute-done((f32[128,128]{1,0:T(8,128)S(1)}, f32[128,128]{1,0:T(8,128)S(1)}, u32[]{:S(2)}, u32[]{:S(2)}) %collective-permute-start.15) | collective-permute-done | bytes 65568 | tf_op jit(solution)/shard_map/ppermute | solution.py:49
  210.6 3.4 %close.1 = (f32[128,64]{1,0:T(8,128)S(1)}, f32[8,128]{1,0:T(8,128)S(1)}) custom-call(f32[128,64,128]{2,1,0:T(8,128)S(1)} %copy-done.2, f32[128,128]{1,0:T(8,128)S(1)} %slice_add_fusion.4.picked_ref, f32[128,64]{1,0:T(8,128)S(1)} %multiply_add_fusion.base_ref, f32[128,64]{1,0:T(8,128)S(1)} %reshape.151.values_ref.rhs_ref, ...), custom_call_target="tpu_custom_call" | custom-call | flops 4194304 | bytes 4194304 | tf_op jit(solution)/shard_map/close/pallas_call | solution.py:481
  214.6 1.2 collective-permute-done.16
  215.8 1.5 collective-permute-start.17
  217.3 2.1 collective-permute-done.17
  219.4 1.8 collective-permute-start.18
  221.2 1.8 collective-permute-done.18
  223.0 1.1 collective-permute-start.19
  224.1 3.4 %collective-permute-done.19 = f32[8,128]{1,0:T(8,128)S(1)} collective-permute-done((f32[8,128]{1,0:T(8,128)S(1)}, f32[8,128]{1,0:T(8,128)S(1)}, u32[]{:S(2)}, u32[]{:S(2)}) %collective-permute-start.19) | collective-permute-done | bytes 4128 | tf_op jit(solution)/shard_map/ppermute | solution.py:49
  228.1 1.9 finish.1
  (97 shorter events, 16.3 us)
Async XLA Ops:
  1.5 209.1 %copy-start.3 = (f32[128,64]{1,0:T(8,128)}, f32[128,64]{1,0:T(8,128)S(1)}, u32[]{:S(2)}) copy-start(f32[128,64]{1,0:T(8,128)S(1)} %reshape.151.values_ref.rhs_ref) | copy-start | bytes 98308
  2.2 2.2 copy-start
  4.4 6.0 %copy-start.9 = (f32[256,16,256]{2,1,0:T(8,128)S(1)}, f32[256,16,256]{2,1,0:T(8,128)}, u32[]{:S(2)}) copy-start(f32[256,16,256]{2,1,0:T(8,128)} %param.29) | copy-start | bytes 12582916
  6.3 16.7 %collective-permute-start = (f32[1,168,128]{2,0,1:T(1,128)S(1)}, f32[1,168,128]{2,0,1:T(1,128)S(1)}, u32[]{:S(2)}, u32[]{:S(2)}) collective-permute-start(f32[1,168,128]{2,0,1:T(1,128)S(1)} %bitcast.45), channel_id=1, source_target_pairs={{0,8},{1,9},{2,10},{3,11},{4,12},{5,13},{6,14},{7,15},{8,0},{9,1},... | collective-permute-start | bytes 258056 | tf_op jit(solution)/shard_map/ppermute | solution.py:49
  11.4 3.8 %copy-start.13 = (f32[136]{0:T(256)S(1)}, f32[136]{0:T(256)}, u32[]{:S(2)}) copy-start(f32[136]{0:T(256)} %constant.277.clone) | copy-start | bytes 1636
  23.2 5.9 %collective-permute-start.1 = (f32[2,168,128]{2,0,1:T(2,128)S(1)}, f32[2,168,128]{2,0,1:T(2,128)S(1)}, u32[]{:S(2)}, u32[]{:S(2)}) collective-permute-start(f32[2,168,128]{2,0,1:T(2,128)S(1)} %pad_maximum_fusion.5), channel_id=1, source_target_pairs={{0,4},{1,5},{2,6},{3,7},{4,0},{5,1},{6,2},{7,3},{8,12},{9,13},{10,... | collective-permute-start | bytes 516104 | tf_op jit(solution)/shard_map/ppermute | solution.py:49
  29.3 8.7 %collective-permute-start.2 = (f32[4,168,128]{2,0,1:T(4,128)S(1)}, f32[4,168,128]{2,0,1:T(4,128)S(1)}, u32[]{:S(2)}, u32[]{:S(2)}) collective-permute-start(f32[4,168,128]{2,0,1:T(4,128)S(1)} %pad_maximum_fusion.2), channel_id=1, source_target_pairs={{0,2},{1,3},{2,0},{3,1},{4,6},{5,7},{6,4},{7,5},{8,10},{9,11},{10,... | collective-permute-start | bytes 1032200 | tf_op jit(solution)/shard_map/ppermute | solution.py:49
  38.5 8.4 %copy-start.8 = (f32[8,168,128]{2,1,0:T(8,128)}, f32[8,168,128]{2,1,0:T(8,128)S(1)}, u32[]{:S(2)}) copy-start(f32[8,168,128]{2,1,0:T(8,128)S(1)} %copy.35.near_ref) | copy-start | bytes 2064388
  38.5 6.6 %collective-permute-start.3 = (f32[8,168,128]{2,1,0:T(8,128)S(1)}, f32[8,168,128]{2,1,0:T(8,128)S(1)}, u32[]{:S(2)}, u32[]{:S(2)}) collective-permute-start(f32[8,168,128]{2,1,0:T(8,128)S(1)} %copy.35.near_ref), channel_id=1, source_target_pairs={{0,1},{1,0},{2,3},{3,2},{4,5},{5,4},{6,7},{7,6},{8,9},{9,8},{10,11... | collective-permute-start | bytes 2064392 | tf_op jit(solution)/shard_map/ppermute | solution.py:49
  45.0 48.3 %copy-start.14 = (s32[128,2]{0,1:T(2,128)S(1)}, s32[128,2]{0,1:T(2,128)}, u32[]{:S(2)}) copy-start(s32[128,2]{0,1:T(2,128)} %param.27) | copy-start | bytes 3076
  45.1 1.8 copy-start.10
  46.8 51.0 %copy-start.12 = (f32[8192]{0:T(1024)S(1)}, f32[8192]{0:T(1024)}, u32[]{:S(2)}) copy-start(f32[8192]{0:T(1024)} %param.23) | copy-start | bytes 98308
  92.9 2.2 collective-permute-start.4
  96.3 8.7 %collective-permute-start.5 = (f32[512,128]{1,0:T(8,128)S(1)}, f32[512,128]{1,0:T(8,128)S(1)}, u32[]{:S(2)}, u32[]{:S(2)}) collective-permute-start(f32[512,128]{1,0:T(8,128)S(1)} %slice.78), channel_id=1, source_target_pairs={{0,2},{1,3},{2,0},{3,1},{4,6},{5,7},{6,4},{7,5},{8,10},{9,11},{10,... | collective-permute-start | bytes 786440 | tf_op jit(solution)/shard_map/ppermute | solution.py:49
  99.6 15.6 %copy-start.1 = (f32[128,64,128]{2,1,0:T(8,128)S(1)}, f32[128,64,128]{2,1,0:T(8,128)}, u32[]{:S(2)}) copy-start(f32[128,64,128]{2,1,0:T(8,128)} %proj_ref.5) | copy-start | bytes 12582916
  105.0 5.0 %collective-permute-start.6 = (f32[256,128]{1,0:T(8,128)S(1)}, f32[256,128]{1,0:T(8,128)S(1)}, u32[]{:S(2)}, u32[]{:S(2)}) collective-permute-start(f32[256,128]{1,0:T(8,128)S(1)} %slice.80), channel_id=1, source_target_pairs={{0,4},{1,5},{2,6},{3,7},{4,0},{5,1},{6,2},{7,3},{8,12},{9,13},{10,... | collective-permute-start | bytes 393224 | tf_op jit(solution)/shard_map/ppermute | solution.py:49
  110.0 5.2 %collective-permute-start.7 = (f32[128,128]{1,0:T(8,128)S(1)}, f32[128,128]{1,0:T(8,128)S(1)}, u32[]{:S(2)}, u32[]{:S(2)}) collective-permute-start(f32[128,128]{1,0:T(8,128)S(1)} %slice.82), channel_id=1, source_target_pairs={{0,8},{1,9},{2,10},{3,11},{4,12},{5,13},{6,14},{7,15},{8,0},{9,1},... | collective-permute-start | bytes 196616 | tf_op jit(solution)/shard_map/ppermute | solution.py:49
  119.4 91.2 %copy-start.4 = (f32[128,64]{1,0:T(8,128)}, f32[128,64]{1,0:T(8,128)S(1)}, u32[]{:S(2)}) copy-start(f32[128,64]{1,0:T(8,128)S(1)} %get-tuple-element.56.first_ref) | copy-start | bytes 98308
  119.4 5.4 %collective-permute-start.8 = (f32[1,168,128]{2,1,0:T(8,128)S(1)}, f32[1,168,128]{2,1,0:T(8,128)S(1)}, u32[]{:S(2)}, u32[]{:S(2)}) collective-permute-start(f32[1,168,128]{2,1,0:T(8,128)S(1)} %bitcast.49), channel_id=1, source_target_pairs={{0,8},{1,9},{2,10},{3,11},{4,12},{5,13},{6,14},{7,15},{8,0},{9,1},... | collective-permute-start | bytes 258056 | tf_op jit(solution)/shard_map/ppermute | solution.py:49
  124.9 6.0 %collective-permute-start.9 = (f32[2,168,128]{2,1,0:T(8,128)S(1)}, f32[2,168,128]{2,1,0:T(8,128)S(1)}, u32[]{:S(2)}, u32[]{:S(2)}) collective-permute-start(f32[2,168,128]{2,1,0:T(8,128)S(1)} %pad_maximum_fusion.6), channel_id=1, source_target_pairs={{0,4},{1,5},{2,6},{3,7},{4,0},{5,1},{6,2},{7,3},{8,12},{9,13},{10,... | collective-permute-start | bytes 516104 | tf_op jit(solution)/shard_map/ppermute | solution.py:49
  130.9 7.3 %collective-permute-start.10 = (f32[4,168,128]{2,1,0:T(8,128)S(1)}, f32[4,168,128]{2,1,0:T(8,128)S(1)}, u32[]{:S(2)}, u32[]{:S(2)}) collective-permute-start(f32[4,168,128]{2,1,0:T(8,128)S(1)} %pad_maximum_fusion.3), channel_id=1, source_target_pairs={{0,2},{1,3},{2,0},{3,1},{4,6},{5,7},{6,4},{7,5},{8,10},{9,11},{10,... | collective-permute-start | bytes 1032200 | tf_op jit(solution)/shard_map/ppermute | solution.py:49
  138.3 2.2 copy-start.7
  138.3 2.2 collective-permute-start.11
  140.5 0.9 copy-start.11
  187.4 2.6 %collective-permute-start.12 = (f32[1024,128]{1,0:T(8,128)}, f32[1024,128]{1,0:T(8,128)S(1)}, u32[]{:S(2)}, u32[]{:S(2)}) collective-permute-start(f32[1024,128]{1,0:T(8,128)} %get-tuple-element.59), channel_id=1, source_target_pairs={{0,1},{1,0},{2,3},{3,2},{4,5},{5,4},{6,7},{7,6},{8,9},{9,8},{10,11... | collective-permute-start | bytes 1572872 | tf_op jit(solution)/shard_map/ppermute | solution.py:49
  190.0 20.6 %copy-start.2 = (f32[128,64,128]{2,1,0:T(8,128)S(1)}, f32[128,64,128]{2,1,0:T(8,128)}, u32[]{:S(2)}) copy-start(f32[128,64,128]{2,1,0:T(8,128)} %proj_ref.5) | copy-start | bytes 12582916
  191.4 8.6 %collective-permute-start.13 = (f32[512,128]{1,0:T(8,128)S(1)}, f32[512,128]{1,0:T(8,128)S(1)}, u32[]{:S(2)}, u32[]{:S(2)}) collective-permute-start(f32[512,128]{1,0:T(8,128)S(1)} %slice.84), channel_id=1, source_target_pairs={{0,2},{1,3},{2,0},{3,1},{4,6},{5,7},{6,4},{7,5},{8,10},{9,11},{10,... | collective-permute-start | bytes 786440 | tf_op jit(solution)/shard_map/ppermute | solution.py:49
  200.0 5.3 %collective-permute-start.14 = (f32[256,128]{1,0:T(8,128)S(1)}, f32[256,128]{1,0:T(8,128)S(1)}, u32[]{:S(2)}, u32[]{:S(2)}) collective-permute-start(f32[256,128]{1,0:T(8,128)S(1)} %slice.86), channel_id=1, source_target_pairs={{0,4},{1,5},{2,6},{3,7},{4,0},{5,1},{6,2},{7,3},{8,12},{9,13},{10,... | collective-permute-start | bytes 393224 | tf_op jit(solution)/shard_map/ppermute | solution.py:49
  205.3 5.2 %collective-permute-start.15 = (f32[128,128]{1,0:T(8,128)S(1)}, f32[128,128]{1,0:T(8,128)S(1)}, u32[]{:S(2)}, u32[]{:S(2)}) collective-permute-start(f32[128,128]{1,0:T(8,128)S(1)} %slice.88), channel_id=1, source_target_pairs={{0,8},{1,9},{2,10},{3,11},{4,12},{5,13},{6,14},{7,15},{8,0},{9,1},... | collective-permute-start | bytes 196616 | tf_op jit(solution)/shard_map/ppermute | solution.py:49
  206.3 21.8 %copy-start.6 = (f32[1,128]{1,0:T(1,128)}, f32[1,128]{1,0:T(1,128)S(1)}, u32[]{:S(2)}) copy-start(f32[1,128]{1,0:T(1,128)S(1)} %add_bitcast_fusion.sums_ref) | copy-start | bytes 1540
  214.0 0.6 copy-start.5
  214.6 1.2 collective-permute-start.16
  215.8 3.6 %collective-permute-start.17 = (f32[8,128]{1,0:T(8,128)S(1)}, f32[8,128]{1,0:T(8,128)S(1)}, u32[]{:S(2)}, u32[]{:S(2)}) collective-permute-start(f32[8,128]{1,0:T(8,128)S(1)} %add.234), channel_id=1, source_target_pairs={{0,2},{1,3},{2,0},{3,1},{4,6},{5,7},{6,4},{7,5},{8,10},{9,11},{10,... | collective-permute-start | bytes 12296 | tf_op jit(solution)/shard_map/ppermute | solution.py:49
  219.4 3.6 %collective-permute-start.18 = (f32[8,128]{1,0:T(8,128)S(1)}, f32[8,128]{1,0:T(8,128)S(1)}, u32[]{:S(2)}, u32[]{:S(2)}) collective-permute-start(f32[8,128]{1,0:T(8,128)S(1)} %add.235), channel_id=1, source_target_pairs={{0,4},{1,5},{2,6},{3,7},{4,0},{5,1},{6,2},{7,3},{8,12},{9,13},{10,... | collective-permute-start | bytes 12296 | tf_op jit(solution)/shard_map/ppermute | solution.py:49
  223.0 4.5 %collective-permute-start.19 = (f32[8,128]{1,0:T(8,128)S(1)}, f32[8,128]{1,0:T(8,128)S(1)}, u32[]{:S(2)}, u32[]{:S(2)}) collective-permute-start(f32[8,128]{1,0:T(8,128)S(1)} %add.236), channel_id=1, source_target_pairs={{0,8},{1,9},{2,10},{3,11},{4,12},{5,13},{6,14},{7,15},{8,0},{9,1},... | collective-permute-start | bytes 12296 | tf_op jit(solution)/shard_map/ppermute | solution.py:49

commit v3 on v2

--- a/solution.py
+++ b/solution.py
@@ -18,26 +18,8 @@
     return high, low
 
 
-def split_table(table):
-    if isinstance(table, np.ndarray):
-        table = table.astype(np.float32)
-        high = table.astype(jnp.bfloat16)
-        return jnp.asarray(high), jnp.asarray((table - high.astype(np.float32)).astype(jnp.bfloat16))
-    high = lax.reduce_precision(table, 8, 7)
-    return high.astype(jnp.bfloat16), (table - high).astype(jnp.bfloat16)
-
-
 def dot_in(left, right):
     return jnp.dot(left, right, preferred_element_type=jnp.float32)
-
-
-def dot_three(left, right):
-    left_high, left_low = left
-    right_high, right_low = right
-    return dot_in(
-        jnp.concatenate([left_high, left_low, left_high], axis=1),
-        jnp.concatenate([right_high, right_high, right_low], axis=0),
-    )
 
 
 def partner_steps(members):
@@ -71,11 +53,6 @@
     for step in reversed(partner_steps(lax.axis_size("px"))):
         value = value + exchange(value, step)
     return value
-
-
-def angle_tables(numerator, extent):
-    angle = (2.0 * jnp.pi / extent) * (numerator % extent).astype(jnp.float32)
-    return jnp.cos(angle), jnp.sin(angle)
 
 
 def butterfly16(real, imag, sign):
@@ -107,154 +84,172 @@
     return [v[0] for v in out], [v[1] for v in out]
 
 
-def spectral_kernel(
-    parts,
-    extent,
-    chunk,
-    rows_ref,
-    near_ref,
-    distant_ref,
-    onehot_ref,
-    cube_high,
-    cube_low,
-    back_high,
-    back_low,
-    turn_high,
-    turn_low,
-    even_high,
-    even_low,
-    odd_high,
-    odd_low,
-    uneven_high,
-    uneven_low,
-    unodd_high,
-    unodd_low,
-    line_high,
-    line_low,
-    unline_high,
-    unline_low,
-    twist_ref,
-    filter_ref,
-    kept_ref,
-    sent_ref,
-    *scratch,
-):
-    grid = scratch[: 2 * parts]
-    twin = scratch[2 * parts : 4 * parts]
-    rows = scratch[4 * parts :]
+def left_terms(value):
+    high, low = split(value)
+    return jnp.concatenate([high, low, high], axis=1)
+
+
+def right_terms(value):
+    high, low = split(value)
+    return jnp.concatenate([high, high, low], axis=0)
+
+
+def where_equal(left, right):
+    return jnp.where(left == right, 1.0, 0.0).astype(jnp.bfloat16)
+
+
+COPIES = 2
+
+
+def spectral_kernel(extent, chunk, constants, rows_ref, near_ref, distant_ref, codes_ref, *refs):
+    cube_ref, back_ref, turn_ref = refs[:3]
+    sources = refs[3 : 3 + constants]
+    kept_ref, sent_ref = refs[3 + constants : 5 + constants]
+    refs = refs[5 + constants :]
+    tables, refs = refs[:constants], refs[constants:]
+    grids, refs = refs[: 2 * COPIES], refs[2 * COPIES :]
+    grids = [grids[2 * i : 2 * i + 2] for i in range(COPIES)]
+    rows, dense, sem = refs[:2], refs[2], refs[3]
+    even_ref, odd_ref, uneven_ref, unodd_ref = tables[:4]
+    line_ref, unline_ref, twist_ref, filter_ref = tables[4:8]
+    plane_ref, unplane_ref, full_ref, unfull_ref, edge_ref = tables[8:]
     half_count = kept_ref.shape[0]
-    pieces = near_ref.shape[0]
-    blocks = half_count // pieces
-    width = parts * LANES
-    evens, odds = even_high.shape[0] // 2, odd_high.shape[0] // 2
+    blocks = half_count // near_ref.shape[0]
     slabs = extent // CUBE_COLS
+    half = extent // 2
+    moves = [
+        pltpu.make_async_copy(source, table, sem.at[i])
+        for i, (source, table) in enumerate(zip(sources, tables))
+    ]
+    for move in moves:
+        move.start()
 
     def clear(i, _):
-        for ref in grid + twin:
-            ref[pl.ds(i * 64, 64), :] = jnp.zeros((64, LANES), jnp.float32)
+        place = pl.ds(pl.multiple_of(i * 64, 64), 64)
+        for grid in grids:
+            for ref in grid:
+                ref[place, :] = jnp.zeros((64, LANES), jnp.float32)
         return 0
 
     lax.fori_loop(0, slabs * extent // 64, clear, 0)
-
-    def turns(start):
-        picked = onehot_ref[pl.ds(start, chunk), :]
-        both = dot_in(picked, turn_high[...]) + dot_in(picked, turn_low[...])
-        return both[:, :width], both[:, width:]
+    dense[...] = jnp.zeros(dense.shape, jnp.float32)
+
+    def marks(start):
+        codes = codes_ref[pl.ds(start, chunk), :]
+        turn_count = extent // CUBE_ROWS
+        wide = lax.broadcasted_iota(jnp.int32, (chunk, extent), 1)
+        turn_lane = lax.broadcasted_iota(jnp.int32, (chunk, 2 * turn_count), 1) % turn_count
+        turned = dot_in(where_equal(turn_lane, codes[:, 1:2]), turn_ref[...])
+        return codes, wide, turned[:, :LANES], turned[:, LANES:]
 
     def spread(source_ref, offset, step, _):
         start = pl.multiple_of(offset + step * chunk, chunk)
         taken = source_ref[pl.ds(step * (chunk // blocks), chunk // blocks), :blocks, :]
-        values = split(taken.reshape(chunk, LANES))
-        both = dot_three(values, (cube_high[...], cube_low[...]))
-        real, imag = both[:, :width], both[:, width:]
-        cosine, sine = turns(start)
-        turned = (real * cosine + imag * sine, imag * cosine - real * sine)
-        for part in range(2):
-            for half in range(parts):
-                rows[part * parts + half][...] = turned[part][:, half * LANES : (half + 1) * LANES]
+        both = dot_in(left_terms(taken.reshape(chunk, LANES)), cube_ref[...])
+        codes, wide, cosine, sine = marks(start)
+        real, imag = both[:, :LANES], both[:, LANES : 2 * LANES]
+        rows[0][...] = real * cosine + imag * sine
+        rows[1][...] = imag * cosine - real * sine
+        high, low = split(jnp.where(wide // CUBE_COLS == codes[:, 2:3], both[:, 2 * LANES :], 0.0))
+        plane = where_equal(wide, codes[:, 0:1])
+        contract = (((0,), (0,)), ((), ()))
+        dense[...] += lax.dot_general(
+            plane, high, contract, preferred_element_type=jnp.float32
+        ) + lax.dot_general(plane, low, contract, preferred_element_type=jnp.float32)
 
         def add(i, _):
-            for refs, place in ((grid, i), (twin, i + chunk // 2)):
+            for copy in range(COPIES):
+                place = i + copy * (chunk // COPIES)
                 row = rows_ref[start + place]
-                for ref, source in zip(refs, rows):
+                for ref, source in zip(grids[copy], rows):
                     ref[pl.ds(row, 1), :] += source[pl.ds(place, 1), :]
             return 0
 
-        lax.fori_loop(0, chunk // 2, add, 0, unroll=8)
+        lax.fori_loop(0, chunk // COPIES, add, 0, unroll=8)
         return 0
 
     for index, source_ref in enumerate((near_ref, distant_ref)):
         body = functools.partial(spread, source_ref, index * half_count)
         lax.fori_loop(0, half_count // chunk, body, 0)
 
+    grid_real, grid_imag = grids[0]
+
     def across(sign):
         def body(i, _):
             start = pl.multiple_of(i * 8, 8)
-            for half in range(parts):
-                places = [pl.ds(start + slab * extent, 8) for slab in range(slabs)]
-                real = [grid[half][place, :] for place in places]
-                imag = [grid[parts + half][place, :] for place in places]
+            places = [pl.ds(start + slab * extent, 8) for slab in range(slabs)]
+            values = []
+            for part in range(2):
+                values.append([grids[0][part][place, :] for place in places])
                 if sign < 0:
-                    real = [r + twin[half][place, :] for r, place in zip(real, places)]
-                    imag = [r + twin[parts + half][place, :] for r, place in zip(imag, places)]
-                real, imag = butterfly16(real, imag, sign)
-                for place, r, j in zip(places, real, imag):
-                    grid[half][place, :] = r
-                    grid[parts + half][place, :] = j
+                    for grid in grids[1:]:
+                        values[part] = [v + grid[part][p, :] for v, p in zip(values[part], places)]
+            values = butterfly16(*values, sign)
+            for place, r, j in zip(places, *values):
+                grid_real[place, :] = r
+                grid_imag[place, :] = j
             return 0
 
         lax.fori_loop(0, extent // 8, body, 0)
 
     across(-1)
-
-    def middle(b, _):
-        low = pl.ds(pl.multiple_of(b * extent, extent), extent // 2)
-        high = pl.ds(pl.multiple_of(b * extent + extent // 2, extent // 2), extent // 2)
-
-        def joined(place):
+    for move in moves:
+        move.wait()
+
+    def middle(pair, _):
+        starts = [pl.multiple_of((2 * pair + i) * extent, extent) for i in range(2)]
+
+        def joined(offset):
             return jnp.concatenate(
                 [
-                    jnp.concatenate(
-                        [grid[part * parts + half][place, :] for half in range(parts)], axis=1
-                    )
-                    for part in range(2)
+                    jnp.concatenate([ref[pl.ds(start + offset, half), :] for start in starts], axis=1)
+                    for ref in grids[0]
                 ],
                 axis=0,
             )
 
-        first, last = joined(low), joined(high)
-        even = dot_three((even_high[...], even_low[...]), split(first + last))
-        odd = dot_three((odd_high[...], odd_low[...]), split(first - last))
-        real = jnp.concatenate([even[:evens], odd[:odds]], axis=0)
-        imag = jnp.concatenate([even[evens:], odd[odds:]], axis=0)
-        twist_cos, twist_sin = twist_ref[b, 0:1, :], twist_ref[b, 1:2, :]
-        twisted = (real * twist_cos + imag * twist_sin, imag * twist_cos - real * twist_sin)
-        back = ([], [])
-        for half in range(parts):
-            cut = slice(half * LANES, (half + 1) * LANES)
-            line = jnp.concatenate([twisted[0][:, cut], twisted[1][:, cut]], axis=1)
-            full = dot_three(split(line), (line_high[...], line_low[...]))
-            scale = filter_ref[b, :, cut]
-            full = full * jnp.concatenate([scale, scale], axis=1)
-            full = dot_three(split(full), (unline_high[...], unline_low[...]))
-            back[0].append(full[:, :LANES])
-            back[1].append(full[:, LANES:])
-        real, imag = (jnp.concatenate(values, axis=1) for values in back)
-        real, imag = real * twist_cos - imag * twist_sin, imag * twist_cos + real * twist_sin
-        even = jnp.concatenate([real[:evens], imag[:evens]], axis=0)
-        odd = jnp.concatenate([real[evens:], imag[evens:]], axis=0)
-        even = dot_three((uneven_high[...], uneven_low[...]), split(even))
-        odd = dot_three((unodd_high[...], unodd_low[...]), split(odd))
-        for place, planes in ((low, even + odd), (high, even - odd)):
-            for part in range(2):
-                for half in range(parts):
-                    grid[part * parts + half][place, :] = planes[
-                        part * (extent // 2) : (part + 1) * (extent // 2),
-                        half * LANES : (half + 1) * LANES,
+        first, last = joined(0), joined(half)
+        even = dot_in(even_ref[...], right_terms(first + last))
+        odd = dot_in(odd_ref[...], right_terms(first - last))
+        real = jnp.concatenate([even[:half], odd[:half]], axis=0)
+        imag = jnp.concatenate([even[half:], odd[half:]], axis=0)
+        cosine, sine = twist_ref[pair, 0:1, :], twist_ref[pair, 1:2, :]
+        real, imag = real * cosine + imag * sine, imag * cosine - real * sine
+        lines = jnp.concatenate(
+            [
+                jnp.concatenate([real[:, cut], imag[:, cut]], axis=1)
+                for cut in (slice(0, LANES), slice(LANES, 2 * LANES))
+            ],
+            axis=0,
+        )
+        lines = dot_in(left_terms(lines), line_ref[...])
+        scale = jnp.concatenate([filter_ref[2 * pair], filter_ref[2 * pair + 1]], axis=0)
+        lines = lines * jnp.concatenate([scale, scale], axis=1)
+        lines = dot_in(left_terms(lines), unline_ref[...])
+        real = jnp.concatenate([lines[:extent, :LANES], lines[extent:, :LANES]], axis=1)
+        imag = jnp.concatenate([lines[:extent, LANES:], lines[extent:, LANES:]], axis=1)
+        real, imag = real * cosine - imag * sine, imag * cosine + real * sine
+        even = jnp.concatenate([real[:half], imag[:half]], axis=0)
+        odd = jnp.concatenate([real[half:], imag[half:]], axis=0)
+        even = dot_in(uneven_ref[...], right_terms(even))
+        odd = dot_in(unodd_ref[...], right_terms(odd))
+        for offset, planes in ((0, even + odd), (half, even - odd)):
+            for part, ref in enumerate(grids[0]):
+                for i, start in enumerate(starts):
+                    ref[pl.ds(start + offset, half), :] = planes[
+                        part * half : (part + 1) * half, i * LANES : (i + 1) * LANES
                     ]
         return 0
 
-    lax.fori_loop(0, slabs, middle, 0, unroll=4)
+    lax.fori_loop(0, slabs // 2, middle, 0, unroll=2)
+    planes = dot_in(plane_ref[...], right_terms(dense[...]))
+    some = planes.shape[0] // 2
+    planes = jnp.concatenate([planes[:some], planes[some:]], axis=1)
+    planes = dot_in(left_terms(planes), full_ref[...])
+    planes = planes * jnp.concatenate([edge_ref[...], edge_ref[...]], axis=1)
+    planes = dot_in(left_terms(planes), unfull_ref[...])
+    planes = jnp.concatenate([planes[:, :extent], planes[:, extent:]], axis=0)
+    dense[...] = dot_in(unplane_ref[...], right_terms(planes))
     across(1)
 
     def collect(out_ref, offset, step, _):
@@ -262,16 +257,23 @@
 
         def take(i, _):
             row = rows_ref[start + i]
-            for ref, source in zip(rows, grid):
+            for ref, source in zip(rows, grids[0]):
                 ref[pl.ds(i, 1), :] = source[pl.ds(row, 1), :]
             return 0
 
-        lax.fori_loop(0, chunk, take, 0, unroll=8)
-        cosine, sine = turns(start)
-        real = jnp.concatenate([rows[half][...] for half in range(parts)], axis=1)
-        imag = jnp.concatenate([rows[parts + half][...] for half in range(parts)], axis=1)
-        both = jnp.concatenate([real * cosine - imag * sine, imag * cosine + real * sine], axis=1)
-        out_ref[pl.ds(pl.multiple_of(step * chunk, chunk), chunk), :] = dot_three(split(both), (back_high[...], back_low[...]))
+        lax.fori_loop(0, chunk, take, 0, unroll=16)
+        codes, wide, cosine, sine = marks(start)
+        plane = where_equal(wide, codes[:, 0:1])
+        high, low = split(dense[...])
+        edge = dot_in(plane, high) + dot_in(plane, low)
+        edge = jnp.where(wide // CUBE_COLS == codes[:, 2:3], edge, 0.0)
+        real, imag = rows[0][...], rows[1][...]
+        both = jnp.concatenate(
+            [real * cosine - imag * sine, imag * cosine + real * sine, edge], axis=1
+        )
+        out_ref[pl.ds(pl.multiple_of(step * chunk, chunk), chunk), :] = dot_in(
+            left_terms(both), back_ref[...]
+        )
         return 0
 
     for index, out_ref in enumerate((kept_ref, sent_ref)):
@@ -279,84 +281,204 @@
         lax.fori_loop(0, half_count // chunk, body, 0)
 
 
+def stacked_table(table, axis):
+    table = np.asarray(table, np.float32)
+    high = table.astype(jnp.bfloat16)
+    low = (table - high.astype(np.float32)).astype(jnp.bfloat16)
+    order = [high, high, low] if axis == 0 else [high, low, high]
+    return jnp.asarray(np.concatenate(order, axis=axis))
+
+
+def constant_tables(extent):
+    half = extent // 2
+    n0 = np.arange(half)
+    planes = []
+    for k0 in (np.arange(0, extent, 2), np.arange(1, extent, 2)):
+        angle = 2.0 * np.pi / extent * (k0[:, None] * n0[None, :] % extent)
+        cosine, sine = np.cos(angle), np.sin(angle)
+        planes.append(np.block([[cosine, sine], [-sine, cosine]]))
+    small = np.arange(CUBE_COLS)
+    angle = 2.0 * np.pi / CUBE_COLS * (small[:, None] * small[None, :] % CUBE_COLS)
+    cosine = np.kron(np.eye(LANES // CUBE_COLS), np.cos(angle))
+    sine = np.kron(np.eye(LANES // CUBE_COLS), np.sin(angle))
+    line = np.block([[cosine, -sine], [sine, cosine]])
+    angle = 2.0 * np.pi / extent * (small[:, None] * (np.arange(LANES) % CUBE_COLS)[None, :])
+    twist = np.stack([np.cos(angle), np.sin(angle)], axis=1)
+    twist = np.concatenate([twist[0::2], twist[1::2]], axis=2)
+    some = np.arange(-(-(half + 1) // 8) * 8)
+    whole = np.arange(extent)
+    angle = 2.0 * np.pi / extent * (some[:, None] * whole[None, :] % extent)
+    plane = np.concatenate([np.cos(angle), -np.sin(angle)], axis=0)
+    angle = 2.0 * np.pi / extent * (whole[:, None] * whole[None, :] % extent)
+    cosine, sine = np.cos(angle), np.sin(angle)
+    full = np.block([[cosine, -sine], [sine, cosine]])
+    first = [stacked_table(table, 1) for table in (*planes, planes[0].T, planes[1].T)]
+    first += [stacked_table(line, 0), stacked_table(line.T, 0), jnp.asarray(twist, jnp.float32)]
+    last = [stacked_table(plane, 1), stacked_table(plane.T, 1)]
+    last += [stacked_table(full, 0), stacked_table(full.T, 0)]
+    return first, last
+
+
+def tables_kernel(
+    extent, slab, place_ref, kernel_ref, sort_ref, cube_ref, back_ref, turn_ref, filter_ref, *lines
+):
+    first, shift = place_ref[0], place_ref[1]
+    held = slab // 2
+    points = CUBE_ROWS * CUBE_COLS
+
+    def angles(numerator):
+        angle = (2.0 * np.pi / extent) * (numerator % extent).astype(jnp.float32)
+        return jnp.cos(angle), jnp.sin(angle)
+
+    for shape, axis in (((points, LANES), 0), ((LANES, points), 1)):
+        point = lax.broadcasted_iota(jnp.int32, shape, axis)
+        column = lax.broadcasted_iota(jnp.int32, shape, 1 - axis)
+        k1 = first + column // CUBE_COLS
+        cosine, sine = angles((point // CUBE_COLS) * k1)
+        same = (point % CUBE_COLS == column % CUBE_COLS) & (column // CUBE_COLS < held)
+        shape = (points, extent) if axis == 0 else (extent, points)
+        point = lax.broadcasted_iota(jnp.int32, shape, axis)
+        column = lax.broadcasted_iota(jnp.int32, shape, 1 - axis)
+        flip = 1.0 - 2.0 * ((point // CUBE_COLS) % 2).astype(jnp.float32)
+        edge = jnp.where(point % CUBE_COLS == column % CUBE_COLS, flip, 0.0)
+        table = jnp.concatenate(
+            [jnp.where(same, cosine, 0.0), jnp.where(same, -sine, 0.0), edge], axis=1 - axis
+        )
+        (cube_ref if axis == 0 else back_ref)[...] = right_terms(table)
+    shape = (extent // CUBE_ROWS, LANES)
+    column = lax.broadcasted_iota(jnp.int32, shape, 1)
+    turn = lax.broadcasted_iota(jnp.int32, shape, 0) * CUBE_ROWS
+    high, low = split(jnp.concatenate(angles(turn * (first + column // CUBE_COLS)), axis=1))
+    turn_ref[...] = jnp.concatenate([high, low], axis=0)
+
+    batch = 512
+
+    def sort(i, _):
+        place = pl.ds(pl.multiple_of(i * batch, batch), batch)
+        values = kernel_ref[place, :]
+        high = values.astype(jnp.bfloat16)
+        rest = values - high.astype(jnp.float32)
+        middle, low = split(rest)
+        terms = jnp.concatenate([high, middle, low], axis=1)
+        values = dot_in(terms, sort_ref[...])
+        for side, ref in enumerate(lines):
+            ref[place, :] = values[:, side * LANES : (side + 1) * LANES]
+        return 0
+
+    lax.fori_loop(0, extent * slab // batch, sort, 0)
+    groups = LANES // CUBE_COLS
+    lane = lax.broadcasted_iota(jnp.int32, (1, LANES), 1)
+    k1 = first + lane // CUBE_COLS
+    weight = jnp.where(k1 == 0, 1.0, 2.0) / float(extent) ** 3
+    weight = jnp.where(lane // CUBE_COLS < held, weight, 0.0)
+    count = 32
+    for odd in range(2):
+
+        def turn_over(i, _):
+            for side, ref in enumerate(lines):
+                values = [
+                    ref[
+                        pl.ds(shift + k + (2 * i * count + odd) * slab, count, stride=2 * slab), :
+                    ]
+                    if k < held
+                    else jnp.zeros((count, LANES), jnp.float32)
+                    for k in range(groups)
+                ]
+                group = lax.broadcasted_iota(jnp.int32, (count, LANES), 1) // CUBE_COLS
+                step = 1
+                while step < groups:
+                    upper = group // step % 2 == 1
+                    turned = list(values)
+                    for k in range(groups):
+                        if k // step % 2 == 0:
+                            one, two = values[k], values[k + step]
+                            turned[k] = jnp.where(upper, pltpu.roll(two, step * CUBE_COLS, 1), one)
+                            turned[k + step] = jnp.where(
+                                upper, two, pltpu.roll(one, LANES - step * CUBE_COLS, 1)
+                            )
+                    values = turned
+                    step *= 2
+                row = pl.multiple_of(odd * (extent // 2) + i * count, count)
+                for k in range(groups):
+                    filter_ref[side * groups + k, pl.ds(row, count), :] = values[k] * weight
+            return 0
+
+        lax.fori_loop(0, extent // 2 // count, turn_over, 0)
+
+
 def spectral_tables(kernel_local):
     members = lax.axis_size("px")
-    extent = kernel_local.shape[0]
-    slab = kernel_local.shape[1]
-    padded_slab = max(LANES // CUBE_COLS, slab)
-    width = padded_slab * CUBE_COLS
-    first = lax.axis_index("px") * slab
-    column = jnp.arange(width, dtype=jnp.int32)
-    k1 = first + column // CUBE_COLS
-    real_slab = (column // CUBE_COLS < slab).astype(jnp.float32)
-    point = jnp.arange(CUBE_ROWS * CUBE_COLS, dtype=jnp.int32)
-    cosine, sine = angle_tables((point // CUBE_COLS)[:, None] * k1[None, :], extent)
-    same = (point[:, None] % CUBE_COLS == column[None, :] % CUBE_COLS) * real_slab[None, :]
-    cube = jnp.concatenate([cosine * same, -sine * same], axis=1)
-    turn_row = jnp.arange(extent // CUBE_ROWS, dtype=jnp.int32) * CUBE_ROWS
-    cosine, sine = angle_tables(turn_row[:, None] * k1[None, :], extent)
-    turn = jnp.concatenate([cosine, sine], axis=1)
-    half = extent // 2
-    n0 = np.arange(half)
-    k0_even = np.arange(0, -(-(half // 2 + 1) // 8) * 16, 2)
-    k0_odd = np.arange(1, half, 2)
-    k0 = np.concatenate([k0_even, k0_odd])
-    planes = []
-    for k0_part in (k0_even, k0_odd):
-        angle = 2.0 * np.pi / extent * (k0_part[:, None] * n0[None, :] % extent)
-        cosine, sine = np.cos(angle), np.sin(angle)
-        planes.append(np.block([[cosine, sine], [-sine, cosine]]))
-    inside = LANES // CUBE_COLS
-    small = np.arange(CUBE_COLS)
-    angle = 2.0 * np.pi / CUBE_COLS * (small[:, None] * small[None, :] % CUBE_COLS)
-    cosine = np.kron(np.eye(inside), np.cos(angle))
-    sine = np.kron(np.eye(inside), np.sin(angle))
-    line = np.block([[cosine, -sine], [sine, cosine]])
-    unline = np.block([[cosine, sine], [-sine, cosine]])
-    lane = np.arange(width) % CUBE_COLS
-    angle = 2.0 * np.pi / extent * (small[:, None] * lane[None, :])
-    twist = np.stack([np.cos(angle), np.sin(angle)], axis=1)
-    weight = np.where((k0 == 0) | (k0 == half), 1.0, 2.0) * (k0 <= half)
-    weight = weight / float(extent) ** 3
-    filters = jnp.concatenate(
-        [kernel_local[: k0_even[-1] + 1 : 2], kernel_local[1:half:2]], axis=0
+    me = lax.axis_index("px")
+    extent, slab = kernel_local.shape[:2]
+    shift = (me >= members // 2).astype(jnp.int32)
+    k2 = np.arange(extent)
+    sort = np.zeros((extent, extent), np.float32)
+    sort[k2, k2 % CUBE_COLS * CUBE_COLS + k2 // CUBE_COLS] = 1.0
+    whole = pl.BlockSpec(memory_space=pltpu.VMEM)
+    points = CUBE_ROWS * CUBE_COLS
+    size = 2 * LANES + extent
+    cube, back, turn, filters = pl.pallas_call(
+        functools.partial(tables_kernel, extent, slab),
+        out_shape=(
+            jax.ShapeDtypeStruct((3 * points, size), jnp.bfloat16),
+            jax.ShapeDtypeStruct((3 * size, points), jnp.bfloat16),
+            jax.ShapeDtypeStruct((2 * extent // CUBE_ROWS, 2 * LANES), jnp.bfloat16),
+            jax.ShapeDtypeStruct((CUBE_COLS, extent, LANES), jnp.float32),
+        ),
+        in_specs=[pl.BlockSpec(memory_space=pltpu.SMEM), whole, whole],
+        out_specs=(whole,) * 4,
+        scratch_shapes=[pltpu.VMEM((extent * slab, LANES), jnp.float32)] * 2,
+        cost_estimate=pl.CostEstimate(
+            flops=2 * extent * slab * 3 * extent * extent,
+            bytes_accessed=8 * extent * slab * extent,
+            transcendentals=0,
+        ),
+        compiler_params=pltpu.CompilerParams(vmem_limit_bytes=32 * 1024 * 1024),
+        name="tables",
+    )(
+        jnp.stack([me * slab + shift, shift]),
+        kernel_local.reshape(extent * slab, extent),
+        jnp.asarray(np.concatenate([sort] * 3, axis=0), jnp.bfloat16),
     )
-    filters = filters * jnp.asarray(weight, jnp.float32)[:, None, None]
-    filters = jnp.pad(filters, ((0, 0), (0, padded_slab - slab), (0, 0)))
-    filters = filters.reshape(len(k0), padded_slab, extent // CUBE_COLS, CUBE_COLS)
-    filters = filters.transpose(3, 0, 1, 2).reshape(CUBE_COLS, len(k0), width)
-    tables = []
-    for table in (cube, cube.T, turn, *planes, *(plane.T for plane in planes), line, unline):
-        tables.extend(split_table(table))
-    return tables + [jnp.asarray(twist, jnp.float32), filters]
+    first, last = constant_tables(extent)
+    some = last[0].shape[0] // 2
+    k0 = np.arange(some)
+    weight = np.where((k0 == 0) | (k0 == extent // 2), 1.0, 2.0) * (k0 <= extent // 2)
+    weight = jnp.asarray(weight / float(extent) ** 3, jnp.float32)[:, None]
+    edge = jnp.where(me == members // 2, kernel_local[:some, 0, :] * weight, 0.0)
+    return cube, back, turn, (*first, filters, *last, edge)
 
 
 def cube_places(cubes, extent):
     slabs = extent // CUBE_COLS
     turns = extent // CUBE_ROWS
-    rows = (cubes % slabs) * extent + cubes // (turns * slabs)
-    turn_index = cubes // slabs % turns
-    onehot = turn_index[:, None] == jnp.arange(turns, dtype=jnp.int32)[None, :]
-    return rows, onehot.astype(jnp.bfloat16)
+    plane, turn, slab = cubes // (turns * slabs), cubes // slabs % turns, cubes % slabs
+    codes = jnp.stack([plane, turn, slab] + [jnp.zeros_like(slab)] * 5, axis=1)
+    return slab * extent + plane, codes
 
 
 def spectral(places, extent, blocks, gathered, tables):
+    cube, back, turn, constants = tables
     half_count = gathered[0].shape[0] * blocks
-    parts = tables[-1].shape[2] // LANES
     slabs = extent // CUBE_COLS
     chunk = min(512, half_count)
     whole = pl.BlockSpec(memory_space=pltpu.VMEM)
     out = jax.ShapeDtypeStruct((half_count, LANES), jnp.float32)
     return pl.pallas_call(
-        functools.partial(spectral_kernel, parts, extent, chunk),
+        functools.partial(spectral_kernel, extent, chunk, len(constants)),
         out_shape=(out, out),
-        in_specs=[pl.BlockSpec(memory_space=pltpu.SMEM)] + [whole] * (3 + len(tables)),
+        in_specs=[pl.BlockSpec(memory_space=pltpu.SMEM)]
+        + [whole] * 6
+        + [pl.BlockSpec(memory_space=pl.ANY)] * len(constants),
         out_specs=(whole, whole),
-        scratch_shapes=[pltpu.VMEM((slabs * extent, LANES), jnp.float32)] * (4 * parts)
-        + [pltpu.VMEM((chunk, LANES), jnp.float32)] * (2 * parts),
-        compiler_params=pltpu.CompilerParams(vmem_limit_bytes=56 * 1024 * 1024),
+        scratch_shapes=[pltpu.VMEM(table.shape, table.dtype) for table in constants]
+        + [pltpu.VMEM((slabs * extent, LANES), jnp.float32)] * (2 * COPIES)
+        + [pltpu.VMEM((chunk, LANES), jnp.float32)] * 2
+        + [pltpu.VMEM((extent, extent), jnp.float32)]
+        + [pltpu.SemaphoreType.DMA((len(constants),))],
+        compiler_params=pltpu.CompilerParams(vmem_limit_bytes=60 * 1024 * 1024),
         name="spectral",
-    )(places[0], *gathered, places[1], *tables)
+    )(places[0], *gathered, places[1], cube, back, turn, *constants)
 
 
 NOTE_ROWS = 8

time: 231 us -> 206 us (0.89)
  Pallas kernels: 103 us -> 92.1 us
  local copies, waits for them, and re-layouts: 22.4 us -> 14.5 us
  other arithmetic: 21.5 us -> 16.3 us
  waiting for transfers between devices: 55.5 us -> 52.4 us
  starting transfers between devices: 26.1 us -> 29.2 us
    pallas_call x2 -> x3, Pallas kernels: 92.1 us -> 80.7 us  [the longest x2 73 us: spectral(): pl.pallas_call(functools.partial(spectral_kernel, extent, chunk, len(cons...]
    optimization_barrier x4 -> x1, local copies, waits for them, and re-layouts: 6.64 us -> 0.13 us  [gather_pieces(): pieces, beside = lax.optimization_barrier((pieces, beside))]
    transpose x1 -> x0, local copies, waits for them, and re-layouts: 4.4 us -> none  [spectral_tables(): filters = filters.transpose(3, 0, 1, 2).reshape(CUBE_COLS, len(k0), width)]
    ppermute x20, waiting for transfers between devices: 55.5 us -> 52.4 us  [exchange(): return lax.ppermute(value, 'px', [(i, i ^ step) for i in range(members)])]
    ppermute x20, starting transfers between devices: 26.1 us -> 29.2 us  [exchange(): return lax.ppermute(value, 'px', [(i, i ^ step) for i in range(members)])]
    transpose x1 -> x0, other arithmetic: 2.74 us -> none  [spectral_tables(): filters = filters.transpose(3, 0, 1, 2).reshape(CUBE_COLS, len(k0), width)]
    convert_element_type x5 -> x1, other arithmetic: 2.56 us -> 0.01 us  [on_device(): all_cubes.astype(jnp.int32).reshape(members * blocks)]
    unnamed x32 -> x40, local copies, waits for them, and re-layouts: 7.38 us -> 8.81 us
  transfers between devices with their start and end apart: 20 -> 20, of which waited for: 16 -> 18; matrix products, arithmetic and copies ran while one was open for 14% -> 7% of each run, Pallas kernels for 0% -> 4%
where the time goes in v3:
time: 206 us; the launch traced here: 205 us
  Pallas kernels  92.1 us (45%)
  waiting for transfers between devices  52.4 us (25%)
  starting transfers between devices  29.2 us (14%)
  other arithmetic  16.3 us (8%)
  local copies, waits for them, and re-layouts  14.5 us (7%)
    pallas_call x2, Pallas kernels, spectral(): pl.pallas_call(functools.partial(spectral_kernel, extent, chunk, len(cons...  73 us
    ppermute x20, waiting for transfers between devices, exchange(): return lax.ppermute(value, 'px', [(i, i ^ step) for i in range(members)])  52.4 us
    ppermute x20, starting transfers between devices, exchange(): return lax.ppermute(value, 'px', [(i, i ^ step) for i in range(members)])  29.2 us
    pallas_call x3, Pallas kernels, local_call(): pl.pallas_call(kernel, grid=(blocks // STEP_BLOCKS,), out_shape=[jax.Shap...  9.46 us
    unnamed x40, local copies, waits for them, and re-layouts  8.81 us
    pallas_call x1, Pallas kernels, spectral_tables(): pl.pallas_call(functools.partial(tables_kernel, extent, slab), out_shape=...  7.71 us
    reduce_sum x2, other arithmetic, base_of(): jnp.sum(near_tiles * sources[:, None, :], axis=2)  6.68 us
  transfers between devices with their start and end apart: 20, of which 18 were waited for; matrix products, arithmetic and copies ran while one was open for 7% of the time, Pallas kernels for 4%

profile of v3, /device:TPU:0, one launch (start us, length us, event | category | flops | bytes accessed | tf_op | source)
XLA Modules:
  0.0 205.5 jit_solution(2647914764023436144)
XLA Ops:
  0.6 0.8 reshape.198.values_ref.rhs_ref
  2.2 2.2 %copy-done = f32[128,64,128]{2,1,0:T(8,128)S(1)} copy-done((f32[128,64,128]{2,1,0:T(8,128)S(1)}, f32[128,64,128]{2,1,0:T(8,128)}, u32[]{:S(2)}) %copy-start) | copy-done | bytes 4194328
  4.4 1.9 project.1
  6.3 4.1 %collective-permute-start = (f32[1,168,128]{2,0,1:T(1,128)S(1)}, f32[1,168,128]{2,0,1:T(1,128)S(1)}, u32[]{:S(2)}, u32[]{:S(2)}) collective-permute-start(f32[1,168,128]{2,0,1:T(1,128)S(1)} %bitcast.55), channel_id=1, source_target_pairs={{0,8},{1,9},{2,10},{3,11},{4,12},{5,13},{6,14},{7,15},{8,0},{9,1},... | collective-permute-start | bytes 258056 | tf_op jit(solution)/shard_map/ppermute | solution.py:31
  10.4 4.4 %collective-permute-done = f32[1,168,128]{2,0,1:T(1,128)S(1)} collective-permute-done((f32[1,168,128]{2,0,1:T(1,128)S(1)}, f32[1,168,128]{2,0,1:T(1,128)S(1)}, u32[]{:S(2)}, u32[]{:S(2)}) %collective-permute-start) | collective-permute-done | bytes 86048 | tf_op jit(solution)/shard_map/ppermute | solution.py:31
  14.9 0.8 collective-permute-start.1
  15.7 1.3 slice.51
  17.1 3.3 %collective-permute-done.1 = f32[2,168,128]{2,0,1:T(2,128)S(1)} collective-permute-done((f32[2,168,128]{2,0,1:T(2,128)S(1)}, f32[2,168,128]{2,0,1:T(2,128)S(1)}, u32[]{:S(2)}, u32[]{:S(2)}) %collective-permute-start.1) | collective-permute-done | bytes 172064 | tf_op jit(solution)/shard_map/ppermute | solution.py:31
  20.6 1.7 collective-permute-start.2
  22.3 2.2 %copy-done.10 = f32[256,16,256]{2,1,0:T(8,128)S(1)} copy-done((f32[256,16,256]{2,1,0:T(8,128)S(1)}, f32[256,16,256]{2,1,0:T(8,128)}, u32[]{:S(2)}) %copy-start.10) | copy-done | bytes 4194328
  24.5 7.7 %tables.1 = (bf16[384,512]{1,0:T(8,128)(2,1)S(1)}, bf16[1536,128]{1,0:T(8,128)(2,1)S(1)}, bf16[64,256]{1,0:T(8,128)(2,1)S(1)}, f32[16,256,128]{2,1,0:T(8,128)S(1)}) custom-call(s32[2]{0:T(128)S(1)} %pad_add_fusion.place_ref, f32[4096,256]{1,0:T(8,128)S(1)} %bitcast.63, bf16[768,256]{1,0:T(8,128)(2,1)S(1)} %copy-done.12), custom_call_target="tpu_custom_call" | custom-call | flops 1610612736 | bytes 8388608 | tf_op jit(solution)/shard_map/tables/pallas_call | solution.py:420
  32.2 1.4 copy-done.3
  36.4 2.1 %collective-permute-done.3.distant_ref = f32[8,168,128]{2,1,0:T(8,128)S(1)} collective-permute-done((f32[8,168,128]{2,1,0:T(8,128)S(1)}, f32[8,168,128]{2,1,0:T(8,128)S(1)}, u32[]{:S(2)}, u32[]{:S(2)}) %collective-permute-start.3) | collective-permute-done | bytes 688160 | tf_op jit(solution)/shard_map/ppermute | solution.py:31
  39.5 1.3 copy.45.codes_ref
  40.8 36.6 %spectral.2 = (f32[1024,128]{1,0:T(8,128)}, f32[1024,128]{1,0:T(8,128)}) custom-call(s32[2048]{0:T(1024)} %fusion.3.rows_ref, f32[8,168,128]{2,1,0:T(8,128)} %copy-done.14, f32[8,168,128]{2,1,0:T(8,128)} %copy-done.15, s32[2048,8]{1,0:T(8,128)} %copy.45.codes_ref, bf16[384,512]{1,0:T(8,128)(2,1)} %copy-done.5, bf16[1536,128]{1,0:T(8,128)(2,1)} %copy-done.6, ...), custom_call_target="tpu_custom_call" | custom-call | tf_op jit(solution)/shard_map/spectral/pallas_call | solution.py:467
  77.9 1.7 collective-permute-done.4
  79.6 1.1 add.168
  81.3 0.9 select_bitcast_fusion.3
  83.0 6.2 %collective-permute-done.5 = f32[512,128]{1,0:T(8,128)S(1)} collective-permute-done((f32[512,128]{1,0:T(8,128)S(1)}, f32[512,128]{1,0:T(8,128)S(1)}, u32[]{:S(2)}, u32[]{:S(2)}) %collective-permute-start.5) | collective-permute-done | bytes 262176 | tf_op jit(solution)/shard_map/ppermute | solution.py:31
  89.2 1.4 collective-permute-start.6
  90.7 3.3 %multiply_reduce_fusion.1 = f32[128,64]{1,0:T(8,128)S(1)} fusion(f32[128,64,128]{2,1,0:T(8,128)} %param.27, f32[128,128]{1,0:T(8,128)S(1)} %mul.61), kind=kLoop, calls=%fused_computation.3 | loop fusion | flops 2088960 | bytes 4292608 | tf_op jit(solution)/shard_map/reduce_sum | solution.py:654
  94.3 3.2 %collective-permute-start.7 = (f32[128,128]{1,0:T(8,128)S(1)}, f32[128,128]{1,0:T(8,128)S(1)}, u32[]{:S(2)}, u32[]{:S(2)}) collective-permute-start(f32[128,128]{1,0:T(8,128)S(1)} %slice.78), channel_id=1, source_target_pairs={{0,8},{1,9},{2,10},{3,11},{4,12},{5,13},{6,14},{7,15},{8,0},{9,1},... | collective-permute-start | bytes 196616 | tf_op jit(solution)/shard_map/ppermute | solution.py:31
  97.5 2.2 %collective-permute-done.7 = f32[128,128]{1,0:T(8,128)S(1)} collective-permute-done((f32[128,128]{1,0:T(8,128)S(1)}, f32[128,128]{1,0:T(8,128)S(1)}, u32[]{:S(2)}, u32[]{:S(2)}) %collective-permute-start.7) | collective-permute-done | bytes 65568 | tf_op jit(solution)/shard_map/ppermute | solution.py:31
  99.8 4.1 %complete.1 = (f32[128,64]{1,0:T(8,128)S(1)}, f32[168,128]{1,0:T(8,128)S(1)}) custom-call(f32[128,64,128]{2,1,0:T(8,128)S(1)} %copy-done.1, f32[128,128]{1,0:T(8,128)S(1)} %slice_add_fusion.5.picked_ref, f32[128,64]{1,0:T(8,128)S(1)} %multiply_add_fusion.1.base_ref, f32[128,64]{1,0:T(8,128)S(1)} %reshape.198.values_ref.rhs_ref), custom_call_target="tpu_custom_call" | custom-call | flops 4194304 | bytes 4194304 | tf_op jit(solution)/shard_map/complete/pallas_call | solution.py:603
  104.0 3.0 %collective-permute-start.8 = (f32[1,168,128]{2,1,0:T(8,128)S(1)}, f32[1,168,128]{2,1,0:T(8,128)S(1)}, u32[]{:S(2)}, u32[]{:S(2)}) collective-permute-start(f32[1,168,128]{2,1,0:T(8,128)S(1)} %bitcast.59), channel_id=1, source_target_pairs={{0,8},{1,9},{2,10},{3,11},{4,12},{5,13},{6,14},{7,15},{8,0},{9,1},... | collective-permute-start | bytes 258056 | tf_op jit(solution)/shard_map/ppermute | solution.py:31
  107.0 2.9 %collective-permute-done.8 = f32[1,168,128]{2,1,0:T(8,128)S(1)} collective-permute-done((f32[1,168,128]{2,1,0:T(8,128)S(1)}, f32[1,168,128]{2,1,0:T(8,128)S(1)}, u32[]{:S(2)}, u32[]{:S(2)}) %collective-permute-start.8) | collective-permute-done | bytes 86048 | tf_op jit(solution)/shard_map/ppermute | solution.py:31
  109.9 1.9 collective-permute-start.9
  111.8 3.6 %collective-permute-done.9 = f32[2,168,128]{2,1,0:T(8,128)S(1)} collective-permute-done((f32[2,168,128]{2,1,0:T(8,128)S(1)}, f32[2,168,128]{2,1,0:T(8,128)S(1)}, u32[]{:S(2)}, u32[]{:S(2)}) %collective-permute-start.9) | collective-permute-done | bytes 172064 | tf_op jit(solution)/shard_map/ppermute | solution.py:31
  116.0 6.7 %collective-permute-done.10 = f32[4,168,128]{2,1,0:T(8,128)S(1)} collective-permute-done((f32[4,168,128]{2,1,0:T(8,128)S(1)}, f32[4,168,128]{2,1,0:T(8,128)S(1)}, u32[]{:S(2)}, u32[]{:S(2)}) %collective-permute-start.10) | collective-permute-done | bytes 344096 | tf_op jit(solution)/shard_map/ppermute | solution.py:31
  122.9 2.1 %collective-permute-done.11.distant_ref = f32[8,168,128]{2,1,0:T(8,128)S(1)} collective-permute-done((f32[8,168,128]{2,1,0:T(8,128)S(1)}, f32[8,168,128]{2,1,0:T(8,128)S(1)}, u32[]{:S(2)}, u32[]{:S(2)}) %collective-permute-start.11) | collective-permute-done | bytes 688160 | tf_op jit(solution)/shard_map/ppermute | solution.py:31
  125.0 0.9 copy-done.16
  125.9 36.4 %spectral.3 = (f32[1024,128]{1,0:T(8,128)}, f32[1024,128]{1,0:T(8,128)}) custom-call(s32[2048]{0:T(1024)} %fusion.3.rows_ref, f32[8,168,128]{2,1,0:T(8,128)} %copy-done.13, f32[8,168,128]{2,1,0:T(8,128)} %copy-done.16, s32[2048,8]{1,0:T(8,128)} %copy.45.codes_ref, bf16[384,512]{1,0:T(8,128)(2,1)} %copy-done.5, bf16[1536,128]{1,0:T(8,128)(2,1)} %copy-done.6, ...), custom_call_target="tpu_custom_call" | custom-call | tf_op jit(solution)/shard_map/spectral/pallas_call | solution.py:467
  163.3 0.9 select_bitcast_fusion.1
  165.0 1.3 add.187
  166.9 3.3 %multiply_reduce_fusion = f32[128,64]{1,0:T(8,128)S(1)} fusion(f32[128,64,128]{2,1,0:T(8,128)} %param.27, f32[128,128]{1,0:T(8,128)S(1)} %mul.65), kind=kLoop, calls=%fused_computation.2 | loop fusion | flops 2088960 | bytes 4292608 | tf_op jit(solution)/shard_map/reduce_sum | solution.py:654
  170.2 4.7 %collective-permute-done.13 = f32[512,128]{1,0:T(8,128)S(1)} collective-permute-done((f32[512,128]{1,0:T(8,128)S(1)}, f32[512,128]{1,0:T(8,128)S(1)}, u32[]{:S(2)}, u32[]{:S(2)}) %collective-permute-start.13) | collective-permute-done | bytes 262176 | tf_op jit(solution)/shard_map/ppermute | solution.py:31
  174.9 1.9 collective-permute-start.14
  177.6 2.4 %collective-permute-done.14 = f32[256,128]{1,0:T(8,128)S(1)} collective-permute-done((f32[256,128]{1,0:T(8,128)S(1)}, f32[256,128]{1,0:T(8,128)S(1)}, u32[]{:S(2)}, u32[]{:S(2)}) %collective-permute-start.14) | collective-permute-done | bytes 131104 | tf_op jit(solution)/shard_map/ppermute | solution.py:31
  180.1 3.5 %collective-permute-start.15 = (f32[128,128]{1,0:T(8,128)S(1)}, f32[128,128]{1,0:T(8,128)S(1)}, u32[]{:S(2)}, u32[]{:S(2)}) collective-permute-start(f32[128,128]{1,0:T(8,128)S(1)} %slice.84), channel_id=1, source_target_pairs={{0,8},{1,9},{2,10},{3,11},{4,12},{5,13},{6,14},{7,15},{8,0},{9,1},... | collective-permute-start | bytes 196616 | tf_op jit(solution)/shard_map/ppermute | solution.py:31
  183.6 2.2 %collective-permute-done.15 = f32[128,128]{1,0:T(8,128)S(1)} collective-permute-done((f32[128,128]{1,0:T(8,128)S(1)}, f32[128,128]{1,0:T(8,128)S(1)}, u32[]{:S(2)}, u32[]{:S(2)}) %collective-permute-start.15) | collective-permute-done | bytes 65568 | tf_op jit(solution)/shard_map/ppermute | solution.py:31
  185.9 3.4 %close.1 = (f32[128,64]{1,0:T(8,128)S(1)}, f32[8,128]{1,0:T(8,128)S(1)}) custom-call(f32[128,64,128]{2,1,0:T(8,128)S(1)} %copy-done.2, f32[128,128]{1,0:T(8,128)S(1)} %slice_add_fusion.4.picked_ref, f32[128,64]{1,0:T(8,128)S(1)} %multiply_add_fusion.base_ref, f32[128,64]{1,0:T(8,128)S(1)} %reshape.198.values_ref.rhs_ref, ...), custom_call_target="tpu_custom_call" | custom-call | flops 4194304 | bytes 4194304 | tf_op jit(solution)/shard_map/close/pallas_call | solution.py:603
  189.9 1.2 collective-permute-done.16
  191.8 2.9 %collective-permute-done.17 = f32[8,128]{1,0:T(8,128)S(1)} collective-permute-done((f32[8,128]{1,0:T(8,128)S(1)}, f32[8,128]{1,0:T(8,128)S(1)}, u32[]{:S(2)}, u32[]{:S(2)}) %collective-permute-start.17) | collective-permute-done | bytes 4128 | tf_op jit(solution)/shard_map/ppermute | solution.py:31
  194.7 1.7 collective-permute-start.18
  196.4 1.9 collective-permute-done.18
  198.3 3.1 %collective-permute-start.19 = (f32[8,128]{1,0:T(8,128)S(1)}, f32[8,128]{1,0:T(8,128)S(1)}, u32[]{:S(2)}, u32[]{:S(2)}) collective-permute-start(f32[8,128]{1,0:T(8,128)S(1)} %add.196), channel_id=1, source_target_pairs={{0,8},{1,9},{2,10},{3,11},{4,12},{5,13},{6,14},{7,15},{8,0},{9,1},... | collective-permute-start | bytes 12296 | tf_op jit(solution)/shard_map/ppermute | solution.py:31
  201.4 1.6 collective-permute-done.19
  203.6 1.9 finish.1
  (99 shorter events, 13.0 us)
Async XLA Ops:
  1.5 184.4 %copy-start.4 = (f32[128,64]{1,0:T(8,128)}, f32[128,64]{1,0:T(8,128)S(1)}, u32[]{:S(2)}) copy-start(f32[128,64]{1,0:T(8,128)S(1)} %reshape.198.values_ref.rhs_ref) | copy-start | bytes 98308
  2.2 2.2 %copy-start = (f32[128,64,128]{2,1,0:T(8,128)S(1)}, f32[128,64,128]{2,1,0:T(8,128)}, u32[]{:S(2)}) copy-start(f32[128,64,128]{2,1,0:T(8,128)} %proj_ref.5) | copy-start | bytes 12582916
  4.4 18.0 %copy-start.12 = (bf16[768,256]{1,0:T(8,128)(2,1)S(1)}, bf16[768,256]{1,0:T(8,128)(2,1)}, u32[]{:S(2)}) copy-start(bf16[768,256]{1,0:T(8,128)(2,1)} %constant.208.clone.sort_ref) | copy-start | bytes 1179652
  6.3 28.8 %copy-start.18 = (f32[136]{0:T(256)S(1)}, f32[136]{0:T(256)}, u32[]{:S(2)}) copy-start(f32[136]{0:T(256)} %constant.220.clone) | copy-start | bytes 1636
  6.3 8.4 %collective-permute-start = (f32[1,168,128]{2,0,1:T(1,128)S(1)}, f32[1,168,128]{2,0,1:T(1,128)S(1)}, u32[]{:S(2)}, u32[]{:S(2)}) collective-permute-start(f32[1,168,128]{2,0,1:T(1,128)S(1)} %bitcast.55), channel_id=1, source_target_pairs={{0,8},{1,9},{2,10},{3,11},{4,12},{5,13},{6,14},{7,15},{8,0},{9,1},... | collective-permute-start | bytes 258056 | tf_op jit(solution)/shard_map/ppermute | solution.py:31
  14.9 5.5 %collective-permute-start.1 = (f32[2,168,128]{2,0,1:T(2,128)S(1)}, f32[2,168,128]{2,0,1:T(2,128)S(1)}, u32[]{:S(2)}, u32[]{:S(2)}) collective-permute-start(f32[2,168,128]{2,0,1:T(2,128)S(1)} %pad_maximum_fusion.4), channel_id=1, source_target_pairs={{0,4},{1,5},{2,6},{3,7},{4,0},{5,1},{6,2},{7,3},{8,12},{9,13},{10,... | collective-permute-start | bytes 516104 | tf_op jit(solution)/shard_map/ppermute | solution.py:31
  20.6 15.2 %collective-permute-start.2 = (f32[4,168,128]{2,0,1:T(4,128)S(1)}, f32[4,168,128]{2,0,1:T(4,128)S(1)}, u32[]{:S(2)}, u32[]{:S(2)}) collective-permute-start(f32[4,168,128]{2,0,1:T(4,128)S(1)} %pad_maximum_fusion.2), channel_id=1, source_target_pairs={{0,2},{1,3},{2,0},{3,1},{4,6},{5,7},{6,4},{7,5},{8,10},{9,11},{10,... | collective-permute-start | bytes 1032200 | tf_op jit(solution)/shard_map/ppermute | solution.py:31
  22.3 2.2 %copy-start.10 = (f32[256,16,256]{2,1,0:T(8,128)S(1)}, f32[256,16,256]{2,1,0:T(8,128)}, u32[]{:S(2)}) copy-start(f32[256,16,256]{2,1,0:T(8,128)} %param.28) | copy-start | bytes 12582916
  32.2 1.4 copy-start.3
  33.6 0.8 copy-start.5
  34.4 0.8 copy-start.6
  35.1 1.1 copy-start.8
  36.3 4.5 %copy-start.14 = (f32[8,168,128]{2,1,0:T(8,128)}, f32[8,168,128]{2,1,0:T(8,128)S(1)}, u32[]{:S(2)}) copy-start(f32[8,168,128]{2,1,0:T(8,128)S(1)} %copy.43.near_ref) | copy-start | bytes 2064388
  36.4 2.2 %collective-permute-start.3 = (f32[8,168,128]{2,1,0:T(8,128)S(1)}, f32[8,168,128]{2,1,0:T(8,128)S(1)}, u32[]{:S(2)}, u32[]{:S(2)}) collective-permute-start(f32[8,168,128]{2,1,0:T(8,128)S(1)} %copy.43.near_ref), channel_id=1, source_target_pairs={{0,1},{1,0},{2,3},{3,2},{4,5},{5,4},{6,7},{7,6},{8,9},{9,8},{10,11... | collective-permute-start | bytes 2064392 | tf_op jit(solution)/shard_map/ppermute | solution.py:31
  38.6 2.3 %copy-start.15 = (f32[8,168,128]{2,1,0:T(8,128)}, f32[8,168,128]{2,1,0:T(8,128)S(1)}, u32[]{:S(2)}) copy-start(f32[8,168,128]{2,1,0:T(8,128)S(1)} %collective-permute-done.3.distant_ref) | copy-start | bytes 2064388
  40.8 36.8 %copy-start.19 = (s32[128,2]{0,1:T(2,128)S(1)}, s32[128,2]{0,1:T(2,128)}, u32[]{:S(2)}) copy-start(s32[128,2]{0,1:T(2,128)} %param.26) | copy-start | bytes 3076
  40.8 40.4 %copy-start.17 = (f32[8192]{0:T(1024)S(1)}, f32[8192]{0:T(1024)}, u32[]{:S(2)}) copy-start(f32[8192]{0:T(1024)} %param.22) | copy-start | bytes 98308
  77.4 2.2 %collective-permute-start.4 = (f32[1024,128]{1,0:T(8,128)}, f32[1024,128]{1,0:T(8,128)S(1)}, u32[]{:S(2)}, u32[]{:S(2)}) collective-permute-start(f32[1024,128]{1,0:T(8,128)} %get-tuple-element.55), channel_id=1, source_target_pairs={{0,1},{1,0},{2,3},{3,2},{4,5},{5,4},{6,7},{7,6},{8,9},{9,8},{10,11... | collective-permute-start | bytes 1572872 | tf_op jit(solution)/shard_map/ppermute | solution.py:31
  80.8 8.4 %collective-permute-start.5 = (f32[512,128]{1,0:T(8,128)S(1)}, f32[512,128]{1,0:T(8,128)S(1)}, u32[]{:S(2)}, u32[]{:S(2)}) collective-permute-start(f32[512,128]{1,0:T(8,128)S(1)} %slice.74), channel_id=1, source_target_pairs={{0,2},{1,3},{2,0},{3,1},{4,6},{5,7},{6,4},{7,5},{8,10},{9,11},{10,... | collective-permute-start | bytes 786440 | tf_op jit(solution)/shard_map/ppermute | solution.py:31
  83.0 16.8 %copy-start.1 = (f32[128,64,128]{2,1,0:T(8,128)S(1)}, f32[128,64,128]{2,1,0:T(8,128)}, u32[]{:S(2)}) copy-start(f32[128,64,128]{2,1,0:T(8,128)} %proj_ref.5) | copy-start | bytes 12582916
  89.2 5.0 %collective-permute-start.6 = (f32[256,128]{1,0:T(8,128)S(1)}, f32[256,128]{1,0:T(8,128)S(1)}, u32[]{:S(2)}, u32[]{:S(2)}) collective-permute-start(f32[256,128]{1,0:T(8,128)S(1)} %slice.76), channel_id=1, source_target_pairs={{0,4},{1,5},{2,6},{3,7},{4,0},{5,1},{6,2},{7,3},{8,12},{9,13},{10,... | collective-permute-start | bytes 393224 | tf_op jit(solution)/shard_map/ppermute | solution.py:31
  94.3 5.5 %collective-permute-start.7 = (f32[128,128]{1,0:T(8,128)S(1)}, f32[128,128]{1,0:T(8,128)S(1)}, u32[]{:S(2)}, u32[]{:S(2)}) collective-permute-start(f32[128,128]{1,0:T(8,128)S(1)} %slice.78), channel_id=1, source_target_pairs={{0,8},{1,9},{2,10},{3,11},{4,12},{5,13},{6,14},{7,15},{8,0},{9,1},... | collective-permute-start | bytes 196616 | tf_op jit(solution)/shard_map/ppermute | solution.py:31
  103.9 81.9 %copy-start.7 = (f32[128,64]{1,0:T(8,128)}, f32[128,64]{1,0:T(8,128)S(1)}, u32[]{:S(2)}) copy-start(f32[128,64]{1,0:T(8,128)S(1)} %get-tuple-element.56.first_ref) | copy-start | bytes 98308
  104.0 5.9 %collective-permute-start.8 = (f32[1,168,128]{2,1,0:T(8,128)S(1)}, f32[1,168,128]{2,1,0:T(8,128)S(1)}, u32[]{:S(2)}, u32[]{:S(2)}) collective-permute-start(f32[1,168,128]{2,1,0:T(8,128)S(1)} %bitcast.59), channel_id=1, source_target_pairs={{0,8},{1,9},{2,10},{3,11},{4,12},{5,13},{6,14},{7,15},{8,0},{9,1},... | collective-permute-start | bytes 258056 | tf_op jit(solution)/shard_map/ppermute | solution.py:31
  109.9 5.5 %collective-permute-start.9 = (f32[2,168,128]{2,1,0:T(8,128)S(1)}, f32[2,168,128]{2,1,0:T(8,128)S(1)}, u32[]{:S(2)}, u32[]{:S(2)}) collective-permute-start(f32[2,168,128]{2,1,0:T(8,128)S(1)} %pad_maximum_fusion.5), channel_id=1, source_target_pairs={{0,4},{1,5},{2,6},{3,7},{4,0},{5,1},{6,2},{7,3},{8,12},{9,13},{10,... | collective-permute-start | bytes 516104 | tf_op jit(solution)/shard_map/ppermute | solution.py:31
  115.4 7.3 %collective-permute-start.10 = (f32[4,168,128]{2,1,0:T(8,128)S(1)}, f32[4,168,128]{2,1,0:T(8,128)S(1)}, u32[]{:S(2)}, u32[]{:S(2)}) collective-permute-start(f32[4,168,128]{2,1,0:T(8,128)S(1)} %pad_maximum_fusion.3), channel_id=1, source_target_pairs={{0,2},{1,3},{2,0},{3,1},{4,6},{5,7},{6,4},{7,5},{8,10},{9,11},{10,... | collective-permute-start | bytes 1032200 | tf_op jit(solution)/shard_map/ppermute | solution.py:31
  122.8 2.2 %copy-start.13 = (f32[8,168,128]{2,1,0:T(8,128)}, f32[8,168,128]{2,1,0:T(8,128)S(1)}, u32[]{:S(2)}) copy-start(f32[8,168,128]{2,1,0:T(8,128)S(1)} %pad_maximum_fusion.1.near_ref) | copy-start | bytes 2064388
  122.8 2.2 %collective-permute-start.11 = (f32[8,168,128]{2,1,0:T(8,128)S(1)}, f32[8,168,128]{2,1,0:T(8,128)S(1)}, u32[]{:S(2)}, u32[]{:S(2)}) collective-permute-start(f32[8,168,128]{2,1,0:T(8,128)S(1)} %pad_maximum_fusion.1.near_ref), channel_id=1, source_target_pairs={{0,1},{1,0},{2,3},{3,2},{4,5},{5,4},{6,7},{7,6},{8,9},{9,8},{10,11... | collective-permute-start | bytes 2064392 | tf_op jit(solution)/shard_map/ppermute | solution.py:31
  125.0 0.9 copy-start.16
  162.3 2.7 %collective-permute-start.12 = (f32[1024,128]{1,0:T(8,128)}, f32[1024,128]{1,0:T(8,128)S(1)}, u32[]{:S(2)}, u32[]{:S(2)}) collective-permute-start(f32[1024,128]{1,0:T(8,128)} %get-tuple-element.59), channel_id=1, source_target_pairs={{0,1},{1,0},{2,3},{3,2},{4,5},{5,4},{6,7},{7,6},{8,9},{9,8},{10,11... | collective-permute-start | bytes 1572872 | tf_op jit(solution)/shard_map/ppermute | solution.py:31
  165.0 20.9 %copy-start.2 = (f32[128,64,128]{2,1,0:T(8,128)S(1)}, f32[128,64,128]{2,1,0:T(8,128)}, u32[]{:S(2)}) copy-start(f32[128,64,128]{2,1,0:T(8,128)} %proj_ref.5) | copy-start | bytes 12582916
  166.3 8.6 %collective-permute-start.13 = (f32[512,128]{1,0:T(8,128)S(1)}, f32[512,128]{1,0:T(8,128)S(1)}, u32[]{:S(2)}, u32[]{:S(2)}) collective-permute-start(f32[512,128]{1,0:T(8,128)S(1)} %slice.80), channel_id=1, source_target_pairs={{0,2},{1,3},{2,0},{3,1},{4,6},{5,7},{6,4},{7,5},{8,10},{9,11},{10,... | collective-permute-start | bytes 786440 | tf_op jit(solution)/shard_map/ppermute | solution.py:31
  174.9 5.1 %collective-permute-start.14 = (f32[256,128]{1,0:T(8,128)S(1)}, f32[256,128]{1,0:T(8,128)S(1)}, u32[]{:S(2)}, u32[]{:S(2)}) collective-permute-start(f32[256,128]{1,0:T(8,128)S(1)} %slice.82), channel_id=1, source_target_pairs={{0,4},{1,5},{2,6},{3,7},{4,0},{5,1},{6,2},{7,3},{8,12},{9,13},{10,... | collective-permute-start | bytes 393224 | tf_op jit(solution)/shard_map/ppermute | solution.py:31
  180.1 5.8 %collective-permute-start.15 = (f32[128,128]{1,0:T(8,128)S(1)}, f32[128,128]{1,0:T(8,128)S(1)}, u32[]{:S(2)}, u32[]{:S(2)}) collective-permute-start(f32[128,128]{1,0:T(8,128)S(1)} %slice.84), channel_id=1, source_target_pairs={{0,8},{1,9},{2,10},{3,11},{4,12},{5,13},{6,14},{7,15},{8,0},{9,1},... | collective-permute-start | bytes 196616 | tf_op jit(solution)/shard_map/ppermute | solution.py:31
  183.6 19.9 %copy-start.11 = (f32[1,128]{1,0:T(1,128)}, f32[1,128]{1,0:T(1,128)S(1)}, u32[]{:S(2)}) copy-start(f32[1,128]{1,0:T(1,128)S(1)} %add_bitcast_fusion.sums_ref) | copy-start | bytes 1540
  189.3 0.6 copy-start.9
  189.9 1.2 collective-permute-start.16
  191.1 3.6 %collective-permute-start.17 = (f32[8,128]{1,0:T(8,128)S(1)}, f32[8,128]{1,0:T(8,128)S(1)}, u32[]{:S(2)}, u32[]{:S(2)}) collective-permute-start(f32[8,128]{1,0:T(8,128)S(1)} %add.194), channel_id=1, source_target_pairs={{0,2},{1,3},{2,0},{3,1},{4,6},{5,7},{6,4},{7,5},{8,10},{9,11},{10,... | collective-permute-start | bytes 12296 | tf_op jit(solution)/shard_map/ppermute | solution.py:31
  194.7 3.6 %collective-permute-start.18 = (f32[8,128]{1,0:T(8,128)S(1)}, f32[8,128]{1,0:T(8,128)S(1)}, u32[]{:S(2)}, u32[]{:S(2)}) collective-permute-start(f32[8,128]{1,0:T(8,128)S(1)} %add.195), channel_id=1, source_target_pairs={{0,4},{1,5},{2,6},{3,7},{4,0},{5,1},{6,2},{7,3},{8,12},{9,13},{10,... | collective-permute-start | bytes 12296 | tf_op jit(solution)/shard_map/ppermute | solution.py:31
  198.3 4.6 %collective-permute-start.19 = (f32[8,128]{1,0:T(8,128)S(1)}, f32[8,128]{1,0:T(8,128)S(1)}, u32[]{:S(2)}, u32[]{:S(2)}) collective-permute-start(f32[8,128]{1,0:T(8,128)S(1)} %add.196), channel_id=1, source_target_pairs={{0,8},{1,9},{2,10},{3,11},{4,12},{5,13},{6,14},{7,15},{8,0},{9,1},... | collective-permute-start | bytes 12296 | tf_op jit(solution)/shard_map/ppermute | solution.py:31

commit v4 on v3

--- a/solution.py
+++ b/solution.py
@@ -10,6 +10,8 @@
 LANES = 128
 CUBE_ROWS = 8
 CUBE_COLS = 16
+VMEM_BYTES = 60 * 1024 * 1024
+SPECTRAL_BYTES = 60 * 1024 * 1024
 
 
 def split(value):
@@ -34,10 +36,13 @@
 def gather_pieces(piece, beside):
     steps = partner_steps(lax.axis_size("px"))
     pieces = piece[None]
-    for step in steps[:-1]:
+    done = []
+    for index, step in enumerate(steps[:-1]):
         pieces = jnp.concatenate([pieces, exchange(pieces, step)], axis=0)
-    pieces, beside = lax.optimization_barrier((pieces, beside))
-    return (pieces, exchange(pieces, steps[-1])), beside
+        if index < len(beside):
+            pieces, value = lax.optimization_barrier((pieces, beside[index]))
+            done.append(value)
+    return (pieces, exchange(pieces, steps[-1])), done
 
 
 def scatter_pieces(kept, sent):
@@ -50,9 +55,9 @@
 
 
 def total(value):
-    for step in reversed(partner_steps(lax.axis_size("px"))):
-        value = value + exchange(value, step)
-    return value
+    members = lax.axis_size("px")
+    copies = jnp.broadcast_to(value[None], (members, *value.shape))
+    return jnp.sum(lax.all_to_all(copies, "px", 0, 0), axis=0)
 
 
 def butterfly16(real, imag, sign):
@@ -98,21 +103,20 @@
     return jnp.where(left == right, 1.0, 0.0).astype(jnp.bfloat16)
 
 
-COPIES = 2
-
-
-def spectral_kernel(extent, chunk, constants, rows_ref, near_ref, distant_ref, codes_ref, *refs):
-    cube_ref, back_ref, turn_ref = refs[:3]
-    sources = refs[3 : 3 + constants]
-    kept_ref, sent_ref = refs[3 + constants : 5 + constants]
-    refs = refs[5 + constants :]
-    tables, refs = refs[:constants], refs[constants:]
+COPIES = 4
+GROUP = 8
+
+
+def spectral_kernel(extent, chunk, operands, rows_ref, codes_ref, *refs):
+    sources, (kept_out, sent_out), refs = refs[:operands], refs[operands : operands + 2], refs[operands + 2 :]
+    tables, (kept_ref, sent_ref), refs = refs[:operands], refs[operands : operands + 2], refs[operands + 2 :]
     grids, refs = refs[: 2 * COPIES], refs[2 * COPIES :]
     grids = [grids[2 * i : 2 * i + 2] for i in range(COPIES)]
-    rows, dense, sem = refs[:2], refs[2], refs[3]
-    even_ref, odd_ref, uneven_ref, unodd_ref = tables[:4]
-    line_ref, unline_ref, twist_ref, filter_ref = tables[4:8]
-    plane_ref, unplane_ref, full_ref, unfull_ref, edge_ref = tables[8:]
+    rows, dense, sem, out_sem = refs[:2], refs[2], refs[3], refs[4]
+    near_ref, cube_ref, turn_ref, distant_ref, back_ref = tables[:5]
+    even_ref, odd_ref, uneven_ref, unodd_ref = tables[5:9]
+    line_ref, unline_ref, twist_ref, filter_ref = tables[9:13]
+    plane_ref, unplane_ref, full_ref, unfull_ref, edge_ref = tables[13:]
     half_count = kept_ref.shape[0]
     blocks = half_count // near_ref.shape[0]
     slabs = extent // CUBE_COLS
@@ -121,7 +125,7 @@
         pltpu.make_async_copy(source, table, sem.at[i])
         for i, (source, table) in enumerate(zip(sources, tables))
     ]
-    for move in moves:
+    for move in moves[:3]:
         move.start()
 
     def clear(i, _):
@@ -135,7 +139,7 @@
     dense[...] = jnp.zeros(dense.shape, jnp.float32)
 
     def marks(start):
-        codes = codes_ref[pl.ds(start, chunk), :]
+        codes = jnp.transpose(codes_ref[:, pl.ds(start, chunk)])
         turn_count = extent // CUBE_ROWS
         wide = lax.broadcasted_iota(jnp.int32, (chunk, extent), 1)
         turn_lane = lax.broadcasted_iota(jnp.int32, (chunk, 2 * turn_count), 1) % turn_count
@@ -168,7 +172,13 @@
         lax.fori_loop(0, chunk // COPIES, add, 0, unroll=8)
         return 0
 
+    for move in moves[:3]:
+        move.wait()
+    for move in moves[3:]:
+        move.start()
     for index, source_ref in enumerate((near_ref, distant_ref)):
+        if index:
+            moves[3].wait()
         body = functools.partial(spread, source_ref, index * half_count)
         lax.fori_loop(0, half_count // chunk, body, 0)
 
@@ -193,11 +203,12 @@
         lax.fori_loop(0, extent // 8, body, 0)
 
     across(-1)
-    for move in moves:
+    for move in moves[4:]:
         move.wait()
 
-    def middle(pair, _):
-        starts = [pl.multiple_of((2 * pair + i) * extent, extent) for i in range(2)]
+    def middle(group, _):
+        starts = [pl.multiple_of((GROUP * group + i) * extent, extent) for i in range(GROUP)]
+        cuts = [slice(i * LANES, (i + 1) * LANES) for i in range(GROUP)]
 
         def joined(offset):
             return jnp.concatenate(
@@ -213,21 +224,22 @@
         odd = dot_in(odd_ref[...], right_terms(first - last))
         real = jnp.concatenate([even[:half], odd[:half]], axis=0)
         imag = jnp.concatenate([even[half:], odd[half:]], axis=0)
-        cosine, sine = twist_ref[pair, 0:1, :], twist_ref[pair, 1:2, :]
+        cosine, sine = twist_ref[group, 0:1, :], twist_ref[group, 1:2, :]
         real, imag = real * cosine + imag * sine, imag * cosine - real * sine
         lines = jnp.concatenate(
             [
                 jnp.concatenate([real[:, cut], imag[:, cut]], axis=1)
-                for cut in (slice(0, LANES), slice(LANES, 2 * LANES))
+                for cut in cuts
             ],
             axis=0,
         )
         lines = dot_in(left_terms(lines), line_ref[...])
-        scale = jnp.concatenate([filter_ref[2 * pair], filter_ref[2 * pair + 1]], axis=0)
+        scale = jnp.concatenate([filter_ref[GROUP * group + i] for i in range(GROUP)], axis=0)
         lines = lines * jnp.concatenate([scale, scale], axis=1)
         lines = dot_in(left_terms(lines), unline_ref[...])
-        real = jnp.concatenate([lines[:extent, :LANES], lines[extent:, :LANES]], axis=1)
-        imag = jnp.concatenate([lines[:extent, LANES:], lines[extent:, LANES:]], axis=1)
+        lines = [lines[i * extent : (i + 1) * extent] for i in range(GROUP)]
+        real = jnp.concatenate([line[:, :LANES] for line in lines], axis=1)
+        imag = jnp.concatenate([line[:, LANES:] for line in lines], axis=1)
         real, imag = real * cosine - imag * sine, imag * cosine + real * sine
         even = jnp.concatenate([real[:half], imag[:half]], axis=0)
         odd = jnp.concatenate([real[half:], imag[half:]], axis=0)
@@ -241,7 +253,7 @@
                     ]
         return 0
 
-    lax.fori_loop(0, slabs // 2, middle, 0, unroll=2)
+    lax.fori_loop(0, slabs // GROUP, middle, 0, unroll=1)
     planes = dot_in(plane_ref[...], right_terms(dense[...]))
     some = planes.shape[0] // 2
     planes = jnp.concatenate([planes[:some], planes[some:]], axis=1)
@@ -252,7 +264,16 @@
     dense[...] = dot_in(unplane_ref[...], right_terms(planes))
     across(1)
 
-    def collect(out_ref, offset, step, _):
+    def leave(index, step):
+        place = pl.ds(pl.multiple_of(step * chunk, chunk), chunk)
+        out_ref = (kept_ref, sent_ref)[index]
+        return pltpu.make_async_copy(
+            out_ref.at[place, :], (kept_out, sent_out)[index].at[place, :], out_sem.at[index, step]
+        )
+
+    def collect(index, step, _):
+        out_ref = (kept_ref, sent_ref)[index]
+        offset = index * half_count
         start = pl.multiple_of(offset + step * chunk, chunk)
 
         def take(i, _):
@@ -274,11 +295,18 @@
         out_ref[pl.ds(pl.multiple_of(step * chunk, chunk), chunk), :] = dot_in(
             left_terms(both), back_ref[...]
         )
+        leave(index, step).start()
         return 0
 
-    for index, out_ref in enumerate((kept_ref, sent_ref)):
-        body = functools.partial(collect, out_ref, index * half_count)
-        lax.fori_loop(0, half_count // chunk, body, 0)
+    for index in range(2):
+        lax.fori_loop(0, half_count // chunk, functools.partial(collect, index), 0)
+
+    def finish(step, _):
+        for index in range(2):
+            leave(index, step).wait()
+        return 0
+
+    lax.fori_loop(0, half_count // chunk, finish, 0)
 
 
 def stacked_table(table, axis):
@@ -304,7 +332,7 @@
     line = np.block([[cosine, -sine], [sine, cosine]])
     angle = 2.0 * np.pi / extent * (small[:, None] * (np.arange(LANES) % CUBE_COLS)[None, :])
     twist = np.stack([np.cos(angle), np.sin(angle)], axis=1)
-    twist = np.concatenate([twist[0::2], twist[1::2]], axis=2)
+    twist = np.concatenate([twist[i::GROUP] for i in range(GROUP)], axis=2)
     some = np.arange(-(-(half + 1) // 8) * 8)
     whole = np.arange(extent)
     angle = 2.0 * np.pi / extent * (some[:, None] * whole[None, :] % extent)
@@ -319,11 +347,8 @@
     return first, last
 
 
-def tables_kernel(
-    extent, slab, place_ref, kernel_ref, sort_ref, cube_ref, back_ref, turn_ref, filter_ref, *lines
-):
-    first, shift = place_ref[0], place_ref[1]
-    held = slab // 2
+def tables_kernel(extent, held, place_ref, cube_ref, back_ref, turn_ref):
+    first = place_ref[0]
     points = CUBE_ROWS * CUBE_COLS
 
     def angles(numerator):
@@ -351,59 +376,48 @@
     high, low = split(jnp.concatenate(angles(turn * (first + column // CUBE_COLS)), axis=1))
     turn_ref[...] = jnp.concatenate([high, low], axis=0)
 
-    batch = 512
-
-    def sort(i, _):
-        place = pl.ds(pl.multiple_of(i * batch, batch), batch)
-        values = kernel_ref[place, :]
-        high = values.astype(jnp.bfloat16)
-        rest = values - high.astype(jnp.float32)
-        middle, low = split(rest)
-        terms = jnp.concatenate([high, middle, low], axis=1)
-        values = dot_in(terms, sort_ref[...])
-        for side, ref in enumerate(lines):
-            ref[place, :] = values[:, side * LANES : (side + 1) * LANES]
-        return 0
-
-    lax.fori_loop(0, extent * slab // batch, sort, 0)
+
+def filter_kernel(extent, slab, place_ref, kernel_ref, sort_ref, filter_ref, *lines):
+    first, shift = place_ref[0], place_ref[1]
+    held = slab // 2
+    batch = kernel_ref.shape[0]
+    count = batch // slab // 2
+    step = pl.program_id(0)
+    values = kernel_ref[...]
+    high = values.astype(jnp.bfloat16)
+    rest = values - high.astype(jnp.float32)
+    values = dot_in(jnp.concatenate([high, *split(rest)], axis=1), sort_ref[...])
+    for side, ref in enumerate(lines):
+        ref[...] = values[:, side * LANES : (side + 1) * LANES]
     groups = LANES // CUBE_COLS
     lane = lax.broadcasted_iota(jnp.int32, (1, LANES), 1)
-    k1 = first + lane // CUBE_COLS
-    weight = jnp.where(k1 == 0, 1.0, 2.0) / float(extent) ** 3
+    weight = jnp.where(first + lane // CUBE_COLS == 0, 1.0, 2.0) / float(extent) ** 3
     weight = jnp.where(lane // CUBE_COLS < held, weight, 0.0)
-    count = 32
+    group = lax.broadcasted_iota(jnp.int32, (count, LANES), 1) // CUBE_COLS
     for odd in range(2):
-
-        def turn_over(i, _):
-            for side, ref in enumerate(lines):
-                values = [
-                    ref[
-                        pl.ds(shift + k + (2 * i * count + odd) * slab, count, stride=2 * slab), :
-                    ]
-                    if k < held
-                    else jnp.zeros((count, LANES), jnp.float32)
-                    for k in range(groups)
-                ]
-                group = lax.broadcasted_iota(jnp.int32, (count, LANES), 1) // CUBE_COLS
-                step = 1
-                while step < groups:
-                    upper = group // step % 2 == 1
-                    turned = list(values)
-                    for k in range(groups):
-                        if k // step % 2 == 0:
-                            one, two = values[k], values[k + step]
-                            turned[k] = jnp.where(upper, pltpu.roll(two, step * CUBE_COLS, 1), one)
-                            turned[k + step] = jnp.where(
-                                upper, two, pltpu.roll(one, LANES - step * CUBE_COLS, 1)
-                            )
-                    values = turned
-                    step *= 2
-                row = pl.multiple_of(odd * (extent // 2) + i * count, count)
+        row = pl.multiple_of(odd * (extent // 2) + step * count, count)
+        for side, ref in enumerate(lines):
+            values = [
+                ref[pl.ds(shift + k + odd * slab, count, stride=2 * slab), :]
+                if k < held
+                else jnp.zeros((count, LANES), jnp.float32)
+                for k in range(groups)
+            ]
+            apart = 1
+            while apart < groups:
+                upper = group // apart % 2 == 1
+                turned = list(values)
                 for k in range(groups):
-                    filter_ref[side * groups + k, pl.ds(row, count), :] = values[k] * weight
-            return 0
-
-        lax.fori_loop(0, extent // 2 // count, turn_over, 0)
+                    if k // apart % 2 == 0:
+                        one, two = values[k], values[k + apart]
+                        turned[k] = jnp.where(upper, pltpu.roll(two, apart * CUBE_COLS, 1), one)
+                        turned[k + apart] = jnp.where(
+                            upper, two, pltpu.roll(one, LANES - apart * CUBE_COLS, 1)
+                        )
+                values = turned
+                apart *= 2
+            for k in range(groups):
+                filter_ref[side * groups + k, pl.ds(row, count), :] = values[k] * weight
 
 
 def spectral_tables(kernel_local):
@@ -417,26 +431,44 @@
     whole = pl.BlockSpec(memory_space=pltpu.VMEM)
     points = CUBE_ROWS * CUBE_COLS
     size = 2 * LANES + extent
-    cube, back, turn, filters = pl.pallas_call(
-        functools.partial(tables_kernel, extent, slab),
+    place = jnp.stack([me * slab + shift, shift])
+    scalars = pl.BlockSpec(memory_space=pltpu.SMEM)
+    cube_tables = pl.pallas_call(
+        functools.partial(tables_kernel, extent, slab // 2),
         out_shape=(
             jax.ShapeDtypeStruct((3 * points, size), jnp.bfloat16),
             jax.ShapeDtypeStruct((3 * size, points), jnp.bfloat16),
             jax.ShapeDtypeStruct((2 * extent // CUBE_ROWS, 2 * LANES), jnp.bfloat16),
-            jax.ShapeDtypeStruct((CUBE_COLS, extent, LANES), jnp.float32),
         ),
-        in_specs=[pl.BlockSpec(memory_space=pltpu.SMEM), whole, whole],
-        out_specs=(whole,) * 4,
-        scratch_shapes=[pltpu.VMEM((extent * slab, LANES), jnp.float32)] * 2,
+        in_specs=[scalars],
+        out_specs=(whole,) * 3,
+        cost_estimate=pl.CostEstimate(
+            flops=0, bytes_accessed=128 * extent * extent, transcendentals=0
+        ),
+        compiler_params=pltpu.CompilerParams(vmem_limit_bytes=VMEM_BYTES),
+        name="tables",
+    )(place)
+    batch = 32 * slab
+    filters = pl.pallas_call(
+        functools.partial(filter_kernel, extent, slab),
+        grid=(extent * slab // batch,),
+        out_shape=jax.ShapeDtypeStruct((CUBE_COLS, extent, LANES), jnp.float32),
+        in_specs=[
+            scalars,
+            pl.BlockSpec((batch, extent), lambda i: (i, 0)),
+            pl.BlockSpec((3 * extent, extent), lambda i: (0, 0)),
+        ],
+        out_specs=pl.BlockSpec((CUBE_COLS, extent, LANES), lambda i: (0, 0, 0)),
+        scratch_shapes=[pltpu.VMEM((batch, LANES), jnp.float32)] * 2,
         cost_estimate=pl.CostEstimate(
             flops=2 * extent * slab * 3 * extent * extent,
             bytes_accessed=8 * extent * slab * extent,
             transcendentals=0,
         ),
-        compiler_params=pltpu.CompilerParams(vmem_limit_bytes=32 * 1024 * 1024),
-        name="tables",
+        compiler_params=pltpu.CompilerParams(vmem_limit_bytes=VMEM_BYTES // 4),
+        name="filters",
     )(
-        jnp.stack([me * slab + shift, shift]),
+        place,
         kernel_local.reshape(extent * slab, extent),
         jnp.asarray(np.concatenate([sort] * 3, axis=0), jnp.bfloat16),
     )
@@ -446,14 +478,14 @@
     weight = np.where((k0 == 0) | (k0 == extent // 2), 1.0, 2.0) * (k0 <= extent // 2)
     weight = jnp.asarray(weight / float(extent) ** 3, jnp.float32)[:, None]
     edge = jnp.where(me == members // 2, kernel_local[:some, 0, :] * weight, 0.0)
-    return cube, back, turn, (*first, filters, *last, edge)
+    return edge, cube_tables, filters, first, last
 
 
 def cube_places(cubes, extent):
     slabs = extent // CUBE_COLS
     turns = extent // CUBE_ROWS
     plane, turn, slab = cubes // (turns * slabs), cubes // slabs % turns, cubes % slabs
-    codes = jnp.stack([plane, turn, slab] + [jnp.zeros_like(slab)] * 5, axis=1)
+    codes = jnp.stack([plane, turn, slab] + [jnp.zeros_like(slab)] * 5, axis=0)
     return slab * extent + plane, codes
 
 
@@ -462,27 +494,32 @@
     half_count = gathered[0].shape[0] * blocks
     slabs = extent // CUBE_COLS
     chunk = min(512, half_count)
+    operands = (gathered[0], cube, turn, gathered[1], back, *constants)
     whole = pl.BlockSpec(memory_space=pltpu.VMEM)
+    anywhere = pl.BlockSpec(memory_space=pl.ANY)
+    fixed = pl.BlockSpec(memory_space=pltpu.HBM)
     out = jax.ShapeDtypeStruct((half_count, LANES), jnp.float32)
     return pl.pallas_call(
-        functools.partial(spectral_kernel, extent, chunk, len(constants)),
+        functools.partial(spectral_kernel, extent, chunk, len(operands)),
         out_shape=(out, out),
-        in_specs=[pl.BlockSpec(memory_space=pltpu.SMEM)]
-        + [whole] * 6
-        + [pl.BlockSpec(memory_space=pl.ANY)] * len(constants),
-        out_specs=(whole, whole),
-        scratch_shapes=[pltpu.VMEM(table.shape, table.dtype) for table in constants]
+        in_specs=[pl.BlockSpec(memory_space=pltpu.SMEM), whole]
+        + [anywhere, fixed, fixed, anywhere]
+        + [fixed] * (len(operands) - 4),
+        out_specs=(anywhere, anywhere),
+        scratch_shapes=[pltpu.VMEM(operand.shape, operand.dtype) for operand in operands]
+        + [pltpu.VMEM((half_count, LANES), jnp.float32)] * 2
         + [pltpu.VMEM((slabs * extent, LANES), jnp.float32)] * (2 * COPIES)
         + [pltpu.VMEM((chunk, LANES), jnp.float32)] * 2
         + [pltpu.VMEM((extent, extent), jnp.float32)]
-        + [pltpu.SemaphoreType.DMA((len(constants),))],
-        compiler_params=pltpu.CompilerParams(vmem_limit_bytes=60 * 1024 * 1024),
+        + [pltpu.SemaphoreType.DMA((len(operands),))]
+        + [pltpu.SemaphoreType.DMA((2, half_count // chunk))],
+        compiler_params=pltpu.CompilerParams(vmem_limit_bytes=SPECTRAL_BYTES),
         name="spectral",
-    )(places[0], *gathered, places[1], cube, back, turn, *constants)
+    )(places[0], places[1], *operands)
 
 
 NOTE_ROWS = 8
-STEP_BLOCKS = 16
+STEP_BLOCKS = 32
 RIM_PART = 4
 
 
@@ -611,7 +648,7 @@
         cost_estimate=pl.CostEstimate(
             flops=4 * proj_tiles.size, bytes_accessed=4 * proj_tiles.size, transcendentals=0
         ),
-        compiler_params=pltpu.CompilerParams(vmem_limit_bytes=16 * 1024 * 1024),
+        compiler_params=pltpu.CompilerParams(vmem_limit_bytes=VMEM_BYTES // 4),
         name=name,
     )(proj_tiles, *rows, *whole)
 
@@ -644,7 +681,7 @@
     cubes_dev = extent // members * (extent // CUBE_ROWS) * (extent // CUBE_COLS)
     self_local = self_term.reshape(blocks, 64)
     cubes = owner_dev[:, 0] * cubes_dev + cube_slot
-    tables = spectral_tables(kernel_hat)
+    *late, first, last = spectral_tables(kernel_hat)
 
     rhs = right_side.reshape(blocks, 64)
     note_shape = (blocks + NOTE_ROWS + blocks // RIM_PART, LANES)
@@ -658,11 +695,12 @@
 
     note = jnp.pad(cubes.astype(jnp.float32)[None, :], ((0, 0), (0, LANES - blocks)))
     (payload,) = local_call(project_kernel, "project", proj_tiles, [rhs], [note], [note_shape])
-    gathered, tables = gather_pieces(payload, tables)
+    gathered, (edge, cube_tables, filters) = gather_pieces(payload, late)
+    tables = (*cube_tables, (*first, filters, *last, edge))
     base = base_of(rhs, gathered)
     all_cubes = jnp.concatenate([half[:, blocks, :blocks] for half in gathered], axis=0)
     places = cube_places(all_cubes.astype(jnp.int32).reshape(members * blocks), extent)
-    first, payload = local_call(
+    image_one, payload = local_call(
         complete_kernel,
         "complete",
         proj_tiles,
@@ -671,24 +709,24 @@
         [(blocks, 64), note_shape],
     )
     gathered, _ = gather_pieces(payload, ())
-    base = base_of(first, gathered)
+    base = base_of(image_one, gathered)
     sums = sum(jnp.sum(half[:, blocks, :], axis=0, keepdims=True) for half in gathered)
-    image, last = local_call(
+    image, weights = local_call(
         close_kernel,
         "close",
         proj_tiles,
-        [far(places, gathered), base, rhs, first],
+        [far(places, gathered), base, rhs, image_one],
         [sums],
         [(blocks, 64), (NOTE_ROWS, LANES)],
     )
-    last = total(last)
+    weights = total(weights)
     out = jax.ShapeDtypeStruct((blocks // 2, 128), jnp.float32)
     answer, residual = pl.pallas_call(
         finish_kernel,
         out_shape=(out, out),
         scratch_shapes=[pltpu.VMEM((blocks, 64), jnp.float32)],
         name="finish",
-    )(rhs, first, image, sums, last)
+    )(rhs, image_one, image, sums, weights)
     return (answer.reshape(blocks * 64), residual.reshape(blocks * 64))
 
 

time: 206 us -> 193 us (0.937)
  blocking collectives: 0 us -> 12.7 us
  waiting for transfers between devices: 52.4 us -> 41.5 us
  Pallas kernels: 92.1 us -> 83.7 us
  starting transfers between devices: 29.2 us -> 23.7 us
    all_to_all x0 -> x1, blocking collectives: none -> 12.7 us  [total(): return jnp.sum(lax.all_to_all(copies, 'px', 0, 0), axis=0)]
    ppermute x20 -> x16, waiting for transfers between devices: 52.4 us -> 41.5 us  [exchange(): return lax.ppermute(value, 'px', [(i, i ^ step) for i in range(members)])]
    pallas_call x3 -> x4, Pallas kernels: 80.7 us -> 74.7 us  [the longest x2 66.1 us: spectral(): pl.pallas_call(functools.partial(spectral_kernel, extent, chunk, len(oper...]
    ppermute x20 -> x16, starting transfers between devices: 29.2 us -> 23.7 us  [exchange(): return lax.ppermute(value, 'px', [(i, i ^ step) for i in range(members)])]
    pallas_call x3, Pallas kernels: 9.46 us -> 7.06 us  [local_call(): pl.pallas_call(kernel, grid=(blocks // STEP_BLOCKS,), out_shape=[jax.Shap...]
    unnamed x40 -> x36, local copies, waits for them, and re-layouts: 8.81 us -> 7.84 us
  transfers between devices with their start and end apart: 20 -> 16, of which waited for: 18 -> 14; matrix products, arithmetic and copies ran while one was open for 7% -> 8% of each run, Pallas kernels for 4% -> 4%
where the time goes in v4:
time: 193 us; the launch traced here: 192 us
  Pallas kernels  83.7 us (43%)
  waiting for transfers between devices  41.5 us (22%)
  starting transfers between devices  23.7 us (12%)
  other arithmetic  16.5 us (9%)
  local copies, waits for them, and re-layouts  12.9 us (7%)
  blocking collectives  12.7 us (7%)
    pallas_call x2, Pallas kernels, spectral(): pl.pallas_call(functools.partial(spectral_kernel, extent, chunk, len(oper...  66.1 us
    ppermute x16, waiting for transfers between devices, exchange(): return lax.ppermute(value, 'px', [(i, i ^ step) for i in range(members)])  41.5 us
    ppermute x16, starting transfers between devices, exchange(): return lax.ppermute(value, 'px', [(i, i ^ step) for i in range(members)])  23.7 us
    all_to_all x1, blocking collectives, total(): return jnp.sum(lax.all_to_all(copies, 'px', 0, 0), axis=0)  12.7 us
    unnamed x36, local copies, waits for them, and re-layouts  7.84 us
    pallas_call x3, Pallas kernels, local_call(): pl.pallas_call(kernel, grid=(blocks // STEP_BLOCKS,), out_shape=[jax.Shap...  7.06 us
    reduce_sum x2, other arithmetic, base_of(): jnp.sum(near_tiles * sources[:, None, :], axis=2)  6.68 us
    pallas_call x1, Pallas kernels, spectral_tables(): pl.pallas_call(functools.partial(filter_kernel, extent, slab), grid=(exte...  6.55 us
  transfers between devices with their start and end apart: 16, of which 14 were waited for; matrix products, arithmetic and copies ran while one was open for 8% of the time, Pallas kernels for 4%

profile of v4, /device:TPU:0, one launch (start us, length us, event | category | flops | bytes accessed | tf_op | source)
XLA Modules:
  0.0 192.0 jit_solution(8328159754235679248)
XLA Ops:
  0.6 0.8 reshape.199.values_ref.rhs_ref
  2.2 2.2 %copy-done = f32[128,64,128]{2,1,0:T(8,128)S(1)} copy-done((f32[128,64,128]{2,1,0:T(8,128)S(1)}, f32[128,64,128]{2,1,0:T(8,128)}, u32[]{:S(2)}) %copy-start) | copy-done | bytes 4194328
  4.4 1.5 project.1
  5.9 4.1 %collective-permute-start = (f32[1,168,128]{2,0,1:T(1,128)S(1)}, f32[1,168,128]{2,0,1:T(1,128)S(1)}, u32[]{:S(2)}, u32[]{:S(2)}) collective-permute-start(f32[1,168,128]{2,0,1:T(1,128)S(1)} %bitcast.60), channel_id=1, source_target_pairs={{0,8},{1,9},{2,10},{3,11},{4,12},{5,13},{6,14},{7,15},{8,0},{9,1},... | collective-permute-start | bytes 258056 | tf_op jit(solution)/shard_map/ppermute | solution.py:33
  10.0 1.3 slice.51
  11.3 0.8 fusion.1.refs_17_
  12.1 2.3 %collective-permute-done = f32[1,168,128]{2,0,1:T(1,128)S(1)} collective-permute-done((f32[1,168,128]{2,0,1:T(1,128)S(1)}, f32[1,168,128]{2,0,1:T(1,128)S(1)}, u32[]{:S(2)}, u32[]{:S(2)}) %collective-permute-start) | collective-permute-done | bytes 86048 | tf_op jit(solution)/shard_map/ppermute | solution.py:33
  14.5 0.8 collective-permute-start.1
  15.9 2.1 %tables.1 = (bf16[384,512]{1,0:T(8,128)(2,1)}, bf16[1536,128]{1,0:T(8,128)(2,1)}, bf16[64,256]{1,0:T(8,128)(2,1)}) custom-call(s32[2]{0:T(128)} %pad_add_fusion.place_ref), custom_call_target="tpu_custom_call" | custom-call | bytes 8388608 | tf_op jit(solution)/shard_map/tables/pallas_call | solution.py:436
  18.0 2.0 %collective-permute-done.1 = f32[2,168,128]{2,0,1:T(2,128)S(1)} collective-permute-done((f32[2,168,128]{2,0,1:T(2,128)S(1)}, f32[2,168,128]{2,0,1:T(2,128)S(1)}, u32[]{:S(2)}, u32[]{:S(2)}) %collective-permute-start.1) | collective-permute-done | bytes 172064 | tf_op jit(solution)/shard_map/ppermute | solution.py:33
  20.1 1.7 collective-permute-start.2
  21.8 2.2 %copy-done.4 = f32[256,16,256]{2,1,0:T(8,128)S(1)} copy-done((f32[256,16,256]{2,1,0:T(8,128)S(1)}, f32[256,16,256]{2,1,0:T(8,128)}, u32[]{:S(2)}) %copy-start.4) | copy-done | bytes 4194328
  24.6 6.5 %filters.1.refs_12_ = f32[16,256,128]{2,1,0:T(8,128)S(1)} custom-call(s32[2]{0:T(128)S(1)} %copy-done.10, f32[4096,256]{1,0:T(8,128)S(1)} %bitcast.55, bf16[768,256]{1,0:T(8,128)(2,1)S(1)} %copy-done.7), custom_call_target="tpu_custom_call" | custom-call | flops 1610612736 | bytes 8388608 | tf_op jit(solution)/shard_map/filters/pallas_call | solution.py:452
  31.2 1.3 copy-done.3
  32.9 2.1 %collective-permute-done.3.refs_3_ = f32[8,168,128]{2,1,0:T(8,128)S(1)} collective-permute-done((f32[8,168,128]{2,1,0:T(8,128)S(1)}, f32[8,168,128]{2,1,0:T(8,128)S(1)}, u32[]{:S(2)}, u32[]{:S(2)}) %collective-permute-start.3) | collective-permute-done | bytes 688160 | tf_op jit(solution)/shard_map/ppermute | solution.py:33
  36.6 33.1 %spectral.2 = (f32[1024,128]{1,0:T(8,128)}, f32[1024,128]{1,0:T(8,128)}) custom-call(s32[2048]{0:T(1024)} %fusion.3.rows_ref, s32[8,2048]{1,0:T(8,128)} %stack.22.codes_ref, f32[8,168,128]{2,1,0:T(8,128)} %copy-done.12, bf16[384,512]{1,0:T(8,128)(2,1)} %get-tuple-element.29.refs_1_, bf16[64,256]{1,0:T(8,128)(2,1)} %get-tuple-element.30.refs_2_, ...), custom_call_target="tpu_custom_call" | custom-call | tf_op jit(solution)/shard_map/spectral/pallas_call | solution.py:502
  70.2 1.7 collective-permute-done.4
  71.9 1.1 add.156
  73.6 0.9 select_bitcast_fusion.3
  74.5 0.7 gather_fusion
  75.3 6.2 %collective-permute-done.5 = f32[512,128]{1,0:T(8,128)S(1)} collective-permute-done((f32[512,128]{1,0:T(8,128)S(1)}, f32[512,128]{1,0:T(8,128)S(1)}, u32[]{:S(2)}, u32[]{:S(2)}) %collective-permute-start.5) | collective-permute-done | bytes 262176 | tf_op jit(solution)/shard_map/ppermute | solution.py:33
  81.5 1.4 collective-permute-start.6
  83.0 3.3 %multiply_reduce_fusion.1 = f32[128,64]{1,0:T(8,128)S(1)} fusion(f32[128,64,128]{2,1,0:T(8,128)} %param.27, f32[128,128]{1,0:T(8,128)S(1)} %mul.61), kind=kLoop, calls=%fused_computation.3 | loop fusion | flops 2088960 | bytes 4292608 | tf_op jit(solution)/shard_map/reduce_sum | solution.py:691
  86.6 3.2 %collective-permute-start.7 = (f32[128,128]{1,0:T(8,128)S(1)}, f32[128,128]{1,0:T(8,128)S(1)}, u32[]{:S(2)}, u32[]{:S(2)}) collective-permute-start(f32[128,128]{1,0:T(8,128)S(1)} %slice.78), channel_id=1, source_target_pairs={{0,8},{1,9},{2,10},{3,11},{4,12},{5,13},{6,14},{7,15},{8,0},{9,1},... | collective-permute-start | bytes 196616 | tf_op jit(solution)/shard_map/ppermute | solution.py:33
  89.8 2.2 %collective-permute-done.7 = f32[128,128]{1,0:T(8,128)S(1)} collective-permute-done((f32[128,128]{1,0:T(8,128)S(1)}, f32[128,128]{1,0:T(8,128)S(1)}, u32[]{:S(2)}, u32[]{:S(2)}) %collective-permute-start.7) | collective-permute-done | bytes 65568 | tf_op jit(solution)/shard_map/ppermute | solution.py:33
  92.1 3.2 %complete.1 = (f32[128,64]{1,0:T(8,128)S(1)}, f32[168,128]{1,0:T(8,128)S(1)}) custom-call(f32[128,64,128]{2,1,0:T(8,128)S(1)} %copy-done.1, f32[128,128]{1,0:T(8,128)S(1)} %slice_add_fusion.5.picked_ref, f32[128,64]{1,0:T(8,128)S(1)} %multiply_add_fusion.1.base_ref, f32[128,64]{1,0:T(8,128)S(1)} %reshape.199.values_ref.rhs_ref), custom_call_target="tpu_custom_call" | custom-call | flops 4194304 | bytes 4194304 | tf_op jit(solution)/shard_map/complete/pallas_call | solution.py:640
  95.2 3.0 %collective-permute-start.8 = (f32[1,168,128]{2,1,0:T(8,128)S(1)}, f32[1,168,128]{2,1,0:T(8,128)S(1)}, u32[]{:S(2)}, u32[]{:S(2)}) collective-permute-start(f32[1,168,128]{2,1,0:T(8,128)S(1)} %bitcast.56), channel_id=1, source_target_pairs={{0,8},{1,9},{2,10},{3,11},{4,12},{5,13},{6,14},{7,15},{8,0},{9,1},... | collective-permute-start | bytes 258056 | tf_op jit(solution)/shard_map/ppermute | solution.py:33
  98.3 2.9 %collective-permute-done.8 = f32[1,168,128]{2,1,0:T(8,128)S(1)} collective-permute-done((f32[1,168,128]{2,1,0:T(8,128)S(1)}, f32[1,168,128]{2,1,0:T(8,128)S(1)}, u32[]{:S(2)}, u32[]{:S(2)}) %collective-permute-start.8) | collective-permute-done | bytes 86048 | tf_op jit(solution)/shard_map/ppermute | solution.py:33
  101.2 1.9 collective-permute-start.9
  103.1 3.6 %collective-permute-done.9 = f32[2,168,128]{2,1,0:T(8,128)S(1)} collective-permute-done((f32[2,168,128]{2,1,0:T(8,128)S(1)}, f32[2,168,128]{2,1,0:T(8,128)S(1)}, u32[]{:S(2)}, u32[]{:S(2)}) %collective-permute-start.9) | collective-permute-done | bytes 172064 | tf_op jit(solution)/shard_map/ppermute | solution.py:33
  107.3 6.7 %collective-permute-done.10 = f32[4,168,128]{2,1,0:T(8,128)S(1)} collective-permute-done((f32[4,168,128]{2,1,0:T(8,128)S(1)}, f32[4,168,128]{2,1,0:T(8,128)S(1)}, u32[]{:S(2)}, u32[]{:S(2)}) %collective-permute-start.10) | collective-permute-done | bytes 344096 | tf_op jit(solution)/shard_map/ppermute | solution.py:33
  114.2 2.1 %collective-permute-done.11.refs_3_ = f32[8,168,128]{2,1,0:T(8,128)S(1)} collective-permute-done((f32[8,168,128]{2,1,0:T(8,128)S(1)}, f32[8,168,128]{2,1,0:T(8,128)S(1)}, u32[]{:S(2)}, u32[]{:S(2)}) %collective-permute-start.11) | collective-permute-done | bytes 688160 | tf_op jit(solution)/shard_map/ppermute | solution.py:33
  116.3 0.9 copy-done.14
  117.2 33.0 %spectral.3 = (f32[1024,128]{1,0:T(8,128)}, f32[1024,128]{1,0:T(8,128)}) custom-call(s32[2048]{0:T(1024)} %fusion.3.rows_ref, s32[8,2048]{1,0:T(8,128)} %stack.22.codes_ref, f32[8,168,128]{2,1,0:T(8,128)} %copy-done.11, bf16[384,512]{1,0:T(8,128)(2,1)} %get-tuple-element.29.refs_1_, bf16[64,256]{1,0:T(8,128)(2,1)} %get-tuple-element.30.refs_2_, ...), custom_call_target="tpu_custom_call" | custom-call | tf_op jit(solution)/shard_map/spectral/pallas_call | solution.py:502
  150.4 0.8 slice_reduce_fusion.1
  151.2 0.9 select_bitcast_fusion.1
  152.0 0.7 gather_fusion.1
  152.9 1.3 add.175
  154.7 3.3 %multiply_reduce_fusion = f32[128,64]{1,0:T(8,128)S(1)} fusion(f32[128,64,128]{2,1,0:T(8,128)} %param.27, f32[128,128]{1,0:T(8,128)S(1)} %mul.65), kind=kLoop, calls=%fused_computation.2 | loop fusion | flops 2088960 | bytes 4292608 | tf_op jit(solution)/shard_map/reduce_sum | solution.py:691
  158.1 4.7 %collective-permute-done.13 = f32[512,128]{1,0:T(8,128)S(1)} collective-permute-done((f32[512,128]{1,0:T(8,128)S(1)}, f32[512,128]{1,0:T(8,128)S(1)}, u32[]{:S(2)}, u32[]{:S(2)}) %collective-permute-start.13) | collective-permute-done | bytes 262176 | tf_op jit(solution)/shard_map/ppermute | solution.py:33
  162.8 1.9 collective-permute-start.14
  164.7 0.8 slice_reduce_fusion
  165.5 2.4 %collective-permute-done.14 = f32[256,128]{1,0:T(8,128)S(1)} collective-permute-done((f32[256,128]{1,0:T(8,128)S(1)}, f32[256,128]{1,0:T(8,128)S(1)}, u32[]{:S(2)}, u32[]{:S(2)}) %collective-permute-start.14) | collective-permute-done | bytes 131104 | tf_op jit(solution)/shard_map/ppermute | solution.py:33
  168.0 3.5 %collective-permute-start.15 = (f32[128,128]{1,0:T(8,128)S(1)}, f32[128,128]{1,0:T(8,128)S(1)}, u32[]{:S(2)}, u32[]{:S(2)}) collective-permute-start(f32[128,128]{1,0:T(8,128)S(1)} %slice.84), channel_id=1, source_target_pairs={{0,8},{1,9},{2,10},{3,11},{4,12},{5,13},{6,14},{7,15},{8,0},{9,1},... | collective-permute-start | bytes 196616 | tf_op jit(solution)/shard_map/ppermute | solution.py:33
  171.5 2.2 %collective-permute-done.15 = f32[128,128]{1,0:T(8,128)S(1)} collective-permute-done((f32[128,128]{1,0:T(8,128)S(1)}, f32[128,128]{1,0:T(8,128)S(1)}, u32[]{:S(2)}, u32[]{:S(2)}) %collective-permute-start.15) | collective-permute-done | bytes 65568 | tf_op jit(solution)/shard_map/ppermute | solution.py:33
  173.8 2.4 %close.1 = (f32[128,64]{1,0:T(8,128)S(1)}, f32[8,128]{1,0:T(8,128)S(1)}) custom-call(f32[128,64,128]{2,1,0:T(8,128)S(1)} %copy-done.2, f32[128,128]{1,0:T(8,128)S(1)} %slice_add_fusion.4.picked_ref, f32[128,64]{1,0:T(8,128)S(1)} %multiply_add_fusion.base_ref, f32[128,64]{1,0:T(8,128)S(1)} %reshape.199.values_ref.rhs_ref, ...), custom_call_target="tpu_custom_call" | custom-call | flops 4194304 | bytes 4194304 | tf_op jit(solution)/shard_map/close/pallas_call | solution.py:640
  176.8 12.7 %all_to_all.5 = f32[16,8,128]{2,1,0:T(8,128)S(1)} all-to-all(f32[16,8,128]{2,1,0:T(8,128)S(1)} %broadcast_in_dim.39), channel_id=1, replica_groups=mesh['groups'=2,'px'=16] {'px'}, dimensions={0} | all-to-all | bytes 131072 | tf_op jit(solution)/shard_map/all_to_all | solution.py:60
  190.1 1.9 finish.1
  (86 shorter events, 8.6 us)
Async XLA Ops:
  0.6 10.7 %copy-start.16 = (f32[136]{0:T(256)S(1)}, f32[136]{0:T(256)}, u32[]{:S(2)}) copy-start(f32[136]{0:T(256)} %constant.220.clone) | copy-start | bytes 1636
  1.5 172.3 %copy-start.5 = (f32[128,64]{1,0:T(8,128)}, f32[128,64]{1,0:T(8,128)S(1)}, u32[]{:S(2)}) copy-start(f32[128,64]{1,0:T(8,128)S(1)} %reshape.199.values_ref.rhs_ref) | copy-start | bytes 98308
  2.2 2.2 %copy-start = (f32[128,64,128]{2,1,0:T(8,128)S(1)}, f32[128,64,128]{2,1,0:T(8,128)}, u32[]{:S(2)}) copy-start(f32[128,64,128]{2,1,0:T(8,128)} %proj_ref.5) | copy-start | bytes 12582916
  4.4 17.5 %copy-start.7 = (bf16[768,256]{1,0:T(8,128)(2,1)S(1)}, bf16[768,256]{1,0:T(8,128)(2,1)}, u32[]{:S(2)}) copy-start(bf16[768,256]{1,0:T(8,128)(2,1)} %constant.208.clone.sort_ref) | copy-start | bytes 1179652
  5.9 8.4 %collective-permute-start = (f32[1,168,128]{2,0,1:T(1,128)S(1)}, f32[1,168,128]{2,0,1:T(1,128)S(1)}, u32[]{:S(2)}, u32[]{:S(2)}) collective-permute-start(f32[1,168,128]{2,0,1:T(1,128)S(1)} %bitcast.60), channel_id=1, source_target_pairs={{0,8},{1,9},{2,10},{3,11},{4,12},{5,13},{6,14},{7,15},{8,0},{9,1},... | collective-permute-start | bytes 258056 | tf_op jit(solution)/shard_map/ppermute | solution.py:33
  14.5 5.5 %collective-permute-start.1 = (f32[2,168,128]{2,0,1:T(2,128)S(1)}, f32[2,168,128]{2,0,1:T(2,128)S(1)}, u32[]{:S(2)}, u32[]{:S(2)}) collective-permute-start(f32[2,168,128]{2,0,1:T(2,128)S(1)} %pad_maximum_fusion.4), channel_id=1, source_target_pairs={{0,4},{1,5},{2,6},{3,7},{4,0},{5,1},{6,2},{7,3},{8,12},{9,13},{10,... | collective-permute-start | bytes 516104 | tf_op jit(solution)/shard_map/ppermute | solution.py:33
  20.1 12.4 %collective-permute-start.2 = (f32[4,168,128]{2,0,1:T(4,128)S(1)}, f32[4,168,128]{2,0,1:T(4,128)S(1)}, u32[]{:S(2)}, u32[]{:S(2)}) collective-permute-start(f32[4,168,128]{2,0,1:T(4,128)S(1)} %pad_maximum_fusion.2), channel_id=1, source_target_pairs={{0,2},{1,3},{2,0},{3,1},{4,6},{5,7},{6,4},{7,5},{8,10},{9,11},{10,... | collective-permute-start | bytes 1032200 | tf_op jit(solution)/shard_map/ppermute | solution.py:33
  21.8 2.2 %copy-start.4 = (f32[256,16,256]{2,1,0:T(8,128)S(1)}, f32[256,16,256]{2,1,0:T(8,128)}, u32[]{:S(2)}) copy-start(f32[256,16,256]{2,1,0:T(8,128)} %param.28) | copy-start | bytes 12582916
  24.0 0.6 copy-start.10
  31.2 1.3 copy-start.3
  32.8 3.8 %copy-start.12 = (f32[8,168,128]{2,1,0:T(8,128)}, f32[8,168,128]{2,1,0:T(8,128)S(1)}, u32[]{:S(2)}) copy-start(f32[8,168,128]{2,1,0:T(8,128)S(1)} %copy.31.refs_0_) | copy-start | bytes 2064388
  32.8 2.2 %collective-permute-start.3 = (f32[8,168,128]{2,1,0:T(8,128)S(1)}, f32[8,168,128]{2,1,0:T(8,128)S(1)}, u32[]{:S(2)}, u32[]{:S(2)}) collective-permute-start(f32[8,168,128]{2,1,0:T(8,128)S(1)} %copy.31.refs_0_), channel_id=1, source_target_pairs={{0,1},{1,0},{2,3},{3,2},{4,5},{5,4},{6,7},{7,6},{8,9},{9,8},{10,11... | collective-permute-start | bytes 2064392 | tf_op jit(solution)/shard_map/ppermute | solution.py:33
  35.1 1.6 copy-start.13
  36.6 33.3 %copy-start.17 = (s32[128,2]{0,1:T(2,128)S(1)}, s32[128,2]{0,1:T(2,128)}, u32[]{:S(2)}) copy-start(s32[128,2]{0,1:T(2,128)} %param.26) | copy-start | bytes 3076
  36.6 36.9 %copy-start.15 = (f32[8192]{0:T(1024)S(1)}, f32[8192]{0:T(1024)}, u32[]{:S(2)}) copy-start(f32[8192]{0:T(1024)} %param.22) | copy-start | bytes 98308
  69.7 2.2 %collective-permute-start.4 = (f32[1024,128]{1,0:T(8,128)}, f32[1024,128]{1,0:T(8,128)S(1)}, u32[]{:S(2)}, u32[]{:S(2)}) collective-permute-start(f32[1024,128]{1,0:T(8,128)} %get-tuple-element.35), channel_id=1, source_target_pairs={{0,1},{1,0},{2,3},{3,2},{4,5},{5,4},{6,7},{7,6},{8,9},{9,8},{10,11... | collective-permute-start | bytes 1572872 | tf_op jit(solution)/shard_map/ppermute | solution.py:33
  73.1 8.4 %collective-permute-start.5 = (f32[512,128]{1,0:T(8,128)S(1)}, f32[512,128]{1,0:T(8,128)S(1)}, u32[]{:S(2)}, u32[]{:S(2)}) collective-permute-start(f32[512,128]{1,0:T(8,128)S(1)} %slice.74), channel_id=1, source_target_pairs={{0,2},{1,3},{2,0},{3,1},{4,6},{5,7},{6,4},{7,5},{8,10},{9,11},{10,... | collective-permute-start | bytes 786440 | tf_op jit(solution)/shard_map/ppermute | solution.py:33
  75.3 16.7 %copy-start.1 = (f32[128,64,128]{2,1,0:T(8,128)S(1)}, f32[128,64,128]{2,1,0:T(8,128)}, u32[]{:S(2)}) copy-start(f32[128,64,128]{2,1,0:T(8,128)} %proj_ref.5) | copy-start | bytes 12582916
  81.5 5.0 %collective-permute-start.6 = (f32[256,128]{1,0:T(8,128)S(1)}, f32[256,128]{1,0:T(8,128)S(1)}, u32[]{:S(2)}, u32[]{:S(2)}) collective-permute-start(f32[256,128]{1,0:T(8,128)S(1)} %slice.76), channel_id=1, source_target_pairs={{0,4},{1,5},{2,6},{3,7},{4,0},{5,1},{6,2},{7,3},{8,12},{9,13},{10,... | collective-permute-start | bytes 393224 | tf_op jit(solution)/shard_map/ppermute | solution.py:33
  86.6 5.4 %collective-permute-start.7 = (f32[128,128]{1,0:T(8,128)S(1)}, f32[128,128]{1,0:T(8,128)S(1)}, u32[]{:S(2)}, u32[]{:S(2)}) collective-permute-start(f32[128,128]{1,0:T(8,128)S(1)} %slice.78), channel_id=1, source_target_pairs={{0,8},{1,9},{2,10},{3,11},{4,12},{5,13},{6,14},{7,15},{8,0},{9,1},... | collective-permute-start | bytes 196616 | tf_op jit(solution)/shard_map/ppermute | solution.py:33
  95.2 78.5 %copy-start.6 = (f32[128,64]{1,0:T(8,128)}, f32[128,64]{1,0:T(8,128)S(1)}, u32[]{:S(2)}) copy-start(f32[128,64]{1,0:T(8,128)S(1)} %get-tuple-element.36.first_ref) | copy-start | bytes 98308
  95.2 5.9 %collective-permute-start.8 = (f32[1,168,128]{2,1,0:T(8,128)S(1)}, f32[1,168,128]{2,1,0:T(8,128)S(1)}, u32[]{:S(2)}, u32[]{:S(2)}) collective-permute-start(f32[1,168,128]{2,1,0:T(8,128)S(1)} %bitcast.56), channel_id=1, source_target_pairs={{0,8},{1,9},{2,10},{3,11},{4,12},{5,13},{6,14},{7,15},{8,0},{9,1},... | collective-permute-start | bytes 258056 | tf_op jit(solution)/shard_map/ppermute | solution.py:33
  101.2 5.5 %collective-permute-start.9 = (f32[2,168,128]{2,1,0:T(8,128)S(1)}, f32[2,168,128]{2,1,0:T(8,128)S(1)}, u32[]{:S(2)}, u32[]{:S(2)}) collective-permute-start(f32[2,168,128]{2,1,0:T(8,128)S(1)} %pad_maximum_fusion.5), channel_id=1, source_target_pairs={{0,4},{1,5},{2,6},{3,7},{4,0},{5,1},{6,2},{7,3},{8,12},{9,13},{10,... | collective-permute-start | bytes 516104 | tf_op jit(solution)/shard_map/ppermute | solution.py:33
  106.7 7.3 %collective-permute-start.10 = (f32[4,168,128]{2,1,0:T(8,128)S(1)}, f32[4,168,128]{2,1,0:T(8,128)S(1)}, u32[]{:S(2)}, u32[]{:S(2)}) collective-permute-start(f32[4,168,128]{2,1,0:T(8,128)S(1)} %pad_maximum_fusion.3), channel_id=1, source_target_pairs={{0,2},{1,3},{2,0},{3,1},{4,6},{5,7},{6,4},{7,5},{8,10},{9,11},{10,... | collective-permute-start | bytes 1032200 | tf_op jit(solution)/shard_map/ppermute | solution.py:33
  114.1 2.2 %copy-start.11 = (f32[8,168,128]{2,1,0:T(8,128)}, f32[8,168,128]{2,1,0:T(8,128)S(1)}, u32[]{:S(2)}) copy-start(f32[8,168,128]{2,1,0:T(8,128)S(1)} %pad_maximum_fusion.1.refs_0_) | copy-start | bytes 2064388
  114.1 2.2 %collective-permute-start.11 = (f32[8,168,128]{2,1,0:T(8,128)S(1)}, f32[8,168,128]{2,1,0:T(8,128)S(1)}, u32[]{:S(2)}, u32[]{:S(2)}) collective-permute-start(f32[8,168,128]{2,1,0:T(8,128)S(1)} %pad_maximum_fusion.1.refs_0_), channel_id=1, source_target_pairs={{0,1},{1,0},{2,3},{3,2},{4,5},{5,4},{6,7},{7,6},{8,9},{9,8},{10,11... | collective-permute-start | bytes 2064392 | tf_op jit(solution)/shard_map/ppermute | solution.py:33
  116.3 0.9 copy-start.14
  150.2 2.7 %collective-permute-start.12 = (f32[1024,128]{1,0:T(8,128)}, f32[1024,128]{1,0:T(8,128)S(1)}, u32[]{:S(2)}, u32[]{:S(2)}) collective-permute-start(f32[1024,128]{1,0:T(8,128)} %get-tuple-element.39), channel_id=1, source_target_pairs={{0,1},{1,0},{2,3},{3,2},{4,5},{5,4},{6,7},{7,6},{8,9},{9,8},{10,11... | collective-permute-start | bytes 1572872 | tf_op jit(solution)/shard_map/ppermute | solution.py:33
  152.9 20.9 %copy-start.2 = (f32[128,64,128]{2,1,0:T(8,128)S(1)}, f32[128,64,128]{2,1,0:T(8,128)}, u32[]{:S(2)}) copy-start(f32[128,64,128]{2,1,0:T(8,128)} %proj_ref.5) | copy-start | bytes 12582916
  154.2 8.6 %collective-permute-start.13 = (f32[512,128]{1,0:T(8,128)S(1)}, f32[512,128]{1,0:T(8,128)S(1)}, u32[]{:S(2)}, u32[]{:S(2)}) collective-permute-start(f32[512,128]{1,0:T(8,128)S(1)} %slice.80), channel_id=1, source_target_pairs={{0,2},{1,3},{2,0},{3,1},{4,6},{5,7},{6,4},{7,5},{8,10},{9,11},{10,... | collective-permute-start | bytes 786440 | tf_op jit(solution)/shard_map/ppermute | solution.py:33
  162.8 5.1 %collective-permute-start.14 = (f32[256,128]{1,0:T(8,128)S(1)}, f32[256,128]{1,0:T(8,128)S(1)}, u32[]{:S(2)}, u32[]{:S(2)}) collective-permute-start(f32[256,128]{1,0:T(8,128)S(1)} %slice.82), channel_id=1, source_target_pairs={{0,4},{1,5},{2,6},{3,7},{4,0},{5,1},{6,2},{7,3},{8,12},{9,13},{10,... | collective-permute-start | bytes 393224 | tf_op jit(solution)/shard_map/ppermute | solution.py:33
  168.0 5.8 %collective-permute-start.15 = (f32[128,128]{1,0:T(8,128)S(1)}, f32[128,128]{1,0:T(8,128)S(1)}, u32[]{:S(2)}, u32[]{:S(2)}) collective-permute-start(f32[128,128]{1,0:T(8,128)S(1)} %slice.84), channel_id=1, source_target_pairs={{0,8},{1,9},{2,10},{3,11},{4,12},{5,13},{6,14},{7,15},{8,0},{9,1},... | collective-permute-start | bytes 196616 | tf_op jit(solution)/shard_map/ppermute | solution.py:33
  171.5 18.6 %copy-start.9 = (f32[1,128]{1,0:T(1,128)}, f32[1,128]{1,0:T(1,128)S(1)}, u32[]{:S(2)}) copy-start(f32[1,128]{1,0:T(1,128)S(1)} %add_bitcast_fusion.sums_ref) | copy-start | bytes 1540
  176.2 0.6 copy-start.8

commit v5 on v4

--- a/solution.py
+++ b/solution.py
@@ -31,6 +31,11 @@
 def exchange(value, step):
     members = lax.axis_size("px")
     return lax.ppermute(value, "px", [(i, i ^ step) for i in range(members)])
+
+
+def step_orders(members):
+    steps = partner_steps(members)
+    return steps[:-3], (steps[-3:-1], steps[-3:-1][::-1]), steps[-1]
 
 
 def gather_pieces(piece, beside):
@@ -45,13 +50,19 @@
     return (pieces, exchange(pieces, steps[-1])), done
 
 
-def scatter_pieces(kept, sent):
-    steps = list(reversed(partner_steps(lax.axis_size("px"))))
-    pieces = kept + exchange(sent, steps[0])
-    for step in steps[1:]:
+def scatter_pieces(kept, sent, beside):
+    lead, orders, last = step_orders(lax.axis_size("px"))
+    arrived = exchange(sent, last)
+    parts = [kept[i] + arrived[i] for i in range(2)]
+    parts, beside = lax.optimization_barrier((parts, beside))
+    for steps in zip(*(order[::-1] for order in orders)):
+        half = parts[0].shape[0] // 2
+        parts = [part[:half] + exchange(part[half:], step) for part, step in zip(parts, steps)]
+    pieces = jnp.concatenate(parts, axis=1)
+    for step in lead[::-1]:
         half = pieces.shape[0] // 2
         pieces = pieces[:half] + exchange(pieces[half:], step)
-    return pieces
+    return pieces[0], beside
 
 
 def total(value):
@@ -113,19 +124,28 @@
     grids, refs = refs[: 2 * COPIES], refs[2 * COPIES :]
     grids = [grids[2 * i : 2 * i + 2] for i in range(COPIES)]
     rows, dense, sem, out_sem = refs[:2], refs[2], refs[3], refs[4]
-    near_ref, cube_ref, turn_ref, distant_ref, back_ref = tables[:5]
+    near_ref, distant_ref, cube_ref, turn_ref, back_ref = tables[:5]
     even_ref, odd_ref, uneven_ref, unodd_ref = tables[5:9]
     line_ref, unline_ref, twist_ref, filter_ref = tables[9:13]
     plane_ref, unplane_ref, full_ref, unfull_ref, edge_ref = tables[13:]
-    half_count = kept_ref.shape[0]
-    blocks = half_count // near_ref.shape[0]
+    pieces, blocks = kept_ref.shape[:2]
+    half_count = pieces * blocks
     slabs = extent // CUBE_COLS
     half = extent // 2
+    lead = pieces // 4
+    taken = chunk // blocks
+    bunch = min(lead, taken)
+
+    def other_place(place):
+        first, second = place // lead % 2, place // (2 * lead)
+        return place % lead + lead * (second + 2 * first)
+
     moves = [
         pltpu.make_async_copy(source, table, sem.at[i])
         for i, (source, table) in enumerate(zip(sources, tables))
     ]
-    for move in moves[:3]:
+    early, late = [moves[0], *moves[2:4]], moves[1:2]
+    for move in early:
         move.start()
 
     def clear(i, _):
@@ -148,8 +168,8 @@
 
     def spread(source_ref, offset, step, _):
         start = pl.multiple_of(offset + step * chunk, chunk)
-        taken = source_ref[pl.ds(step * (chunk // blocks), chunk // blocks), :blocks, :]
-        both = dot_in(left_terms(taken.reshape(chunk, LANES)), cube_ref[...])
+        values = source_ref[pl.ds(step * taken, taken), :blocks, :]
+        both = dot_in(left_terms(values.reshape(chunk, LANES)), cube_ref[...])
         codes, wide, cosine, sine = marks(start)
         real, imag = both[:, :LANES], both[:, LANES : 2 * LANES]
         rows[0][...] = real * cosine + imag * sine
@@ -172,13 +192,14 @@
         lax.fori_loop(0, chunk // COPIES, add, 0, unroll=8)
         return 0
 
-    for move in moves[:3]:
+    for move in early:
         move.wait()
-    for move in moves[3:]:
+    for move in late + moves[4:]:
         move.start()
     for index, source_ref in enumerate((near_ref, distant_ref)):
         if index:
-            moves[3].wait()
+            for move in late:
+                move.wait()
         body = functools.partial(spread, source_ref, index * half_count)
         lax.fori_loop(0, half_count // chunk, body, 0)
 
@@ -264,12 +285,19 @@
     dense[...] = dot_in(unplane_ref[...], right_terms(planes))
     across(1)
 
-    def leave(index, step):
-        place = pl.ds(pl.multiple_of(step * chunk, chunk), chunk)
-        out_ref = (kept_ref, sent_ref)[index]
-        return pltpu.make_async_copy(
-            out_ref.at[place, :], (kept_out, sent_out)[index].at[place, :], out_sem.at[index, step]
-        )
+    def leaving(index, step):
+        out, ref = (kept_out, sent_out)[index], (kept_ref, sent_ref)[index]
+        cut = blocks // 2
+        place = pl.ds(step * taken, taken)
+        moves = [(ref.at[place, :cut, :], out.at[0, place])]
+        for i in range(taken // bunch):
+            start = step * taken + i * bunch
+            goal = out.at[1, pl.ds(other_place(start), bunch)]
+            moves.append((ref.at[pl.ds(start, bunch), cut:, :], goal))
+        return [
+            pltpu.make_async_copy(*move, out_sem.at[index, step, i])
+            for i, move in enumerate(moves)
+        ]
 
     def collect(index, step, _):
         out_ref = (kept_ref, sent_ref)[index]
@@ -292,10 +320,10 @@
         both = jnp.concatenate(
             [real * cosine - imag * sine, imag * cosine + real * sine, edge], axis=1
         )
-        out_ref[pl.ds(pl.multiple_of(step * chunk, chunk), chunk), :] = dot_in(
-            left_terms(both), back_ref[...]
-        )
-        leave(index, step).start()
+        both = dot_in(left_terms(both), back_ref[...])
+        out_ref[pl.ds(step * taken, taken), :, :] = both.reshape(taken, blocks, LANES)
+        for move in leaving(index, step):
+            move.start()
         return 0
 
     for index in range(2):
@@ -303,7 +331,8 @@
 
     def finish(step, _):
         for index in range(2):
-            leave(index, step).wait()
+            for move in leaving(index, step):
+                move.wait()
         return 0
 
     lax.fori_loop(0, half_count // chunk, finish, 0)
@@ -491,28 +520,31 @@
 
 def spectral(places, extent, blocks, gathered, tables):
     cube, back, turn, constants = tables
-    half_count = gathered[0].shape[0] * blocks
+    pieces = gathered[0].shape[0]
     slabs = extent // CUBE_COLS
-    chunk = min(512, half_count)
-    operands = (gathered[0], cube, turn, gathered[1], back, *constants)
-    whole = pl.BlockSpec(memory_space=pltpu.VMEM)
+    taken = min(4, pieces)
+    chunk = taken * blocks
+    operands = (*gathered, cube, turn, back, *constants)
     anywhere = pl.BlockSpec(memory_space=pl.ANY)
     fixed = pl.BlockSpec(memory_space=pltpu.HBM)
-    out = jax.ShapeDtypeStruct((half_count, LANES), jnp.float32)
+    out = jax.ShapeDtypeStruct((2, pieces, blocks // 2, LANES), jnp.float32)
     return pl.pallas_call(
         functools.partial(spectral_kernel, extent, chunk, len(operands)),
         out_shape=(out, out),
-        in_specs=[pl.BlockSpec(memory_space=pltpu.SMEM), whole]
-        + [anywhere, fixed, fixed, anywhere]
-        + [fixed] * (len(operands) - 4),
+        in_specs=[
+            pl.BlockSpec(memory_space=pltpu.SMEM),
+            pl.BlockSpec(memory_space=pltpu.VMEM),
+            *[anywhere] * 2,
+            *[fixed] * (len(operands) - 2),
+        ],
         out_specs=(anywhere, anywhere),
         scratch_shapes=[pltpu.VMEM(operand.shape, operand.dtype) for operand in operands]
-        + [pltpu.VMEM((half_count, LANES), jnp.float32)] * 2
+        + [pltpu.VMEM((pieces, blocks, LANES), jnp.float32)] * 2
         + [pltpu.VMEM((slabs * extent, LANES), jnp.float32)] * (2 * COPIES)
         + [pltpu.VMEM((chunk, LANES), jnp.float32)] * 2
         + [pltpu.VMEM((extent, extent), jnp.float32)]
         + [pltpu.SemaphoreType.DMA((len(operands),))]
-        + [pltpu.SemaphoreType.DMA((2, half_count // chunk))],
+        + [pltpu.SemaphoreType.DMA((2, pieces // taken, 5))],
         compiler_params=pltpu.CompilerParams(vmem_limit_bytes=SPECTRAL_BYTES),
         name="spectral",
     )(places[0], places[1], *operands)
@@ -686,36 +718,37 @@
     rhs = right_side.reshape(blocks, 64)
     note_shape = (blocks + NOTE_ROWS + blocks // RIM_PART, LANES)
 
-    def base_of(values, gathered):
-        sources = halo(values, gathered[1])[near_src].reshape(blocks, near_tiles.shape[2])
+    def base_of(values, extended):
+        sources = extended[near_src].reshape(blocks, near_tiles.shape[2])
         return self_local * values + jnp.sum(near_tiles * sources[:, None, :], axis=2)
 
-    def far(places, gathered):
-        return scatter_pieces(*spectral(places, extent, blocks, gathered, tables))
+    def far(places, gathered, values):
+        extended = halo(values, gathered[1])
+        shares = spectral(places, extent, blocks, gathered, tables)
+        picked, extended = scatter_pieces(*shares, extended)
+        return picked, base_of(values, extended)
 
     note = jnp.pad(cubes.astype(jnp.float32)[None, :], ((0, 0), (0, LANES - blocks)))
     (payload,) = local_call(project_kernel, "project", proj_tiles, [rhs], [note], [note_shape])
     gathered, (edge, cube_tables, filters) = gather_pieces(payload, late)
     tables = (*cube_tables, (*first, filters, *last, edge))
-    base = base_of(rhs, gathered)
     all_cubes = jnp.concatenate([half[:, blocks, :blocks] for half in gathered], axis=0)
     places = cube_places(all_cubes.astype(jnp.int32).reshape(members * blocks), extent)
     image_one, payload = local_call(
         complete_kernel,
         "complete",
         proj_tiles,
-        [far(places, gathered), base, rhs],
+        [*far(places, gathered, rhs), rhs],
         [],
         [(blocks, 64), note_shape],
     )
     gathered, _ = gather_pieces(payload, ())
-    base = base_of(image_one, gathered)
     sums = sum(jnp.sum(half[:, blocks, :], axis=0, keepdims=True) for half in gathered)
     image, weights = local_call(
         close_kernel,
         "close",
         proj_tiles,
-        [far(places, gathered), base, rhs, image_one],
+        [*far(places, gathered, image_one), rhs, image_one],
         [sums],
         [(blocks, 64), (NOTE_ROWS, LANES)],
     )

time: 193 us -> 189 us (0.979)
  waiting for transfers between devices: 41.5 us -> 34.6 us
  starting transfers between devices: 23.7 us -> 26.6 us
    ppermute x16 -> x20, waiting for transfers between devices: 41.5 us -> 34.6 us  [exchange(): return lax.ppermute(value, 'px', [(i, i ^ step) for i in range(members)])]
    ppermute x16 -> x20, starting transfers between devices: 23.7 us -> 26.6 us  [exchange(): return lax.ppermute(value, 'px', [(i, i ^ step) for i in range(members)])]
  transfers between devices with their start and end apart: 16 -> 20, of which waited for: 14 -> 16; matrix products, arithmetic and copies ran while one was open for 8% -> 8% of each run, Pallas kernels for 4% -> 5%
where the time goes in v5:
time: 189 us
  Pallas kernels  84.3 us (45%)
  waiting for transfers between devices  34.6 us (18%)
  starting transfers between devices  26.6 us (14%)
  other arithmetic  15.9 us (8%)
  blocking collectives  13.1 us (7%)
  local copies, waits for them, and re-layouts  12.8 us (7%)
    pallas_call x2, Pallas kernels, spectral(): pl.pallas_call(functools.partial(spectral_kernel, extent, chunk, len(oper...  66.7 us
    ppermute x20, waiting for transfers between devices, exchange(): return lax.ppermute(value, 'px', [(i, i ^ step) for i in range(members)])  34.6 us
    ppermute x20, starting transfers between devices, exchange(): return lax.ppermute(value, 'px', [(i, i ^ step) for i in range(members)])  26.6 us
    all_to_all x1, blocking collectives, total(): return jnp.sum(lax.all_to_all(copies, 'px', 0, 0), axis=0)  13.1 us
    unnamed x36, local copies, waits for them, and re-layouts  7.83 us
    pallas_call x3, Pallas kernels, local_call(): pl.pallas_call(kernel, grid=(blocks // STEP_BLOCKS,), out_shape=[jax.Shap...  7.06 us
    reduce_sum x2, other arithmetic, base_of(): jnp.sum(near_tiles * sources[:, None, :], axis=2)  7 us
    pallas_call x1, Pallas kernels, spectral_tables(): pl.pallas_call(functools.partial(filter_kernel, extent, slab), grid=(exte...  6.55 us
  transfers between devices with their start and end apart: 20, of which 16 were waited for; matrix products, arithmetic and copies ran while one was open for 8% of the time, Pallas kernels for 5%

profile of v5, /device:TPU:0, one launch (start us, length us, event | category | flops | bytes accessed | tf_op | source)
XLA Modules:
  0.0 188.7 jit_solution(8634545997188738203)
XLA Ops:
  0.6 0.8 reshape.203.values_ref.rhs_ref
  2.2 2.2 %copy-done = f32[128,64,128]{2,1,0:T(8,128)S(1)} copy-done((f32[128,64,128]{2,1,0:T(8,128)S(1)}, f32[128,64,128]{2,1,0:T(8,128)}, u32[]{:S(2)}) %copy-start) | copy-done | bytes 4194328
  4.4 1.5 project.1
  5.9 4.1 %collective-permute-start = (f32[1,168,128]{2,0,1:T(1,128)S(1)}, f32[1,168,128]{2,0,1:T(1,128)S(1)}, u32[]{:S(2)}, u32[]{:S(2)}) collective-permute-start(f32[1,168,128]{2,0,1:T(1,128)S(1)} %bitcast.72), channel_id=1, source_target_pairs={{0,8},{1,9},{2,10},{3,11},{4,12},{5,13},{6,14},{7,15},{8,0},{9,1},... | collective-permute-start | bytes 258056 | tf_op jit(solution)/shard_map/ppermute | solution.py:33
  10.0 1.3 slice.99
  11.3 0.8 fusion.5.refs_17_
  12.1 2.3 %collective-permute-done = f32[1,168,128]{2,0,1:T(1,128)S(1)} collective-permute-done((f32[1,168,128]{2,0,1:T(1,128)S(1)}, f32[1,168,128]{2,0,1:T(1,128)S(1)}, u32[]{:S(2)}, u32[]{:S(2)}) %collective-permute-start) | collective-permute-done | bytes 86048 | tf_op jit(solution)/shard_map/ppermute | solution.py:33
  14.5 0.8 collective-permute-start.1
  15.9 2.1 %tables.1 = (bf16[384,512]{1,0:T(8,128)(2,1)}, bf16[1536,128]{1,0:T(8,128)(2,1)}, bf16[64,256]{1,0:T(8,128)(2,1)}) custom-call(s32[2]{0:T(128)} %pad_add_fusion.place_ref), custom_call_target="tpu_custom_call" | custom-call | bytes 8388608 | tf_op jit(solution)/shard_map/tables/pallas_call | solution.py:465
  17.9 2.0 %collective-permute-done.1 = f32[2,168,128]{2,0,1:T(2,128)S(1)} collective-permute-done((f32[2,168,128]{2,0,1:T(2,128)S(1)}, f32[2,168,128]{2,0,1:T(2,128)S(1)}, u32[]{:S(2)}, u32[]{:S(2)}) %collective-permute-start.1) | collective-permute-done | bytes 172064 | tf_op jit(solution)/shard_map/ppermute | solution.py:33
  20.1 1.7 collective-permute-start.2
  21.8 2.2 %copy-done.4 = f32[256,16,256]{2,1,0:T(8,128)S(1)} copy-done((f32[256,16,256]{2,1,0:T(8,128)S(1)}, f32[256,16,256]{2,1,0:T(8,128)}, u32[]{:S(2)}) %copy-start.4) | copy-done | bytes 4194328
  24.6 6.5 %filters.1.refs_12_ = f32[16,256,128]{2,1,0:T(8,128)S(1)} custom-call(s32[2]{0:T(128)S(1)} %copy-done.10, f32[4096,256]{1,0:T(8,128)S(1)} %bitcast.67, bf16[768,256]{1,0:T(8,128)(2,1)S(1)} %copy-done.7), custom_call_target="tpu_custom_call" | custom-call | flops 1610612736 | bytes 8388608 | tf_op jit(solution)/shard_map/filters/pallas_call | solution.py:481
  31.2 1.3 copy-done.3
  33.1 1.9 %collective-permute-done.3.refs_1_ = f32[8,168,128]{2,1,0:T(8,128)S(1)} collective-permute-done((f32[8,168,128]{2,1,0:T(8,128)S(1)}, f32[8,168,128]{2,1,0:T(8,128)S(1)}, u32[]{:S(2)}, u32[]{:S(2)}) %collective-permute-start.3) | collective-permute-done | bytes 688160 | tf_op jit(solution)/shard_map/ppermute | solution.py:33
  36.6 33.3 %spectral.2 = (f32[2,8,64,128]{3,2,1,0:T(8,128)}, f32[2,8,64,128]{3,2,1,0:T(8,128)}) custom-call(s32[2048]{0:T(1024)} %fusion.13.rows_ref, s32[8,2048]{1,0:T(8,128)} %stack.22.codes_ref, f32[8,168,128]{2,1,0:T(8,128)} %copy-done.12, f32[8,168,128]{2,1,0:T(8,128)} %copy-done.13, bf16[384,512]{1,0:T(8,128)(2,1)} %get-tuple-element.35.refs_2_, ...), custom_call_target="tpu_custom_call" | custom-call | tf_op jit(solution)/shard_map/spectral/pallas_call | solution.py:531
  70.4 0.9 select_bitcast_fusion.3
  72.1 1.1 fusion.2
  73.2 1.4 collective-permute-start.7
  76.0 3.5 %multiply_reduce_fusion.1 = f32[128,64]{1,0:T(8,128)S(1)} fusion(f32[128,64,128]{2,1,0:T(8,128)} %param.27, f32[128,128]{1,0:T(8,128)S(1)} %mul.61), kind=kLoop, calls=%fused_computation.3 | loop fusion | flops 2088960 | bytes 4292608 | tf_op jit(solution)/shard_map/reduce_sum | solution.py:723
  79.6 1.5 collective-permute-start.8
  81.9 2.0 %collective-permute-done.8 = f32[2,64,128]{2,1,0:T(8,128)S(1)} collective-permute-done((f32[2,64,128]{2,1,0:T(8,128)S(1)}, f32[2,64,128]{2,1,0:T(8,128)S(1)}, u32[]{:S(2)}, u32[]{:S(2)}) %collective-permute-start.8) | collective-permute-done | bytes 65568 | tf_op jit(solution)/shard_map/ppermute | solution.py:33
  83.9 1.6 collective-permute-done.6
  85.5 3.9 %collective-permute-start.9 = (f32[1,128,128]{2,1,0:T(8,128)S(1)}, f32[1,128,128]{2,1,0:T(8,128)S(1)}, u32[]{:S(2)}, u32[]{:S(2)}) collective-permute-start(f32[1,128,128]{2,1,0:T(8,128)S(1)} %pad_maximum_fusion.9), channel_id=1, source_target_pairs={{0,8},{1,9},{2,10},{3,11},{4,12},{5,13},{6,14},{7,15},{8,0},{9,1},... | collective-permute-start | bytes 196616 | tf_op jit(solution)/shard_map/ppermute | solution.py:33
  89.4 2.3 %collective-permute-done.9 = f32[1,128,128]{2,1,0:T(8,128)S(1)} collective-permute-done((f32[1,128,128]{2,1,0:T(8,128)S(1)}, f32[1,128,128]{2,1,0:T(8,128)S(1)}, u32[]{:S(2)}, u32[]{:S(2)}) %collective-permute-start.9) | collective-permute-done | bytes 65568 | tf_op jit(solution)/shard_map/ppermute | solution.py:33
  91.7 3.2 %complete.1 = (f32[128,64]{1,0:T(8,128)S(1)}, f32[168,128]{1,0:T(8,128)S(1)}) custom-call(f32[128,64,128]{2,1,0:T(8,128)S(1)} %copy-done.1, f32[128,128]{1,0:T(8,128)S(1)} %fusion.11.picked_ref, f32[128,64]{1,0:T(8,128)S(1)} %multiply_add_fusion.1.base_ref, f32[128,64]{1,0:T(8,128)S(1)} %reshape.203.values_ref.rhs_ref), custom_call_target="tpu_custom_call" | custom-call | flops 4194304 | bytes 4194304 | tf_op jit(solution)/shard_map/complete/pallas_call | solution.py:672
  94.9 3.0 %collective-permute-start.10 = (f32[1,168,128]{2,1,0:T(8,128)S(1)}, f32[1,168,128]{2,1,0:T(8,128)S(1)}, u32[]{:S(2)}, u32[]{:S(2)}) collective-permute-start(f32[1,168,128]{2,1,0:T(8,128)S(1)} %bitcast.68), channel_id=1, source_target_pairs={{0,8},{1,9},{2,10},{3,11},{4,12},{5,13},{6,14},{7,15},{8,0},{9,1},... | collective-permute-start | bytes 258056 | tf_op jit(solution)/shard_map/ppermute | solution.py:33
  97.8 2.8 %collective-permute-done.10 = f32[1,168,128]{2,1,0:T(8,128)S(1)} collective-permute-done((f32[1,168,128]{2,1,0:T(8,128)S(1)}, f32[1,168,128]{2,1,0:T(8,128)S(1)}, u32[]{:S(2)}, u32[]{:S(2)}) %collective-permute-start.10) | collective-permute-done | bytes 86048 | tf_op jit(solution)/shard_map/ppermute | solution.py:33
  100.7 5.4 %collective-permute-done.11 = f32[2,168,128]{2,1,0:T(8,128)S(1)} collective-permute-done((f32[2,168,128]{2,1,0:T(8,128)S(1)}, f32[2,168,128]{2,1,0:T(8,128)S(1)}, u32[]{:S(2)}, u32[]{:S(2)}) %collective-permute-start.11) | collective-permute-done | bytes 172064 | tf_op jit(solution)/shard_map/ppermute | solution.py:33
  106.2 0.9 collective-permute-start.12
  107.0 6.4 %collective-permute-done.12 = f32[4,168,128]{2,1,0:T(8,128)S(1)} collective-permute-done((f32[4,168,128]{2,1,0:T(8,128)S(1)}, f32[4,168,128]{2,1,0:T(8,128)S(1)}, u32[]{:S(2)}, u32[]{:S(2)}) %collective-permute-start.12) | collective-permute-done | bytes 344096 | tf_op jit(solution)/shard_map/ppermute | solution.py:33
  113.6 2.1 %collective-permute-done.13.refs_1_ = f32[8,168,128]{2,1,0:T(8,128)S(1)} collective-permute-done((f32[8,168,128]{2,1,0:T(8,128)S(1)}, f32[8,168,128]{2,1,0:T(8,128)S(1)}, u32[]{:S(2)}, u32[]{:S(2)}) %collective-permute-start.13) | collective-permute-done | bytes 688160 | tf_op jit(solution)/shard_map/ppermute | solution.py:33
  115.7 0.8 copy-done.14
  116.6 33.4 %spectral.3 = (f32[2,8,64,128]{3,2,1,0:T(8,128)}, f32[2,8,64,128]{3,2,1,0:T(8,128)}) custom-call(s32[2048]{0:T(1024)} %fusion.13.rows_ref, s32[8,2048]{1,0:T(8,128)} %stack.22.codes_ref, f32[8,168,128]{2,1,0:T(8,128)} %copy-done.11, f32[8,168,128]{2,1,0:T(8,128)} %copy-done.14, bf16[384,512]{1,0:T(8,128)(2,1)} %get-tuple-element.35.refs_2_, ...), custom_call_target="tpu_custom_call" | custom-call | tf_op jit(solution)/shard_map/spectral/pallas_call | solution.py:531
  150.2 0.9 select_bitcast_fusion.1
  151.1 0.8 slice_reduce_fusion
  152.2 1.1 fusion
  153.4 0.9 collective-permute-start.15
  155.1 3.5 %multiply_reduce_fusion = f32[128,64]{1,0:T(8,128)S(1)} fusion(f32[128,64,128]{2,1,0:T(8,128)} %param.27, f32[128,128]{1,0:T(8,128)S(1)} %mul.65), kind=kLoop, calls=%fused_computation.2 | loop fusion | flops 2088960 | bytes 4292608 | tf_op jit(solution)/shard_map/reduce_sum | solution.py:723
  159.0 1.0 collective-permute-start.18
  160.0 2.1 %collective-permute-start.16 = (f32[2,64,128]{2,1,0:T(8,128)S(1)}, f32[2,64,128]{2,1,0:T(8,128)S(1)}, u32[]{:S(2)}, u32[]{:S(2)}) collective-permute-start(f32[2,64,128]{2,1,0:T(8,128)S(1)} %slice.148), channel_id=1, source_target_pairs={{0,4},{1,5},{2,6},{3,7},{4,0},{5,1},{6,2},{7,3},{8,12},{9,13},{10,... | collective-permute-start | bytes 196616 | tf_op jit(solution)/shard_map/ppermute | solution.py:33
  162.1 1.2 collective-permute-done.18
  163.3 1.0 collective-permute-done.16
  164.4 3.4 %collective-permute-start.19 = (f32[1,128,128]{2,1,0:T(8,128)S(1)}, f32[1,128,128]{2,1,0:T(8,128)S(1)}, u32[]{:S(2)}, u32[]{:S(2)}) collective-permute-start(f32[1,128,128]{2,1,0:T(8,128)S(1)} %pad_maximum_fusion.8), channel_id=1, source_target_pairs={{0,8},{1,9},{2,10},{3,11},{4,12},{5,13},{6,14},{7,15},{8,0},{9,1},... | collective-permute-start | bytes 196616 | tf_op jit(solution)/shard_map/ppermute | solution.py:33
  167.8 2.2 %collective-permute-done.19 = f32[1,128,128]{2,1,0:T(8,128)S(1)} collective-permute-done((f32[1,128,128]{2,1,0:T(8,128)S(1)}, f32[1,128,128]{2,1,0:T(8,128)S(1)}, u32[]{:S(2)}, u32[]{:S(2)}) %collective-permute-start.19) | collective-permute-done | bytes 65568 | tf_op jit(solution)/shard_map/ppermute | solution.py:33
  170.1 2.4 %close.1 = (f32[128,64]{1,0:T(8,128)S(1)}, f32[8,128]{1,0:T(8,128)S(1)}) custom-call(f32[128,64,128]{2,1,0:T(8,128)S(1)} %copy-done.2, f32[128,128]{1,0:T(8,128)S(1)} %fusion.8.picked_ref, f32[128,64]{1,0:T(8,128)S(1)} %multiply_add_fusion.base_ref, f32[128,64]{1,0:T(8,128)S(1)} %reshape.203.values_ref.rhs_ref, f32[128,64]{1,0:T(8,128)S(1)} %get-tuple-element.45.first_ref, ...), custom_call_target="tpu_custom_call" | custom-call | flops 4194304 | bytes 4194304 | tf_op jit(solution)/shard_map/close/pallas_call | solution.py:672
  173.1 13.1 %all_to_all.5 = f32[16,8,128]{2,1,0:T(8,128)S(1)} all-to-all(f32[16,8,128]{2,1,0:T(8,128)S(1)} %broadcast_in_dim.39), channel_id=1, replica_groups=mesh['groups'=2,'px'=16] {'px'}, dimensions={0} | all-to-all | bytes 131072 | tf_op jit(solution)/shard_map/all_to_all | solution.py:71
  186.8 1.9 %finish.1 = (f32[64,128]{1,0:T(8,128)}, f32[64,128]{1,0:T(8,128)}) custom-call(f32[128,64]{1,0:T(8,128)} %copy-done.5, f32[128,64]{1,0:T(8,128)} %copy-done.6, f32[128,64]{1,0:T(8,128)} %copy-done.8, f32[1,128]{1,0:T(1,128)} %copy-done.9, f32[8,128]{1,0:T(8,128)} %reduce_sum.49.last_ref), custom_call_target="tpu_custom_call" | custom-call | tf_op jit(solution)/shard_map/finish/pallas_call | solution.py:757
  (102 shorter events, 10.9 us)
Async XLA Ops:
  0.6 10.7 %copy-start.16 = (f32[136]{0:T(256)S(1)}, f32[136]{0:T(256)}, u32[]{:S(2)}) copy-start(f32[136]{0:T(256)} %constant.220.clone) | copy-start | bytes 1636
  1.5 168.6 %copy-start.5 = (f32[128,64]{1,0:T(8,128)}, f32[128,64]{1,0:T(8,128)S(1)}, u32[]{:S(2)}) copy-start(f32[128,64]{1,0:T(8,128)S(1)} %reshape.203.values_ref.rhs_ref) | copy-start | bytes 98308
  2.2 2.2 %copy-start = (f32[128,64,128]{2,1,0:T(8,128)S(1)}, f32[128,64,128]{2,1,0:T(8,128)}, u32[]{:S(2)}) copy-start(f32[128,64,128]{2,1,0:T(8,128)} %proj_ref.5) | copy-start | bytes 12582916
  4.4 17.5 %copy-start.7 = (bf16[768,256]{1,0:T(8,128)(2,1)S(1)}, bf16[768,256]{1,0:T(8,128)(2,1)}, u32[]{:S(2)}) copy-start(bf16[768,256]{1,0:T(8,128)(2,1)} %constant.208.clone.sort_ref) | copy-start | bytes 1179652
  5.9 8.4 %collective-permute-start = (f32[1,168,128]{2,0,1:T(1,128)S(1)}, f32[1,168,128]{2,0,1:T(1,128)S(1)}, u32[]{:S(2)}, u32[]{:S(2)}) collective-permute-start(f32[1,168,128]{2,0,1:T(1,128)S(1)} %bitcast.72), channel_id=1, source_target_pairs={{0,8},{1,9},{2,10},{3,11},{4,12},{5,13},{6,14},{7,15},{8,0},{9,1},... | collective-permute-start | bytes 258056 | tf_op jit(solution)/shard_map/ppermute | solution.py:33
  14.5 5.5 %collective-permute-start.1 = (f32[2,168,128]{2,0,1:T(2,128)S(1)}, f32[2,168,128]{2,0,1:T(2,128)S(1)}, u32[]{:S(2)}, u32[]{:S(2)}) collective-permute-start(f32[2,168,128]{2,0,1:T(2,128)S(1)} %pad_maximum_fusion.4), channel_id=1, source_target_pairs={{0,4},{1,5},{2,6},{3,7},{4,0},{5,1},{6,2},{7,3},{8,12},{9,13},{10,... | collective-permute-start | bytes 516104 | tf_op jit(solution)/shard_map/ppermute | solution.py:33
  20.1 12.4 %collective-permute-start.2 = (f32[4,168,128]{2,0,1:T(4,128)S(1)}, f32[4,168,128]{2,0,1:T(4,128)S(1)}, u32[]{:S(2)}, u32[]{:S(2)}) collective-permute-start(f32[4,168,128]{2,0,1:T(4,128)S(1)} %pad_maximum_fusion.2), channel_id=1, source_target_pairs={{0,2},{1,3},{2,0},{3,1},{4,6},{5,7},{6,4},{7,5},{8,10},{9,11},{10,... | collective-permute-start | bytes 1032200 | tf_op jit(solution)/shard_map/ppermute | solution.py:33
  21.8 2.2 %copy-start.4 = (f32[256,16,256]{2,1,0:T(8,128)S(1)}, f32[256,16,256]{2,1,0:T(8,128)}, u32[]{:S(2)}) copy-start(f32[256,16,256]{2,1,0:T(8,128)} %param.28) | copy-start | bytes 12582916
  24.0 0.6 copy-start.10
  31.2 1.3 copy-start.3
  32.8 3.8 %copy-start.12 = (f32[8,168,128]{2,1,0:T(8,128)}, f32[8,168,128]{2,1,0:T(8,128)S(1)}, u32[]{:S(2)}) copy-start(f32[8,168,128]{2,1,0:T(8,128)S(1)} %copy.31.refs_0_) | copy-start | bytes 2064388
  32.8 2.2 %collective-permute-start.3 = (f32[8,168,128]{2,1,0:T(8,128)S(1)}, f32[8,168,128]{2,1,0:T(8,128)S(1)}, u32[]{:S(2)}, u32[]{:S(2)}) collective-permute-start(f32[8,168,128]{2,1,0:T(8,128)S(1)} %copy.31.refs_0_), channel_id=1, source_target_pairs={{0,1},{1,0},{2,3},{3,2},{4,5},{5,4},{6,7},{7,6},{8,9},{9,8},{10,11... | collective-permute-start | bytes 2064392 | tf_op jit(solution)/shard_map/ppermute | solution.py:33
  35.0 1.5 copy-start.13
  36.6 33.5 %copy-start.17 = (s32[128,2]{0,1:T(2,128)S(1)}, s32[128,2]{0,1:T(2,128)}, u32[]{:S(2)}) copy-start(s32[128,2]{0,1:T(2,128)} %param.26) | copy-start | bytes 3076
  36.6 33.8 %copy-start.15 = (f32[8192]{0:T(1024)S(1)}, f32[8192]{0:T(1024)}, u32[]{:S(2)}) copy-start(f32[8192]{0:T(1024)} %param.22) | copy-start | bytes 98308
  69.9 2.2 %collective-permute-start.4 = (f32[2,8,64,128]{3,2,1,0:T(8,128)}, f32[2,8,64,128]{3,2,1,0:T(8,128)S(1)}, u32[]{:S(2)}, u32[]{:S(2)}) collective-permute-start(f32[2,8,64,128]{3,2,1,0:T(8,128)} %get-tuple-element.41), channel_id=1, source_target_pairs={{0,1},{1,0},{2,3},{3,2},{4,5},{5,4},{6,7},{7,6},{8,9},{9,8},{10,11... | collective-permute-start | bytes 1572872 | tf_op jit(solution)/shard_map/ppermute | solution.py:33
  73.2 6.4 %collective-permute-start.7 = (f32[4,64,128]{2,1,0:T(8,128)S(1)}, f32[4,64,128]{2,1,0:T(8,128)S(1)}, u32[]{:S(2)}, u32[]{:S(2)}) collective-permute-start(f32[4,64,128]{2,1,0:T(8,128)S(1)} %slice.111), channel_id=1, source_target_pairs={{0,4},{1,5},{2,6},{3,7},{4,0},{5,1},{6,2},{7,3},{8,12},{9,13},{10,... | collective-permute-start | bytes 393224 | tf_op jit(solution)/shard_map/ppermute | solution.py:33
  74.6 6.5 %collective-permute-start.5 = (f32[4,64,128]{2,1,0:T(8,128)S(1)}, f32[4,64,128]{2,1,0:T(8,128)S(1)}, u32[]{:S(2)}, u32[]{:S(2)}) collective-permute-start(f32[4,64,128]{2,1,0:T(8,128)S(1)} %slice.107), channel_id=1, source_target_pairs={{0,2},{1,3},{2,0},{3,1},{4,6},{5,7},{6,4},{7,5},{8,10},{9,11},{10,... | collective-permute-start | bytes 393224 | tf_op jit(solution)/shard_map/ppermute | solution.py:33
  76.0 15.6 %copy-start.1 = (f32[128,64,128]{2,1,0:T(8,128)S(1)}, f32[128,64,128]{2,1,0:T(8,128)}, u32[]{:S(2)}) copy-start(f32[128,64,128]{2,1,0:T(8,128)} %proj_ref.5) | copy-start | bytes 12582916
  79.6 4.3 %collective-permute-start.8 = (f32[2,64,128]{2,1,0:T(8,128)S(1)}, f32[2,64,128]{2,1,0:T(8,128)S(1)}, u32[]{:S(2)}, u32[]{:S(2)}) collective-permute-start(f32[2,64,128]{2,1,0:T(8,128)S(1)} %slice.142), channel_id=1, source_target_pairs={{0,2},{1,3},{2,0},{3,1},{4,6},{5,7},{6,4},{7,5},{8,10},{9,11},{10,... | collective-permute-start | bytes 196616 | tf_op jit(solution)/shard_map/ppermute | solution.py:33
  81.2 4.3 %collective-permute-start.6 = (f32[2,64,128]{2,1,0:T(8,128)S(1)}, f32[2,64,128]{2,1,0:T(8,128)S(1)}, u32[]{:S(2)}, u32[]{:S(2)}) collective-permute-start(f32[2,64,128]{2,1,0:T(8,128)S(1)} %slice.140), channel_id=1, source_target_pairs={{0,4},{1,5},{2,6},{3,7},{4,0},{5,1},{6,2},{7,3},{8,12},{9,13},{10,... | collective-permute-start | bytes 196616 | tf_op jit(solution)/shard_map/ppermute | solution.py:33
  85.5 6.1 %collective-permute-start.9 = (f32[1,128,128]{2,1,0:T(8,128)S(1)}, f32[1,128,128]{2,1,0:T(8,128)S(1)}, u32[]{:S(2)}, u32[]{:S(2)}) collective-permute-start(f32[1,128,128]{2,1,0:T(8,128)S(1)} %pad_maximum_fusion.9), channel_id=1, source_target_pairs={{0,8},{1,9},{2,10},{3,11},{4,12},{5,13},{6,14},{7,15},{8,0},{9,1},... | collective-permute-start | bytes 196616 | tf_op jit(solution)/shard_map/ppermute | solution.py:33
  94.9 75.2 %copy-start.6 = (f32[128,64]{1,0:T(8,128)}, f32[128,64]{1,0:T(8,128)S(1)}, u32[]{:S(2)}) copy-start(f32[128,64]{1,0:T(8,128)S(1)} %get-tuple-element.45.first_ref) | copy-start | bytes 98308
  94.9 5.8 %collective-permute-start.10 = (f32[1,168,128]{2,1,0:T(8,128)S(1)}, f32[1,168,128]{2,1,0:T(8,128)S(1)}, u32[]{:S(2)}, u32[]{:S(2)}) collective-permute-start(f32[1,168,128]{2,1,0:T(8,128)S(1)} %bitcast.68), channel_id=1, source_target_pairs={{0,8},{1,9},{2,10},{3,11},{4,12},{5,13},{6,14},{7,15},{8,0},{9,1},... | collective-permute-start | bytes 258056 | tf_op jit(solution)/shard_map/ppermute | solution.py:33
  100.7 5.5 %collective-permute-start.11 = (f32[2,168,128]{2,1,0:T(8,128)S(1)}, f32[2,168,128]{2,1,0:T(8,128)S(1)}, u32[]{:S(2)}, u32[]{:S(2)}) collective-permute-start(f32[2,168,128]{2,1,0:T(8,128)S(1)} %pad_maximum_fusion.5), channel_id=1, source_target_pairs={{0,4},{1,5},{2,6},{3,7},{4,0},{5,1},{6,2},{7,3},{8,12},{9,13},{10,... | collective-permute-start | bytes 516104 | tf_op jit(solution)/shard_map/ppermute | solution.py:33
  106.2 7.3 %collective-permute-start.12 = (f32[4,168,128]{2,1,0:T(8,128)S(1)}, f32[4,168,128]{2,1,0:T(8,128)S(1)}, u32[]{:S(2)}, u32[]{:S(2)}) collective-permute-start(f32[4,168,128]{2,1,0:T(8,128)S(1)} %pad_maximum_fusion.3), channel_id=1, source_target_pairs={{0,2},{1,3},{2,0},{3,1},{4,6},{5,7},{6,4},{7,5},{8,10},{9,11},{10,... | collective-permute-start | bytes 1032200 | tf_op jit(solution)/shard_map/ppermute | solution.py:33
  113.5 2.2 %copy-start.11 = (f32[8,168,128]{2,1,0:T(8,128)}, f32[8,168,128]{2,1,0:T(8,128)S(1)}, u32[]{:S(2)}) copy-start(f32[8,168,128]{2,1,0:T(8,128)S(1)} %pad_maximum_fusion.1.refs_0_) | copy-start | bytes 2064388
  113.5 2.2 %collective-permute-start.13 = (f32[8,168,128]{2,1,0:T(8,128)S(1)}, f32[8,168,128]{2,1,0:T(8,128)S(1)}, u32[]{:S(2)}, u32[]{:S(2)}) collective-permute-start(f32[8,168,128]{2,1,0:T(8,128)S(1)} %pad_maximum_fusion.1.refs_0_), channel_id=1, source_target_pairs={{0,1},{1,0},{2,3},{3,2},{4,5},{5,4},{6,7},{7,6},{8,9},{9,8},{10,11... | collective-permute-start | bytes 2064392 | tf_op jit(solution)/shard_map/ppermute | solution.py:33
  115.7 0.9 copy-start.14
  150.0 2.2 %collective-permute-start.14 = (f32[2,8,64,128]{3,2,1,0:T(8,128)}, f32[2,8,64,128]{3,2,1,0:T(8,128)S(1)}, u32[]{:S(2)}, u32[]{:S(2)}) collective-permute-start(f32[2,8,64,128]{3,2,1,0:T(8,128)} %get-tuple-element.48), channel_id=1, source_target_pairs={{0,1},{1,0},{2,3},{3,2},{4,5},{5,4},{6,7},{7,6},{8,9},{9,8},{10,11... | collective-permute-start | bytes 1572872 | tf_op jit(solution)/shard_map/ppermute | solution.py:33
  151.9 18.2 %copy-start.9 = (f32[1,128]{1,0:T(1,128)}, f32[1,128]{1,0:T(1,128)S(1)}, u32[]{:S(2)}) copy-start(f32[1,128]{1,0:T(1,128)S(1)} %add_bitcast_fusion.sums_ref) | copy-start | bytes 1540
  153.3 5.6 %collective-permute-start.17 = (f32[4,64,128]{2,1,0:T(8,128)S(1)}, f32[4,64,128]{2,1,0:T(8,128)S(1)}, u32[]{:S(2)}, u32[]{:S(2)}) collective-permute-start(f32[4,64,128]{2,1,0:T(8,128)S(1)} %slice.125), channel_id=1, source_target_pairs={{0,4},{1,5},{2,6},{3,7},{4,0},{5,1},{6,2},{7,3},{8,12},{9,13},{10,... | collective-permute-start | bytes 393224 | tf_op jit(solution)/shard_map/ppermute | solution.py:33
  153.4 6.6 %collective-permute-start.15 = (f32[4,64,128]{2,1,0:T(8,128)S(1)}, f32[4,64,128]{2,1,0:T(8,128)S(1)}, u32[]{:S(2)}, u32[]{:S(2)}) collective-permute-start(f32[4,64,128]{2,1,0:T(8,128)S(1)} %slice.121), channel_id=1, source_target_pairs={{0,2},{1,3},{2,0},{3,1},{4,6},{5,7},{6,4},{7,5},{8,10},{9,11},{10,... | collective-permute-start | bytes 393224 | tf_op jit(solution)/shard_map/ppermute | solution.py:33
  155.1 15.0 %copy-start.2 = (f32[128,64,128]{2,1,0:T(8,128)S(1)}, f32[128,64,128]{2,1,0:T(8,128)}, u32[]{:S(2)}) copy-start(f32[128,64,128]{2,1,0:T(8,128)} %proj_ref.5) | copy-start | bytes 12582916
  159.0 4.3 %collective-permute-start.18 = (f32[2,64,128]{2,1,0:T(8,128)S(1)}, f32[2,64,128]{2,1,0:T(8,128)S(1)}, u32[]{:S(2)}, u32[]{:S(2)}) collective-permute-start(f32[2,64,128]{2,1,0:T(8,128)S(1)} %slice.150), channel_id=1, source_target_pairs={{0,2},{1,3},{2,0},{3,1},{4,6},{5,7},{6,4},{7,5},{8,10},{9,11},{10,... | collective-permute-start | bytes 196616 | tf_op jit(solution)/shard_map/ppermute | solution.py:33
  160.0 4.3 %collective-permute-start.16 = (f32[2,64,128]{2,1,0:T(8,128)S(1)}, f32[2,64,128]{2,1,0:T(8,128)S(1)}, u32[]{:S(2)}, u32[]{:S(2)}) collective-permute-start(f32[2,64,128]{2,1,0:T(8,128)S(1)} %slice.148), channel_id=1, source_target_pairs={{0,4},{1,5},{2,6},{3,7},{4,0},{5,1},{6,2},{7,3},{8,12},{9,13},{10,... | collective-permute-start | bytes 196616 | tf_op jit(solution)/shard_map/ppermute | solution.py:33
  164.4 5.7 %collective-permute-start.19 = (f32[1,128,128]{2,1,0:T(8,128)S(1)}, f32[1,128,128]{2,1,0:T(8,128)S(1)}, u32[]{:S(2)}, u32[]{:S(2)}) collective-permute-start(f32[1,128,128]{2,1,0:T(8,128)S(1)} %pad_maximum_fusion.8), channel_id=1, source_target_pairs={{0,8},{1,9},{2,10},{3,11},{4,12},{5,13},{6,14},{7,15},{8,0},{9,1},... | collective-permute-start | bytes 196616 | tf_op jit(solution)/shard_map/ppermute | solution.py:33
  172.5 0.6 copy-start.8

commit v6 on v5

--- a/solution.py
+++ b/solution.py
@@ -189,7 +189,7 @@
                     ref[pl.ds(row, 1), :] += source[pl.ds(place, 1), :]
             return 0
 
-        lax.fori_loop(0, chunk // COPIES, add, 0, unroll=8)
+        lax.fori_loop(0, chunk // COPIES, add, 0, unroll=16)
         return 0
 
     for move in early:
@@ -221,7 +221,7 @@
                 grid_imag[place, :] = j
             return 0
 
-        lax.fori_loop(0, extent // 8, body, 0)
+        lax.fori_loop(0, extent // 8, body, 0, unroll=2)
 
     across(-1)
     for move in moves[4:]:
@@ -310,7 +310,7 @@
                 ref[pl.ds(i, 1), :] = source[pl.ds(row, 1), :]
             return 0
 
-        lax.fori_loop(0, chunk, take, 0, unroll=16)
+        lax.fori_loop(0, chunk, take, 0, unroll=32)
         codes, wide, cosine, sine = marks(start)
         plane = where_equal(wide, codes[:, 0:1])
         high, low = split(dense[...])

time: 189 us -> 188 us (level)
  no operation moved by 1% of the time
where the time goes in v6:
time: 188 us; the launch traced here: 187 us
  Pallas kernels  82.8 us (44%)
  waiting for transfers between devices  34.6 us (18%)
  starting transfers between devices  26.7 us (14%)
  other arithmetic  15.9 us (8%)
  blocking collectives  13.1 us (7%)
  local copies, waits for them, and re-layouts  12.8 us (7%)
    pallas_call x2, Pallas kernels, spectral(): pl.pallas_call(functools.partial(spectral_kernel, extent, chunk, len(oper...  65.3 us
    ppermute x20, waiting for transfers between devices, exchange(): return lax.ppermute(value, 'px', [(i, i ^ step) for i in range(members)])  34.6 us
    ppermute x20, starting transfers between devices, exchange(): return lax.ppermute(value, 'px', [(i, i ^ step) for i in range(members)])  26.7 us
    all_to_all x1, blocking collectives, total(): return jnp.sum(lax.all_to_all(copies, 'px', 0, 0), axis=0)  13.1 us
    unnamed x36, local copies, waits for them, and re-layouts  7.83 us
    pallas_call x3, Pallas kernels, local_call(): pl.pallas_call(kernel, grid=(blocks // STEP_BLOCKS,), out_shape=[jax.Shap...  7.06 us
    reduce_sum x2, other arithmetic, base_of(): jnp.sum(near_tiles * sources[:, None, :], axis=2)  7 us
    pallas_call x1, Pallas kernels, spectral_tables(): pl.pallas_call(functools.partial(filter_kernel, extent, slab), grid=(exte...  6.55 us
  transfers between devices with their start and end apart: 20, of which 16 were waited for; matrix products, arithmetic and copies ran while one was open for 8% of the time, Pallas kernels for 5%

profile of v6, /device:TPU:0, one launch (start us, length us, event | category | flops | bytes accessed | tf_op | source)
XLA Modules:
  0.0 187.3 jit_solution(14024472869450070837)
XLA Ops:
  0.6 0.8 reshape.203.values_ref.rhs_ref
  2.2 2.2 %copy-done = f32[128,64,128]{2,1,0:T(8,128)S(1)} copy-done((f32[128,64,128]{2,1,0:T(8,128)S(1)}, f32[128,64,128]{2,1,0:T(8,128)}, u32[]{:S(2)}) %copy-start) | copy-done | bytes 4194328
  4.4 1.5 project.1
  5.9 4.1 %collective-permute-start = (f32[1,168,128]{2,0,1:T(1,128)S(1)}, f32[1,168,128]{2,0,1:T(1,128)S(1)}, u32[]{:S(2)}, u32[]{:S(2)}) collective-permute-start(f32[1,168,128]{2,0,1:T(1,128)S(1)} %bitcast.72), channel_id=1, source_target_pairs={{0,8},{1,9},{2,10},{3,11},{4,12},{5,13},{6,14},{7,15},{8,0},{9,1},... | collective-permute-start | bytes 258056 | tf_op jit(solution)/shard_map/ppermute | solution.py:33
  10.0 1.3 slice.99
  11.3 0.8 fusion.5.refs_17_
  12.1 2.3 %collective-permute-done = f32[1,168,128]{2,0,1:T(1,128)S(1)} collective-permute-done((f32[1,168,128]{2,0,1:T(1,128)S(1)}, f32[1,168,128]{2,0,1:T(1,128)S(1)}, u32[]{:S(2)}, u32[]{:S(2)}) %collective-permute-start) | collective-permute-done | bytes 86048 | tf_op jit(solution)/shard_map/ppermute | solution.py:33
  14.5 0.8 collective-permute-start.1
  15.9 2.1 %tables.1 = (bf16[384,512]{1,0:T(8,128)(2,1)}, bf16[1536,128]{1,0:T(8,128)(2,1)}, bf16[64,256]{1,0:T(8,128)(2,1)}) custom-call(s32[2]{0:T(128)} %pad_add_fusion.place_ref), custom_call_target="tpu_custom_call" | custom-call | bytes 8388608 | tf_op jit(solution)/shard_map/tables/pallas_call | solution.py:465
  17.9 2.0 %collective-permute-done.1 = f32[2,168,128]{2,0,1:T(2,128)S(1)} collective-permute-done((f32[2,168,128]{2,0,1:T(2,128)S(1)}, f32[2,168,128]{2,0,1:T(2,128)S(1)}, u32[]{:S(2)}, u32[]{:S(2)}) %collective-permute-start.1) | collective-permute-done | bytes 172064 | tf_op jit(solution)/shard_map/ppermute | solution.py:33
  20.1 1.7 collective-permute-start.2
  21.8 2.2 %copy-done.4 = f32[256,16,256]{2,1,0:T(8,128)S(1)} copy-done((f32[256,16,256]{2,1,0:T(8,128)S(1)}, f32[256,16,256]{2,1,0:T(8,128)}, u32[]{:S(2)}) %copy-start.4) | copy-done | bytes 4194328
  24.6 6.5 %filters.1.refs_12_ = f32[16,256,128]{2,1,0:T(8,128)S(1)} custom-call(s32[2]{0:T(128)S(1)} %copy-done.10, f32[4096,256]{1,0:T(8,128)S(1)} %bitcast.67, bf16[768,256]{1,0:T(8,128)(2,1)S(1)} %copy-done.7), custom_call_target="tpu_custom_call" | custom-call | flops 1610612736 | bytes 8388608 | tf_op jit(solution)/shard_map/filters/pallas_call | solution.py:481
  31.2 1.3 copy-done.3
  33.1 1.9 %collective-permute-done.3.refs_1_ = f32[8,168,128]{2,1,0:T(8,128)S(1)} collective-permute-done((f32[8,168,128]{2,1,0:T(8,128)S(1)}, f32[8,168,128]{2,1,0:T(8,128)S(1)}, u32[]{:S(2)}, u32[]{:S(2)}) %collective-permute-start.3) | collective-permute-done | bytes 688160 | tf_op jit(solution)/shard_map/ppermute | solution.py:33
  36.6 32.7 %spectral.2 = (f32[2,8,64,128]{3,2,1,0:T(8,128)}, f32[2,8,64,128]{3,2,1,0:T(8,128)}) custom-call(s32[2048]{0:T(1024)} %fusion.13.rows_ref, s32[8,2048]{1,0:T(8,128)} %stack.22.codes_ref, f32[8,168,128]{2,1,0:T(8,128)} %copy-done.12, f32[8,168,128]{2,1,0:T(8,128)} %copy-done.13, bf16[384,512]{1,0:T(8,128)(2,1)} %get-tuple-element.35.refs_2_, ...), custom_call_target="tpu_custom_call" | custom-call | tf_op jit(solution)/shard_map/spectral/pallas_call | solution.py:531
  69.8 0.9 select_bitcast_fusion.3
  71.4 1.1 fusion.2
  72.6 1.4 collective-permute-start.7
  75.4 3.5 %multiply_reduce_fusion.1 = f32[128,64]{1,0:T(8,128)S(1)} fusion(f32[128,64,128]{2,1,0:T(8,128)} %param.27, f32[128,128]{1,0:T(8,128)S(1)} %mul.61), kind=kLoop, calls=%fused_computation.3 | loop fusion | flops 2088960 | bytes 4292608 | tf_op jit(solution)/shard_map/reduce_sum | solution.py:723
  79.0 1.5 collective-permute-start.8
  81.3 2.0 %collective-permute-done.8 = f32[2,64,128]{2,1,0:T(8,128)S(1)} collective-permute-done((f32[2,64,128]{2,1,0:T(8,128)S(1)}, f32[2,64,128]{2,1,0:T(8,128)S(1)}, u32[]{:S(2)}, u32[]{:S(2)}) %collective-permute-start.8) | collective-permute-done | bytes 65568 | tf_op jit(solution)/shard_map/ppermute | solution.py:33
  83.3 1.6 collective-permute-done.6
  84.9 3.9 %collective-permute-start.9 = (f32[1,128,128]{2,1,0:T(8,128)S(1)}, f32[1,128,128]{2,1,0:T(8,128)S(1)}, u32[]{:S(2)}, u32[]{:S(2)}) collective-permute-start(f32[1,128,128]{2,1,0:T(8,128)S(1)} %pad_maximum_fusion.9), channel_id=1, source_target_pairs={{0,8},{1,9},{2,10},{3,11},{4,12},{5,13},{6,14},{7,15},{8,0},{9,1},... | collective-permute-start | bytes 196616 | tf_op jit(solution)/shard_map/ppermute | solution.py:33
  88.8 2.3 %collective-permute-done.9 = f32[1,128,128]{2,1,0:T(8,128)S(1)} collective-permute-done((f32[1,128,128]{2,1,0:T(8,128)S(1)}, f32[1,128,128]{2,1,0:T(8,128)S(1)}, u32[]{:S(2)}, u32[]{:S(2)}) %collective-permute-start.9) | collective-permute-done | bytes 65568 | tf_op jit(solution)/shard_map/ppermute | solution.py:33
  91.1 3.2 %complete.1 = (f32[128,64]{1,0:T(8,128)S(1)}, f32[168,128]{1,0:T(8,128)S(1)}) custom-call(f32[128,64,128]{2,1,0:T(8,128)S(1)} %copy-done.1, f32[128,128]{1,0:T(8,128)S(1)} %fusion.11.picked_ref, f32[128,64]{1,0:T(8,128)S(1)} %multiply_add_fusion.1.base_ref, f32[128,64]{1,0:T(8,128)S(1)} %reshape.203.values_ref.rhs_ref), custom_call_target="tpu_custom_call" | custom-call | flops 4194304 | bytes 4194304 | tf_op jit(solution)/shard_map/complete/pallas_call | solution.py:672
  94.2 3.0 %collective-permute-start.10 = (f32[1,168,128]{2,1,0:T(8,128)S(1)}, f32[1,168,128]{2,1,0:T(8,128)S(1)}, u32[]{:S(2)}, u32[]{:S(2)}) collective-permute-start(f32[1,168,128]{2,1,0:T(8,128)S(1)} %bitcast.68), channel_id=1, source_target_pairs={{0,8},{1,9},{2,10},{3,11},{4,12},{5,13},{6,14},{7,15},{8,0},{9,1},... | collective-permute-start | bytes 258056 | tf_op jit(solution)/shard_map/ppermute | solution.py:33
  97.2 2.8 %collective-permute-done.10 = f32[1,168,128]{2,1,0:T(8,128)S(1)} collective-permute-done((f32[1,168,128]{2,1,0:T(8,128)S(1)}, f32[1,168,128]{2,1,0:T(8,128)S(1)}, u32[]{:S(2)}, u32[]{:S(2)}) %collective-permute-start.10) | collective-permute-done | bytes 86048 | tf_op jit(solution)/shard_map/ppermute | solution.py:33
  100.1 5.4 %collective-permute-done.11 = f32[2,168,128]{2,1,0:T(8,128)S(1)} collective-permute-done((f32[2,168,128]{2,1,0:T(8,128)S(1)}, f32[2,168,128]{2,1,0:T(8,128)S(1)}, u32[]{:S(2)}, u32[]{:S(2)}) %collective-permute-start.11) | collective-permute-done | bytes 172064 | tf_op jit(solution)/shard_map/ppermute | solution.py:33
  105.5 0.9 collective-permute-start.12
  106.4 6.4 %collective-permute-done.12 = f32[4,168,128]{2,1,0:T(8,128)S(1)} collective-permute-done((f32[4,168,128]{2,1,0:T(8,128)S(1)}, f32[4,168,128]{2,1,0:T(8,128)S(1)}, u32[]{:S(2)}, u32[]{:S(2)}) %collective-permute-start.12) | collective-permute-done | bytes 344096 | tf_op jit(solution)/shard_map/ppermute | solution.py:33
  113.0 2.1 %collective-permute-done.13.refs_1_ = f32[8,168,128]{2,1,0:T(8,128)S(1)} collective-permute-done((f32[8,168,128]{2,1,0:T(8,128)S(1)}, f32[8,168,128]{2,1,0:T(8,128)S(1)}, u32[]{:S(2)}, u32[]{:S(2)}) %collective-permute-start.13) | collective-permute-done | bytes 688160 | tf_op jit(solution)/shard_map/ppermute | solution.py:33
  115.1 0.8 copy-done.14
  116.0 32.6 %spectral.3 = (f32[2,8,64,128]{3,2,1,0:T(8,128)}, f32[2,8,64,128]{3,2,1,0:T(8,128)}) custom-call(s32[2048]{0:T(1024)} %fusion.13.rows_ref, s32[8,2048]{1,0:T(8,128)} %stack.22.codes_ref, f32[8,168,128]{2,1,0:T(8,128)} %copy-done.11, f32[8,168,128]{2,1,0:T(8,128)} %copy-done.14, bf16[384,512]{1,0:T(8,128)(2,1)} %get-tuple-element.35.refs_2_, ...), custom_call_target="tpu_custom_call" | custom-call | tf_op jit(solution)/shard_map/spectral/pallas_call | solution.py:531
  148.8 0.9 select_bitcast_fusion.1
  149.6 0.8 slice_reduce_fusion
  150.8 1.1 fusion
  152.0 0.9 collective-permute-start.15
  153.7 3.5 %multiply_reduce_fusion = f32[128,64]{1,0:T(8,128)S(1)} fusion(f32[128,64,128]{2,1,0:T(8,128)} %param.27, f32[128,128]{1,0:T(8,128)S(1)} %mul.65), kind=kLoop, calls=%fused_computation.2 | loop fusion | flops 2088960 | bytes 4292608 | tf_op jit(solution)/shard_map/reduce_sum | solution.py:723
  157.5 1.0 collective-permute-start.18
  158.6 2.1 %collective-permute-start.16 = (f32[2,64,128]{2,1,0:T(8,128)S(1)}, f32[2,64,128]{2,1,0:T(8,128)S(1)}, u32[]{:S(2)}, u32[]{:S(2)}) collective-permute-start(f32[2,64,128]{2,1,0:T(8,128)S(1)} %slice.148), channel_id=1, source_target_pairs={{0,4},{1,5},{2,6},{3,7},{4,0},{5,1},{6,2},{7,3},{8,12},{9,13},{10,... | collective-permute-start | bytes 196616 | tf_op jit(solution)/shard_map/ppermute | solution.py:33
  160.7 1.2 collective-permute-done.18
  161.9 1.0 collective-permute-done.16
  162.9 3.5 %collective-permute-start.19 = (f32[1,128,128]{2,1,0:T(8,128)S(1)}, f32[1,128,128]{2,1,0:T(8,128)S(1)}, u32[]{:S(2)}, u32[]{:S(2)}) collective-permute-start(f32[1,128,128]{2,1,0:T(8,128)S(1)} %pad_maximum_fusion.8), channel_id=1, source_target_pairs={{0,8},{1,9},{2,10},{3,11},{4,12},{5,13},{6,14},{7,15},{8,0},{9,1},... | collective-permute-start | bytes 196616 | tf_op jit(solution)/shard_map/ppermute | solution.py:33
  166.4 2.2 %collective-permute-done.19 = f32[1,128,128]{2,1,0:T(8,128)S(1)} collective-permute-done((f32[1,128,128]{2,1,0:T(8,128)S(1)}, f32[1,128,128]{2,1,0:T(8,128)S(1)}, u32[]{:S(2)}, u32[]{:S(2)}) %collective-permute-start.19) | collective-permute-done | bytes 65568 | tf_op jit(solution)/shard_map/ppermute | solution.py:33
  168.7 2.4 %close.1 = (f32[128,64]{1,0:T(8,128)S(1)}, f32[8,128]{1,0:T(8,128)S(1)}) custom-call(f32[128,64,128]{2,1,0:T(8,128)S(1)} %copy-done.2, f32[128,128]{1,0:T(8,128)S(1)} %fusion.8.picked_ref, f32[128,64]{1,0:T(8,128)S(1)} %multiply_add_fusion.base_ref, f32[128,64]{1,0:T(8,128)S(1)} %reshape.203.values_ref.rhs_ref, f32[128,64]{1,0:T(8,128)S(1)} %get-tuple-element.45.first_ref, ...), custom_call_target="tpu_custom_call" | custom-call | flops 4194304 | bytes 4194304 | tf_op jit(solution)/shard_map/close/pallas_call | solution.py:672
  171.7 13.1 %all_to_all.5 = f32[16,8,128]{2,1,0:T(8,128)S(1)} all-to-all(f32[16,8,128]{2,1,0:T(8,128)S(1)} %broadcast_in_dim.39), channel_id=1, replica_groups=mesh['groups'=2,'px'=16] {'px'}, dimensions={0} | all-to-all | bytes 131072 | tf_op jit(solution)/shard_map/all_to_all | solution.py:71
  185.4 1.9 %finish.1 = (f32[64,128]{1,0:T(8,128)}, f32[64,128]{1,0:T(8,128)}) custom-call(f32[128,64]{1,0:T(8,128)} %copy-done.5, f32[128,64]{1,0:T(8,128)} %copy-done.6, f32[128,64]{1,0:T(8,128)} %copy-done.8, f32[1,128]{1,0:T(1,128)} %copy-done.9, f32[8,128]{1,0:T(8,128)} %reduce_sum.49.last_ref), custom_call_target="tpu_custom_call" | custom-call | tf_op jit(solution)/shard_map/finish/pallas_call | solution.py:757
  (102 shorter events, 10.9 us)
Async XLA Ops:
  0.6 10.7 %copy-start.16 = (f32[136]{0:T(256)S(1)}, f32[136]{0:T(256)}, u32[]{:S(2)}) copy-start(f32[136]{0:T(256)} %constant.220.clone) | copy-start | bytes 1636
  1.5 167.2 %copy-start.5 = (f32[128,64]{1,0:T(8,128)}, f32[128,64]{1,0:T(8,128)S(1)}, u32[]{:S(2)}) copy-start(f32[128,64]{1,0:T(8,128)S(1)} %reshape.203.values_ref.rhs_ref) | copy-start | bytes 98308
  2.2 2.2 %copy-start = (f32[128,64,128]{2,1,0:T(8,128)S(1)}, f32[128,64,128]{2,1,0:T(8,128)}, u32[]{:S(2)}) copy-start(f32[128,64,128]{2,1,0:T(8,128)} %proj_ref.5) | copy-start | bytes 12582916
  4.4 17.5 %copy-start.7 = (bf16[768,256]{1,0:T(8,128)(2,1)S(1)}, bf16[768,256]{1,0:T(8,128)(2,1)}, u32[]{:S(2)}) copy-start(bf16[768,256]{1,0:T(8,128)(2,1)} %constant.208.clone.sort_ref) | copy-start | bytes 1179652
  5.9 8.4 %collective-permute-start = (f32[1,168,128]{2,0,1:T(1,128)S(1)}, f32[1,168,128]{2,0,1:T(1,128)S(1)}, u32[]{:S(2)}, u32[]{:S(2)}) collective-permute-start(f32[1,168,128]{2,0,1:T(1,128)S(1)} %bitcast.72), channel_id=1, source_target_pairs={{0,8},{1,9},{2,10},{3,11},{4,12},{5,13},{6,14},{7,15},{8,0},{9,1},... | collective-permute-start | bytes 258056 | tf_op jit(solution)/shard_map/ppermute | solution.py:33
  14.5 5.5 %collective-permute-start.1 = (f32[2,168,128]{2,0,1:T(2,128)S(1)}, f32[2,168,128]{2,0,1:T(2,128)S(1)}, u32[]{:S(2)}, u32[]{:S(2)}) collective-permute-start(f32[2,168,128]{2,0,1:T(2,128)S(1)} %pad_maximum_fusion.4), channel_id=1, source_target_pairs={{0,4},{1,5},{2,6},{3,7},{4,0},{5,1},{6,2},{7,3},{8,12},{9,13},{10,... | collective-permute-start | bytes 516104 | tf_op jit(solution)/shard_map/ppermute | solution.py:33
  20.1 12.4 %collective-permute-start.2 = (f32[4,168,128]{2,0,1:T(4,128)S(1)}, f32[4,168,128]{2,0,1:T(4,128)S(1)}, u32[]{:S(2)}, u32[]{:S(2)}) collective-permute-start(f32[4,168,128]{2,0,1:T(4,128)S(1)} %pad_maximum_fusion.2), channel_id=1, source_target_pairs={{0,2},{1,3},{2,0},{3,1},{4,6},{5,7},{6,4},{7,5},{8,10},{9,11},{10,... | collective-permute-start | bytes 1032200 | tf_op jit(solution)/shard_map/ppermute | solution.py:33
  21.8 2.2 %copy-start.4 = (f32[256,16,256]{2,1,0:T(8,128)S(1)}, f32[256,16,256]{2,1,0:T(8,128)}, u32[]{:S(2)}) copy-start(f32[256,16,256]{2,1,0:T(8,128)} %param.28) | copy-start | bytes 12582916
  24.0 0.6 copy-start.10
  31.2 1.3 copy-start.3
  32.8 3.8 %copy-start.12 = (f32[8,168,128]{2,1,0:T(8,128)}, f32[8,168,128]{2,1,0:T(8,128)S(1)}, u32[]{:S(2)}) copy-start(f32[8,168,128]{2,1,0:T(8,128)S(1)} %copy.31.refs_0_) | copy-start | bytes 2064388
  32.8 2.2 %collective-permute-start.3 = (f32[8,168,128]{2,1,0:T(8,128)S(1)}, f32[8,168,128]{2,1,0:T(8,128)S(1)}, u32[]{:S(2)}, u32[]{:S(2)}) collective-permute-start(f32[8,168,128]{2,1,0:T(8,128)S(1)} %copy.31.refs_0_), channel_id=1, source_target_pairs={{0,1},{1,0},{2,3},{3,2},{4,5},{5,4},{6,7},{7,6},{8,9},{9,8},{10,11... | collective-permute-start | bytes 2064392 | tf_op jit(solution)/shard_map/ppermute | solution.py:33
  35.0 1.5 copy-start.13
  36.6 32.9 %copy-start.17 = (s32[128,2]{0,1:T(2,128)S(1)}, s32[128,2]{0,1:T(2,128)}, u32[]{:S(2)}) copy-start(s32[128,2]{0,1:T(2,128)} %param.26) | copy-start | bytes 3076
  36.6 33.1 %copy-start.15 = (f32[8192]{0:T(1024)S(1)}, f32[8192]{0:T(1024)}, u32[]{:S(2)}) copy-start(f32[8192]{0:T(1024)} %param.22) | copy-start | bytes 98308
  69.2 2.2 %collective-permute-start.4 = (f32[2,8,64,128]{3,2,1,0:T(8,128)}, f32[2,8,64,128]{3,2,1,0:T(8,128)S(1)}, u32[]{:S(2)}, u32[]{:S(2)}) collective-permute-start(f32[2,8,64,128]{3,2,1,0:T(8,128)} %get-tuple-element.41), channel_id=1, source_target_pairs={{0,1},{1,0},{2,3},{3,2},{4,5},{5,4},{6,7},{7,6},{8,9},{9,8},{10,11... | collective-permute-start | bytes 1572872 | tf_op jit(solution)/shard_map/ppermute | solution.py:33
  72.6 6.4 %collective-permute-start.7 = (f32[4,64,128]{2,1,0:T(8,128)S(1)}, f32[4,64,128]{2,1,0:T(8,128)S(1)}, u32[]{:S(2)}, u32[]{:S(2)}) collective-permute-start(f32[4,64,128]{2,1,0:T(8,128)S(1)} %slice.111), channel_id=1, source_target_pairs={{0,4},{1,5},{2,6},{3,7},{4,0},{5,1},{6,2},{7,3},{8,12},{9,13},{10,... | collective-permute-start | bytes 393224 | tf_op jit(solution)/shard_map/ppermute | solution.py:33
  74.0 6.5 %collective-permute-start.5 = (f32[4,64,128]{2,1,0:T(8,128)S(1)}, f32[4,64,128]{2,1,0:T(8,128)S(1)}, u32[]{:S(2)}, u32[]{:S(2)}) collective-permute-start(f32[4,64,128]{2,1,0:T(8,128)S(1)} %slice.107), channel_id=1, source_target_pairs={{0,2},{1,3},{2,0},{3,1},{4,6},{5,7},{6,4},{7,5},{8,10},{9,11},{10,... | collective-permute-start | bytes 393224 | tf_op jit(solution)/shard_map/ppermute | solution.py:33
  75.4 15.6 %copy-start.1 = (f32[128,64,128]{2,1,0:T(8,128)S(1)}, f32[128,64,128]{2,1,0:T(8,128)}, u32[]{:S(2)}) copy-start(f32[128,64,128]{2,1,0:T(8,128)} %proj_ref.5) | copy-start | bytes 12582916
  79.0 4.3 %collective-permute-start.8 = (f32[2,64,128]{2,1,0:T(8,128)S(1)}, f32[2,64,128]{2,1,0:T(8,128)S(1)}, u32[]{:S(2)}, u32[]{:S(2)}) collective-permute-start(f32[2,64,128]{2,1,0:T(8,128)S(1)} %slice.142), channel_id=1, source_target_pairs={{0,2},{1,3},{2,0},{3,1},{4,6},{5,7},{6,4},{7,5},{8,10},{9,11},{10,... | collective-permute-start | bytes 196616 | tf_op jit(solution)/shard_map/ppermute | solution.py:33
  80.6 4.3 %collective-permute-start.6 = (f32[2,64,128]{2,1,0:T(8,128)S(1)}, f32[2,64,128]{2,1,0:T(8,128)S(1)}, u32[]{:S(2)}, u32[]{:S(2)}) collective-permute-start(f32[2,64,128]{2,1,0:T(8,128)S(1)} %slice.140), channel_id=1, source_target_pairs={{0,4},{1,5},{2,6},{3,7},{4,0},{5,1},{6,2},{7,3},{8,12},{9,13},{10,... | collective-permute-start | bytes 196616 | tf_op jit(solution)/shard_map/ppermute | solution.py:33
  84.9 6.1 %collective-permute-start.9 = (f32[1,128,128]{2,1,0:T(8,128)S(1)}, f32[1,128,128]{2,1,0:T(8,128)S(1)}, u32[]{:S(2)}, u32[]{:S(2)}) collective-permute-start(f32[1,128,128]{2,1,0:T(8,128)S(1)} %pad_maximum_fusion.9), channel_id=1, source_target_pairs={{0,8},{1,9},{2,10},{3,11},{4,12},{5,13},{6,14},{7,15},{8,0},{9,1},... | collective-permute-start | bytes 196616 | tf_op jit(solution)/shard_map/ppermute | solution.py:33
  94.2 74.4 %copy-start.6 = (f32[128,64]{1,0:T(8,128)}, f32[128,64]{1,0:T(8,128)S(1)}, u32[]{:S(2)}) copy-start(f32[128,64]{1,0:T(8,128)S(1)} %get-tuple-element.45.first_ref) | copy-start | bytes 98308
  94.2 5.8 %collective-permute-start.10 = (f32[1,168,128]{2,1,0:T(8,128)S(1)}, f32[1,168,128]{2,1,0:T(8,128)S(1)}, u32[]{:S(2)}, u32[]{:S(2)}) collective-permute-start(f32[1,168,128]{2,1,0:T(8,128)S(1)} %bitcast.68), channel_id=1, source_target_pairs={{0,8},{1,9},{2,10},{3,11},{4,12},{5,13},{6,14},{7,15},{8,0},{9,1},... | collective-permute-start | bytes 258056 | tf_op jit(solution)/shard_map/ppermute | solution.py:33
  100.0 5.5 %collective-permute-start.11 = (f32[2,168,128]{2,1,0:T(8,128)S(1)}, f32[2,168,128]{2,1,0:T(8,128)S(1)}, u32[]{:S(2)}, u32[]{:S(2)}) collective-permute-start(f32[2,168,128]{2,1,0:T(8,128)S(1)} %pad_maximum_fusion.5), channel_id=1, source_target_pairs={{0,4},{1,5},{2,6},{3,7},{4,0},{5,1},{6,2},{7,3},{8,12},{9,13},{10,... | collective-permute-start | bytes 516104 | tf_op jit(solution)/shard_map/ppermute | solution.py:33
  105.5 7.3 %collective-permute-start.12 = (f32[4,168,128]{2,1,0:T(8,128)S(1)}, f32[4,168,128]{2,1,0:T(8,128)S(1)}, u32[]{:S(2)}, u32[]{:S(2)}) collective-permute-start(f32[4,168,128]{2,1,0:T(8,128)S(1)} %pad_maximum_fusion.3), channel_id=1, source_target_pairs={{0,2},{1,3},{2,0},{3,1},{4,6},{5,7},{6,4},{7,5},{8,10},{9,11},{10,... | collective-permute-start | bytes 1032200 | tf_op jit(solution)/shard_map/ppermute | solution.py:33
  112.9 2.2 %copy-start.11 = (f32[8,168,128]{2,1,0:T(8,128)}, f32[8,168,128]{2,1,0:T(8,128)S(1)}, u32[]{:S(2)}) copy-start(f32[8,168,128]{2,1,0:T(8,128)S(1)} %pad_maximum_fusion.1.refs_0_) | copy-start | bytes 2064388
  112.9 2.2 %collective-permute-start.13 = (f32[8,168,128]{2,1,0:T(8,128)S(1)}, f32[8,168,128]{2,1,0:T(8,128)S(1)}, u32[]{:S(2)}, u32[]{:S(2)}) collective-permute-start(f32[8,168,128]{2,1,0:T(8,128)S(1)} %pad_maximum_fusion.1.refs_0_), channel_id=1, source_target_pairs={{0,1},{1,0},{2,3},{3,2},{4,5},{5,4},{6,7},{7,6},{8,9},{9,8},{10,11... | collective-permute-start | bytes 2064392 | tf_op jit(solution)/shard_map/ppermute | solution.py:33
  115.1 0.9 copy-start.14
  148.6 2.2 %collective-permute-start.14 = (f32[2,8,64,128]{3,2,1,0:T(8,128)}, f32[2,8,64,128]{3,2,1,0:T(8,128)S(1)}, u32[]{:S(2)}, u32[]{:S(2)}) collective-permute-start(f32[2,8,64,128]{3,2,1,0:T(8,128)} %get-tuple-element.48), channel_id=1, source_target_pairs={{0,1},{1,0},{2,3},{3,2},{4,5},{5,4},{6,7},{7,6},{8,9},{9,8},{10,11... | collective-permute-start | bytes 1572872 | tf_op jit(solution)/shard_map/ppermute | solution.py:33
  150.5 18.2 %copy-start.9 = (f32[1,128]{1,0:T(1,128)}, f32[1,128]{1,0:T(1,128)S(1)}, u32[]{:S(2)}) copy-start(f32[1,128]{1,0:T(1,128)S(1)} %add_bitcast_fusion.sums_ref) | copy-start | bytes 1540
  151.9 5.6 %collective-permute-start.17 = (f32[4,64,128]{2,1,0:T(8,128)S(1)}, f32[4,64,128]{2,1,0:T(8,128)S(1)}, u32[]{:S(2)}, u32[]{:S(2)}) collective-permute-start(f32[4,64,128]{2,1,0:T(8,128)S(1)} %slice.125), channel_id=1, source_target_pairs={{0,4},{1,5},{2,6},{3,7},{4,0},{5,1},{6,2},{7,3},{8,12},{9,13},{10,... | collective-permute-start | bytes 393224 | tf_op jit(solution)/shard_map/ppermute | solution.py:33
  152.0 6.6 %collective-permute-start.15 = (f32[4,64,128]{2,1,0:T(8,128)S(1)}, f32[4,64,128]{2,1,0:T(8,128)S(1)}, u32[]{:S(2)}, u32[]{:S(2)}) collective-permute-start(f32[4,64,128]{2,1,0:T(8,128)S(1)} %slice.121), channel_id=1, source_target_pairs={{0,2},{1,3},{2,0},{3,1},{4,6},{5,7},{6,4},{7,5},{8,10},{9,11},{10,... | collective-permute-start | bytes 393224 | tf_op jit(solution)/shard_map/ppermute | solution.py:33
  153.7 15.0 %copy-start.2 = (f32[128,64,128]{2,1,0:T(8,128)S(1)}, f32[128,64,128]{2,1,0:T(8,128)}, u32[]{:S(2)}) copy-start(f32[128,64,128]{2,1,0:T(8,128)} %proj_ref.5) | copy-start | bytes 12582916
  157.5 4.3 %collective-permute-start.18 = (f32[2,64,128]{2,1,0:T(8,128)S(1)}, f32[2,64,128]{2,1,0:T(8,128)S(1)}, u32[]{:S(2)}, u32[]{:S(2)}) collective-permute-start(f32[2,64,128]{2,1,0:T(8,128)S(1)} %slice.150), channel_id=1, source_target_pairs={{0,2},{1,3},{2,0},{3,1},{4,6},{5,7},{6,4},{7,5},{8,10},{9,11},{10,... | collective-permute-start | bytes 196616 | tf_op jit(solution)/shard_map/ppermute | solution.py:33
  158.6 4.3 %collective-permute-start.16 = (f32[2,64,128]{2,1,0:T(8,128)S(1)}, f32[2,64,128]{2,1,0:T(8,128)S(1)}, u32[]{:S(2)}, u32[]{:S(2)}) collective-permute-start(f32[2,64,128]{2,1,0:T(8,128)S(1)} %slice.148), channel_id=1, source_target_pairs={{0,4},{1,5},{2,6},{3,7},{4,0},{5,1},{6,2},{7,3},{8,12},{9,13},{10,... | collective-permute-start | bytes 196616 | tf_op jit(solution)/shard_map/ppermute | solution.py:33
  162.9 5.7 %collective-permute-start.19 = (f32[1,128,128]{2,1,0:T(8,128)S(1)}, f32[1,128,128]{2,1,0:T(8,128)S(1)}, u32[]{:S(2)}, u32[]{:S(2)}) collective-permute-start(f32[1,128,128]{2,1,0:T(8,128)S(1)} %pad_maximum_fusion.8), channel_id=1, source_target_pairs={{0,8},{1,9},{2,10},{3,11},{4,12},{5,13},{6,14},{7,15},{8,0},{9,1},... | collective-permute-start | bytes 196616 | tf_op jit(solution)/shard_map/ppermute | solution.py:33
  171.1 0.6 copy-start.8

commit v7 on v6

--- a/solution.py
+++ b/solution.py
@@ -189,7 +189,7 @@
                     ref[pl.ds(row, 1), :] += source[pl.ds(place, 1), :]
             return 0
 
-        lax.fori_loop(0, chunk // COPIES, add, 0, unroll=16)
+        lax.fori_loop(0, chunk // COPIES, add, 0, unroll=32)
         return 0
 
     for move in early:
@@ -221,7 +221,7 @@
                 grid_imag[place, :] = j
             return 0
 
-        lax.fori_loop(0, extent // 8, body, 0, unroll=2)
+        lax.fori_loop(0, extent // 8, body, 0, unroll=4)
 
     across(-1)
     for move in moves[4:]:
@@ -310,7 +310,7 @@
                 ref[pl.ds(i, 1), :] = source[pl.ds(row, 1), :]
             return 0
 
-        lax.fori_loop(0, chunk, take, 0, unroll=32)
+        lax.fori_loop(0, chunk, take, 0, unroll=64)
         codes, wide, cosine, sine = marks(start)
         plane = where_equal(wide, codes[:, 0:1])
         high, low = split(dense[...])

time: 188 us -> 187 us (level)
  no operation moved by 1% of the time
where the time goes in v7:
time: 187 us; the launch traced here: 186 us
  Pallas kernels  82 us (44%)
  waiting for transfers between devices  34.6 us (19%)
  starting transfers between devices  26.7 us (14%)
  other arithmetic  15.9 us (9%)
  blocking collectives  13.1 us (7%)
  local copies, waits for them, and re-layouts  12.8 us (7%)
    pallas_call x2, Pallas kernels, spectral(): pl.pallas_call(functools.partial(spectral_kernel, extent, chunk, len(oper...  64.5 us
    ppermute x20, waiting for transfers between devices, exchange(): return lax.ppermute(value, 'px', [(i, i ^ step) for i in range(members)])  34.6 us
    ppermute x20, starting transfers between devices, exchange(): return lax.ppermute(value, 'px', [(i, i ^ step) for i in range(members)])  26.7 us
    all_to_all x1, blocking collectives, total(): return jnp.sum(lax.all_to_all(copies, 'px', 0, 0), axis=0)  13.1 us
    unnamed x36, local copies, waits for them, and re-layouts  7.83 us
    pallas_call x3, Pallas kernels, local_call(): pl.pallas_call(kernel, grid=(blocks // STEP_BLOCKS,), out_shape=[jax.Shap...  7.06 us
    reduce_sum x2, other arithmetic, base_of(): jnp.sum(near_tiles * sources[:, None, :], axis=2)  7 us
    pallas_call x1, Pallas kernels, spectral_tables(): pl.pallas_call(functools.partial(filter_kernel, extent, slab), grid=(exte...  6.55 us
  transfers between devices with their start and end apart: 20, of which 16 were waited for; matrix products, arithmetic and copies ran while one was open for 8% of the time, Pallas kernels for 5%

profile of v7, /device:TPU:0, one launch (start us, length us, event | category | flops | bytes accessed | tf_op | source)
XLA Modules:
  0.0 186.5 jit_solution(10748290792310200271)
XLA Ops:
  0.6 0.8 reshape.203.values_ref.rhs_ref
  2.2 2.2 %copy-done = f32[128,64,128]{2,1,0:T(8,128)S(1)} copy-done((f32[128,64,128]{2,1,0:T(8,128)S(1)}, f32[128,64,128]{2,1,0:T(8,128)}, u32[]{:S(2)}) %copy-start) | copy-done | bytes 4194328
  4.4 1.5 project.1
  5.9 4.1 %collective-permute-start = (f32[1,168,128]{2,0,1:T(1,128)S(1)}, f32[1,168,128]{2,0,1:T(1,128)S(1)}, u32[]{:S(2)}, u32[]{:S(2)}) collective-permute-start(f32[1,168,128]{2,0,1:T(1,128)S(1)} %bitcast.72), channel_id=1, source_target_pairs={{0,8},{1,9},{2,10},{3,11},{4,12},{5,13},{6,14},{7,15},{8,0},{9,1},... | collective-permute-start | bytes 258056 | tf_op jit(solution)/shard_map/ppermute | solution.py:33
  10.0 1.3 slice.99
  11.3 0.8 fusion.5.refs_17_
  12.1 2.3 %collective-permute-done = f32[1,168,128]{2,0,1:T(1,128)S(1)} collective-permute-done((f32[1,168,128]{2,0,1:T(1,128)S(1)}, f32[1,168,128]{2,0,1:T(1,128)S(1)}, u32[]{:S(2)}, u32[]{:S(2)}) %collective-permute-start) | collective-permute-done | bytes 86048 | tf_op jit(solution)/shard_map/ppermute | solution.py:33
  14.5 0.8 collective-permute-start.1
  15.9 2.1 %tables.1 = (bf16[384,512]{1,0:T(8,128)(2,1)}, bf16[1536,128]{1,0:T(8,128)(2,1)}, bf16[64,256]{1,0:T(8,128)(2,1)}) custom-call(s32[2]{0:T(128)} %pad_add_fusion.place_ref), custom_call_target="tpu_custom_call" | custom-call | bytes 8388608 | tf_op jit(solution)/shard_map/tables/pallas_call | solution.py:465
  17.9 2.0 %collective-permute-done.1 = f32[2,168,128]{2,0,1:T(2,128)S(1)} collective-permute-done((f32[2,168,128]{2,0,1:T(2,128)S(1)}, f32[2,168,128]{2,0,1:T(2,128)S(1)}, u32[]{:S(2)}, u32[]{:S(2)}) %collective-permute-start.1) | collective-permute-done | bytes 172064 | tf_op jit(solution)/shard_map/ppermute | solution.py:33
  20.1 1.7 collective-permute-start.2
  21.8 2.2 %copy-done.4 = f32[256,16,256]{2,1,0:T(8,128)S(1)} copy-done((f32[256,16,256]{2,1,0:T(8,128)S(1)}, f32[256,16,256]{2,1,0:T(8,128)}, u32[]{:S(2)}) %copy-start.4) | copy-done | bytes 4194328
  24.6 6.5 %filters.1.refs_12_ = f32[16,256,128]{2,1,0:T(8,128)S(1)} custom-call(s32[2]{0:T(128)S(1)} %copy-done.10, f32[4096,256]{1,0:T(8,128)S(1)} %bitcast.67, bf16[768,256]{1,0:T(8,128)(2,1)S(1)} %copy-done.7), custom_call_target="tpu_custom_call" | custom-call | flops 1610612736 | bytes 8388608 | tf_op jit(solution)/shard_map/filters/pallas_call | solution.py:481
  31.2 1.3 copy-done.3
  33.1 1.9 %collective-permute-done.3.refs_1_ = f32[8,168,128]{2,1,0:T(8,128)S(1)} collective-permute-done((f32[8,168,128]{2,1,0:T(8,128)S(1)}, f32[8,168,128]{2,1,0:T(8,128)S(1)}, u32[]{:S(2)}, u32[]{:S(2)}) %collective-permute-start.3) | collective-permute-done | bytes 688160 | tf_op jit(solution)/shard_map/ppermute | solution.py:33
  36.6 32.3 %spectral.2 = (f32[2,8,64,128]{3,2,1,0:T(8,128)}, f32[2,8,64,128]{3,2,1,0:T(8,128)}) custom-call(s32[2048]{0:T(1024)} %fusion.13.rows_ref, s32[8,2048]{1,0:T(8,128)} %stack.22.codes_ref, f32[8,168,128]{2,1,0:T(8,128)} %copy-done.12, f32[8,168,128]{2,1,0:T(8,128)} %copy-done.13, bf16[384,512]{1,0:T(8,128)(2,1)} %get-tuple-element.35.refs_2_, ...), custom_call_target="tpu_custom_call" | custom-call | tf_op jit(solution)/shard_map/spectral/pallas_call | solution.py:531
  69.4 0.9 select_bitcast_fusion.3
  71.0 1.1 fusion.2
  72.2 1.4 collective-permute-start.7
  75.0 3.5 %multiply_reduce_fusion.1 = f32[128,64]{1,0:T(8,128)S(1)} fusion(f32[128,64,128]{2,1,0:T(8,128)} %param.27, f32[128,128]{1,0:T(8,128)S(1)} %mul.61), kind=kLoop, calls=%fused_computation.3 | loop fusion | flops 2088960 | bytes 4292608 | tf_op jit(solution)/shard_map/reduce_sum | solution.py:723
  78.6 1.5 collective-permute-start.8
  80.9 2.0 %collective-permute-done.8 = f32[2,64,128]{2,1,0:T(8,128)S(1)} collective-permute-done((f32[2,64,128]{2,1,0:T(8,128)S(1)}, f32[2,64,128]{2,1,0:T(8,128)S(1)}, u32[]{:S(2)}, u32[]{:S(2)}) %collective-permute-start.8) | collective-permute-done | bytes 65568 | tf_op jit(solution)/shard_map/ppermute | solution.py:33
  82.9 1.6 collective-permute-done.6
  84.5 3.8 %collective-permute-start.9 = (f32[1,128,128]{2,1,0:T(8,128)S(1)}, f32[1,128,128]{2,1,0:T(8,128)S(1)}, u32[]{:S(2)}, u32[]{:S(2)}) collective-permute-start(f32[1,128,128]{2,1,0:T(8,128)S(1)} %pad_maximum_fusion.9), channel_id=1, source_target_pairs={{0,8},{1,9},{2,10},{3,11},{4,12},{5,13},{6,14},{7,15},{8,0},{9,1},... | collective-permute-start | bytes 196616 | tf_op jit(solution)/shard_map/ppermute | solution.py:33
  88.4 2.3 %collective-permute-done.9 = f32[1,128,128]{2,1,0:T(8,128)S(1)} collective-permute-done((f32[1,128,128]{2,1,0:T(8,128)S(1)}, f32[1,128,128]{2,1,0:T(8,128)S(1)}, u32[]{:S(2)}, u32[]{:S(2)}) %collective-permute-start.9) | collective-permute-done | bytes 65568 | tf_op jit(solution)/shard_map/ppermute | solution.py:33
  90.7 3.2 %complete.1 = (f32[128,64]{1,0:T(8,128)S(1)}, f32[168,128]{1,0:T(8,128)S(1)}) custom-call(f32[128,64,128]{2,1,0:T(8,128)S(1)} %copy-done.1, f32[128,128]{1,0:T(8,128)S(1)} %fusion.11.picked_ref, f32[128,64]{1,0:T(8,128)S(1)} %multiply_add_fusion.1.base_ref, f32[128,64]{1,0:T(8,128)S(1)} %reshape.203.values_ref.rhs_ref), custom_call_target="tpu_custom_call" | custom-call | flops 4194304 | bytes 4194304 | tf_op jit(solution)/shard_map/complete/pallas_call | solution.py:672
  93.8 2.9 %collective-permute-start.10 = (f32[1,168,128]{2,1,0:T(8,128)S(1)}, f32[1,168,128]{2,1,0:T(8,128)S(1)}, u32[]{:S(2)}, u32[]{:S(2)}) collective-permute-start(f32[1,168,128]{2,1,0:T(8,128)S(1)} %bitcast.68), channel_id=1, source_target_pairs={{0,8},{1,9},{2,10},{3,11},{4,12},{5,13},{6,14},{7,15},{8,0},{9,1},... | collective-permute-start | bytes 258056 | tf_op jit(solution)/shard_map/ppermute | solution.py:33
  96.8 2.8 %collective-permute-done.10 = f32[1,168,128]{2,1,0:T(8,128)S(1)} collective-permute-done((f32[1,168,128]{2,1,0:T(8,128)S(1)}, f32[1,168,128]{2,1,0:T(8,128)S(1)}, u32[]{:S(2)}, u32[]{:S(2)}) %collective-permute-start.10) | collective-permute-done | bytes 86048 | tf_op jit(solution)/shard_map/ppermute | solution.py:33
  99.7 5.4 %collective-permute-done.11 = f32[2,168,128]{2,1,0:T(8,128)S(1)} collective-permute-done((f32[2,168,128]{2,1,0:T(8,128)S(1)}, f32[2,168,128]{2,1,0:T(8,128)S(1)}, u32[]{:S(2)}, u32[]{:S(2)}) %collective-permute-start.11) | collective-permute-done | bytes 172064 | tf_op jit(solution)/shard_map/ppermute | solution.py:33
  105.1 0.9 collective-permute-start.12
  106.0 6.4 %collective-permute-done.12 = f32[4,168,128]{2,1,0:T(8,128)S(1)} collective-permute-done((f32[4,168,128]{2,1,0:T(8,128)S(1)}, f32[4,168,128]{2,1,0:T(8,128)S(1)}, u32[]{:S(2)}, u32[]{:S(2)}) %collective-permute-start.12) | collective-permute-done | bytes 344096 | tf_op jit(solution)/shard_map/ppermute | solution.py:33
  112.6 2.1 %collective-permute-done.13.refs_1_ = f32[8,168,128]{2,1,0:T(8,128)S(1)} collective-permute-done((f32[8,168,128]{2,1,0:T(8,128)S(1)}, f32[8,168,128]{2,1,0:T(8,128)S(1)}, u32[]{:S(2)}, u32[]{:S(2)}) %collective-permute-start.13) | collective-permute-done | bytes 688160 | tf_op jit(solution)/shard_map/ppermute | solution.py:33
  114.7 0.8 copy-done.14
  115.6 32.2 %spectral.3 = (f32[2,8,64,128]{3,2,1,0:T(8,128)}, f32[2,8,64,128]{3,2,1,0:T(8,128)}) custom-call(s32[2048]{0:T(1024)} %fusion.13.rows_ref, s32[8,2048]{1,0:T(8,128)} %stack.22.codes_ref, f32[8,168,128]{2,1,0:T(8,128)} %copy-done.11, f32[8,168,128]{2,1,0:T(8,128)} %copy-done.14, bf16[384,512]{1,0:T(8,128)(2,1)} %get-tuple-element.35.refs_2_, ...), custom_call_target="tpu_custom_call" | custom-call | tf_op jit(solution)/shard_map/spectral/pallas_call | solution.py:531
  148.0 0.9 select_bitcast_fusion.1
  148.9 0.8 slice_reduce_fusion
  150.0 1.1 fusion
  151.2 0.9 collective-permute-start.15
  152.9 3.5 %multiply_reduce_fusion = f32[128,64]{1,0:T(8,128)S(1)} fusion(f32[128,64,128]{2,1,0:T(8,128)} %param.27, f32[128,128]{1,0:T(8,128)S(1)} %mul.65), kind=kLoop, calls=%fused_computation.2 | loop fusion | flops 2088960 | bytes 4292608 | tf_op jit(solution)/shard_map/reduce_sum | solution.py:723
  156.7 1.0 collective-permute-start.18
  157.8 2.1 %collective-permute-start.16 = (f32[2,64,128]{2,1,0:T(8,128)S(1)}, f32[2,64,128]{2,1,0:T(8,128)S(1)}, u32[]{:S(2)}, u32[]{:S(2)}) collective-permute-start(f32[2,64,128]{2,1,0:T(8,128)S(1)} %slice.148), channel_id=1, source_target_pairs={{0,4},{1,5},{2,6},{3,7},{4,0},{5,1},{6,2},{7,3},{8,12},{9,13},{10,... | collective-permute-start | bytes 196616 | tf_op jit(solution)/shard_map/ppermute | solution.py:33
  159.8 1.2 collective-permute-done.18
  161.1 1.0 collective-permute-done.16
  162.1 3.5 %collective-permute-start.19 = (f32[1,128,128]{2,1,0:T(8,128)S(1)}, f32[1,128,128]{2,1,0:T(8,128)S(1)}, u32[]{:S(2)}, u32[]{:S(2)}) collective-permute-start(f32[1,128,128]{2,1,0:T(8,128)S(1)} %pad_maximum_fusion.8), channel_id=1, source_target_pairs={{0,8},{1,9},{2,10},{3,11},{4,12},{5,13},{6,14},{7,15},{8,0},{9,1},... | collective-permute-start | bytes 196616 | tf_op jit(solution)/shard_map/ppermute | solution.py:33
  165.6 2.2 %collective-permute-done.19 = f32[1,128,128]{2,1,0:T(8,128)S(1)} collective-permute-done((f32[1,128,128]{2,1,0:T(8,128)S(1)}, f32[1,128,128]{2,1,0:T(8,128)S(1)}, u32[]{:S(2)}, u32[]{:S(2)}) %collective-permute-start.19) | collective-permute-done | bytes 65568 | tf_op jit(solution)/shard_map/ppermute | solution.py:33
  167.9 2.4 %close.1 = (f32[128,64]{1,0:T(8,128)S(1)}, f32[8,128]{1,0:T(8,128)S(1)}) custom-call(f32[128,64,128]{2,1,0:T(8,128)S(1)} %copy-done.2, f32[128,128]{1,0:T(8,128)S(1)} %fusion.8.picked_ref, f32[128,64]{1,0:T(8,128)S(1)} %multiply_add_fusion.base_ref, f32[128,64]{1,0:T(8,128)S(1)} %reshape.203.values_ref.rhs_ref, f32[128,64]{1,0:T(8,128)S(1)} %get-tuple-element.45.first_ref, ...), custom_call_target="tpu_custom_call" | custom-call | flops 4194304 | bytes 4194304 | tf_op jit(solution)/shard_map/close/pallas_call | solution.py:672
  170.9 13.1 %all_to_all.5 = f32[16,8,128]{2,1,0:T(8,128)S(1)} all-to-all(f32[16,8,128]{2,1,0:T(8,128)S(1)} %broadcast_in_dim.39), channel_id=1, replica_groups=mesh['groups'=2,'px'=16] {'px'}, dimensions={0} | all-to-all | bytes 131072 | tf_op jit(solution)/shard_map/all_to_all | solution.py:71
  184.6 1.9 %finish.1 = (f32[64,128]{1,0:T(8,128)}, f32[64,128]{1,0:T(8,128)}) custom-call(f32[128,64]{1,0:T(8,128)} %copy-done.5, f32[128,64]{1,0:T(8,128)} %copy-done.6, f32[128,64]{1,0:T(8,128)} %copy-done.8, f32[1,128]{1,0:T(1,128)} %copy-done.9, f32[8,128]{1,0:T(8,128)} %reduce_sum.49.last_ref), custom_call_target="tpu_custom_call" | custom-call | tf_op jit(solution)/shard_map/finish/pallas_call | solution.py:757
  (102 shorter events, 10.9 us)
Async XLA Ops:
  0.6 10.7 %copy-start.16 = (f32[136]{0:T(256)S(1)}, f32[136]{0:T(256)}, u32[]{:S(2)}) copy-start(f32[136]{0:T(256)} %constant.220.clone) | copy-start | bytes 1636
  1.5 166.4 %copy-start.5 = (f32[128,64]{1,0:T(8,128)}, f32[128,64]{1,0:T(8,128)S(1)}, u32[]{:S(2)}) copy-start(f32[128,64]{1,0:T(8,128)S(1)} %reshape.203.values_ref.rhs_ref) | copy-start | bytes 98308
  2.2 2.2 %copy-start = (f32[128,64,128]{2,1,0:T(8,128)S(1)}, f32[128,64,128]{2,1,0:T(8,128)}, u32[]{:S(2)}) copy-start(f32[128,64,128]{2,1,0:T(8,128)} %proj_ref.5) | copy-start | bytes 12582916
  4.4 17.5 %copy-start.7 = (bf16[768,256]{1,0:T(8,128)(2,1)S(1)}, bf16[768,256]{1,0:T(8,128)(2,1)}, u32[]{:S(2)}) copy-start(bf16[768,256]{1,0:T(8,128)(2,1)} %constant.208.clone.sort_ref) | copy-start | bytes 1179652
  5.9 8.4 %collective-permute-start = (f32[1,168,128]{2,0,1:T(1,128)S(1)}, f32[1,168,128]{2,0,1:T(1,128)S(1)}, u32[]{:S(2)}, u32[]{:S(2)}) collective-permute-start(f32[1,168,128]{2,0,1:T(1,128)S(1)} %bitcast.72), channel_id=1, source_target_pairs={{0,8},{1,9},{2,10},{3,11},{4,12},{5,13},{6,14},{7,15},{8,0},{9,1},... | collective-permute-start | bytes 258056 | tf_op jit(solution)/shard_map/ppermute | solution.py:33
  14.5 5.5 %collective-permute-start.1 = (f32[2,168,128]{2,0,1:T(2,128)S(1)}, f32[2,168,128]{2,0,1:T(2,128)S(1)}, u32[]{:S(2)}, u32[]{:S(2)}) collective-permute-start(f32[2,168,128]{2,0,1:T(2,128)S(1)} %pad_maximum_fusion.4), channel_id=1, source_target_pairs={{0,4},{1,5},{2,6},{3,7},{4,0},{5,1},{6,2},{7,3},{8,12},{9,13},{10,... | collective-permute-start | bytes 516104 | tf_op jit(solution)/shard_map/ppermute | solution.py:33
  20.1 12.4 %collective-permute-start.2 = (f32[4,168,128]{2,0,1:T(4,128)S(1)}, f32[4,168,128]{2,0,1:T(4,128)S(1)}, u32[]{:S(2)}, u32[]{:S(2)}) collective-permute-start(f32[4,168,128]{2,0,1:T(4,128)S(1)} %pad_maximum_fusion.2), channel_id=1, source_target_pairs={{0,2},{1,3},{2,0},{3,1},{4,6},{5,7},{6,4},{7,5},{8,10},{9,11},{10,... | collective-permute-start | bytes 1032200 | tf_op jit(solution)/shard_map/ppermute | solution.py:33
  21.8 2.2 %copy-start.4 = (f32[256,16,256]{2,1,0:T(8,128)S(1)}, f32[256,16,256]{2,1,0:T(8,128)}, u32[]{:S(2)}) copy-start(f32[256,16,256]{2,1,0:T(8,128)} %param.28) | copy-start | bytes 12582916
  24.0 0.6 copy-start.10
  31.2 1.3 copy-start.3
  32.8 3.8 %copy-start.12 = (f32[8,168,128]{2,1,0:T(8,128)}, f32[8,168,128]{2,1,0:T(8,128)S(1)}, u32[]{:S(2)}) copy-start(f32[8,168,128]{2,1,0:T(8,128)S(1)} %copy.31.refs_0_) | copy-start | bytes 2064388
  32.8 2.2 %collective-permute-start.3 = (f32[8,168,128]{2,1,0:T(8,128)S(1)}, f32[8,168,128]{2,1,0:T(8,128)S(1)}, u32[]{:S(2)}, u32[]{:S(2)}) collective-permute-start(f32[8,168,128]{2,1,0:T(8,128)S(1)} %copy.31.refs_0_), channel_id=1, source_target_pairs={{0,1},{1,0},{2,3},{3,2},{4,5},{5,4},{6,7},{7,6},{8,9},{9,8},{10,11... | collective-permute-start | bytes 2064392 | tf_op jit(solution)/shard_map/ppermute | solution.py:33
  35.0 1.5 copy-start.13
  36.6 32.5 %copy-start.17 = (s32[128,2]{0,1:T(2,128)S(1)}, s32[128,2]{0,1:T(2,128)}, u32[]{:S(2)}) copy-start(s32[128,2]{0,1:T(2,128)} %param.26) | copy-start | bytes 3076
  36.6 32.7 %copy-start.15 = (f32[8192]{0:T(1024)S(1)}, f32[8192]{0:T(1024)}, u32[]{:S(2)}) copy-start(f32[8192]{0:T(1024)} %param.22) | copy-start | bytes 98308
  68.8 2.2 %collective-permute-start.4 = (f32[2,8,64,128]{3,2,1,0:T(8,128)}, f32[2,8,64,128]{3,2,1,0:T(8,128)S(1)}, u32[]{:S(2)}, u32[]{:S(2)}) collective-permute-start(f32[2,8,64,128]{3,2,1,0:T(8,128)} %get-tuple-element.41), channel_id=1, source_target_pairs={{0,1},{1,0},{2,3},{3,2},{4,5},{5,4},{6,7},{7,6},{8,9},{9,8},{10,11... | collective-permute-start | bytes 1572872 | tf_op jit(solution)/shard_map/ppermute | solution.py:33
  72.2 6.4 %collective-permute-start.7 = (f32[4,64,128]{2,1,0:T(8,128)S(1)}, f32[4,64,128]{2,1,0:T(8,128)S(1)}, u32[]{:S(2)}, u32[]{:S(2)}) collective-permute-start(f32[4,64,128]{2,1,0:T(8,128)S(1)} %slice.111), channel_id=1, source_target_pairs={{0,4},{1,5},{2,6},{3,7},{4,0},{5,1},{6,2},{7,3},{8,12},{9,13},{10,... | collective-permute-start | bytes 393224 | tf_op jit(solution)/shard_map/ppermute | solution.py:33
  73.6 6.5 %collective-permute-start.5 = (f32[4,64,128]{2,1,0:T(8,128)S(1)}, f32[4,64,128]{2,1,0:T(8,128)S(1)}, u32[]{:S(2)}, u32[]{:S(2)}) collective-permute-start(f32[4,64,128]{2,1,0:T(8,128)S(1)} %slice.107), channel_id=1, source_target_pairs={{0,2},{1,3},{2,0},{3,1},{4,6},{5,7},{6,4},{7,5},{8,10},{9,11},{10,... | collective-permute-start | bytes 393224 | tf_op jit(solution)/shard_map/ppermute | solution.py:33
  75.0 15.6 %copy-start.1 = (f32[128,64,128]{2,1,0:T(8,128)S(1)}, f32[128,64,128]{2,1,0:T(8,128)}, u32[]{:S(2)}) copy-start(f32[128,64,128]{2,1,0:T(8,128)} %proj_ref.5) | copy-start | bytes 12582916
  78.6 4.3 %collective-permute-start.8 = (f32[2,64,128]{2,1,0:T(8,128)S(1)}, f32[2,64,128]{2,1,0:T(8,128)S(1)}, u32[]{:S(2)}, u32[]{:S(2)}) collective-permute-start(f32[2,64,128]{2,1,0:T(8,128)S(1)} %slice.142), channel_id=1, source_target_pairs={{0,2},{1,3},{2,0},{3,1},{4,6},{5,7},{6,4},{7,5},{8,10},{9,11},{10,... | collective-permute-start | bytes 196616 | tf_op jit(solution)/shard_map/ppermute | solution.py:33
  80.2 4.3 %collective-permute-start.6 = (f32[2,64,128]{2,1,0:T(8,128)S(1)}, f32[2,64,128]{2,1,0:T(8,128)S(1)}, u32[]{:S(2)}, u32[]{:S(2)}) collective-permute-start(f32[2,64,128]{2,1,0:T(8,128)S(1)} %slice.140), channel_id=1, source_target_pairs={{0,4},{1,5},{2,6},{3,7},{4,0},{5,1},{6,2},{7,3},{8,12},{9,13},{10,... | collective-permute-start | bytes 196616 | tf_op jit(solution)/shard_map/ppermute | solution.py:33
  84.5 6.1 %collective-permute-start.9 = (f32[1,128,128]{2,1,0:T(8,128)S(1)}, f32[1,128,128]{2,1,0:T(8,128)S(1)}, u32[]{:S(2)}, u32[]{:S(2)}) collective-permute-start(f32[1,128,128]{2,1,0:T(8,128)S(1)} %pad_maximum_fusion.9), channel_id=1, source_target_pairs={{0,8},{1,9},{2,10},{3,11},{4,12},{5,13},{6,14},{7,15},{8,0},{9,1},... | collective-permute-start | bytes 196616 | tf_op jit(solution)/shard_map/ppermute | solution.py:33
  93.8 74.0 %copy-start.6 = (f32[128,64]{1,0:T(8,128)}, f32[128,64]{1,0:T(8,128)S(1)}, u32[]{:S(2)}) copy-start(f32[128,64]{1,0:T(8,128)S(1)} %get-tuple-element.45.first_ref) | copy-start | bytes 98308
  93.8 5.8 %collective-permute-start.10 = (f32[1,168,128]{2,1,0:T(8,128)S(1)}, f32[1,168,128]{2,1,0:T(8,128)S(1)}, u32[]{:S(2)}, u32[]{:S(2)}) collective-permute-start(f32[1,168,128]{2,1,0:T(8,128)S(1)} %bitcast.68), channel_id=1, source_target_pairs={{0,8},{1,9},{2,10},{3,11},{4,12},{5,13},{6,14},{7,15},{8,0},{9,1},... | collective-permute-start | bytes 258056 | tf_op jit(solution)/shard_map/ppermute | solution.py:33
  99.6 5.5 %collective-permute-start.11 = (f32[2,168,128]{2,1,0:T(8,128)S(1)}, f32[2,168,128]{2,1,0:T(8,128)S(1)}, u32[]{:S(2)}, u32[]{:S(2)}) collective-permute-start(f32[2,168,128]{2,1,0:T(8,128)S(1)} %pad_maximum_fusion.5), channel_id=1, source_target_pairs={{0,4},{1,5},{2,6},{3,7},{4,0},{5,1},{6,2},{7,3},{8,12},{9,13},{10,... | collective-permute-start | bytes 516104 | tf_op jit(solution)/shard_map/ppermute | solution.py:33
  105.1 7.3 %collective-permute-start.12 = (f32[4,168,128]{2,1,0:T(8,128)S(1)}, f32[4,168,128]{2,1,0:T(8,128)S(1)}, u32[]{:S(2)}, u32[]{:S(2)}) collective-permute-start(f32[4,168,128]{2,1,0:T(8,128)S(1)} %pad_maximum_fusion.3), channel_id=1, source_target_pairs={{0,2},{1,3},{2,0},{3,1},{4,6},{5,7},{6,4},{7,5},{8,10},{9,11},{10,... | collective-permute-start | bytes 1032200 | tf_op jit(solution)/shard_map/ppermute | solution.py:33
  112.5 2.2 %copy-start.11 = (f32[8,168,128]{2,1,0:T(8,128)}, f32[8,168,128]{2,1,0:T(8,128)S(1)}, u32[]{:S(2)}) copy-start(f32[8,168,128]{2,1,0:T(8,128)S(1)} %pad_maximum_fusion.1.refs_0_) | copy-start | bytes 2064388
  112.5 2.2 %collective-permute-start.13 = (f32[8,168,128]{2,1,0:T(8,128)S(1)}, f32[8,168,128]{2,1,0:T(8,128)S(1)}, u32[]{:S(2)}, u32[]{:S(2)}) collective-permute-start(f32[8,168,128]{2,1,0:T(8,128)S(1)} %pad_maximum_fusion.1.refs_0_), channel_id=1, source_target_pairs={{0,1},{1,0},{2,3},{3,2},{4,5},{5,4},{6,7},{7,6},{8,9},{9,8},{10,11... | collective-permute-start | bytes 2064392 | tf_op jit(solution)/shard_map/ppermute | solution.py:33
  114.7 0.9 copy-start.14
  147.8 2.2 %collective-permute-start.14 = (f32[2,8,64,128]{3,2,1,0:T(8,128)}, f32[2,8,64,128]{3,2,1,0:T(8,128)S(1)}, u32[]{:S(2)}, u32[]{:S(2)}) collective-permute-start(f32[2,8,64,128]{3,2,1,0:T(8,128)} %get-tuple-element.48), channel_id=1, source_target_pairs={{0,1},{1,0},{2,3},{3,2},{4,5},{5,4},{6,7},{7,6},{8,9},{9,8},{10,11... | collective-permute-start | bytes 1572872 | tf_op jit(solution)/shard_map/ppermute | solution.py:33
  149.7 18.2 %copy-start.9 = (f32[1,128]{1,0:T(1,128)}, f32[1,128]{1,0:T(1,128)S(1)}, u32[]{:S(2)}) copy-start(f32[1,128]{1,0:T(1,128)S(1)} %add_bitcast_fusion.sums_ref) | copy-start | bytes 1540
  151.1 5.6 %collective-permute-start.17 = (f32[4,64,128]{2,1,0:T(8,128)S(1)}, f32[4,64,128]{2,1,0:T(8,128)S(1)}, u32[]{:S(2)}, u32[]{:S(2)}) collective-permute-start(f32[4,64,128]{2,1,0:T(8,128)S(1)} %slice.125), channel_id=1, source_target_pairs={{0,4},{1,5},{2,6},{3,7},{4,0},{5,1},{6,2},{7,3},{8,12},{9,13},{10,... | collective-permute-start | bytes 393224 | tf_op jit(solution)/shard_map/ppermute | solution.py:33
  151.2 6.6 %collective-permute-start.15 = (f32[4,64,128]{2,1,0:T(8,128)S(1)}, f32[4,64,128]{2,1,0:T(8,128)S(1)}, u32[]{:S(2)}, u32[]{:S(2)}) collective-permute-start(f32[4,64,128]{2,1,0:T(8,128)S(1)} %slice.121), channel_id=1, source_target_pairs={{0,2},{1,3},{2,0},{3,1},{4,6},{5,7},{6,4},{7,5},{8,10},{9,11},{10,... | collective-permute-start | bytes 393224 | tf_op jit(solution)/shard_map/ppermute | solution.py:33
  152.9 15.0 %copy-start.2 = (f32[128,64,128]{2,1,0:T(8,128)S(1)}, f32[128,64,128]{2,1,0:T(8,128)}, u32[]{:S(2)}) copy-start(f32[128,64,128]{2,1,0:T(8,128)} %proj_ref.5) | copy-start | bytes 12582916
  156.7 4.3 %collective-permute-start.18 = (f32[2,64,128]{2,1,0:T(8,128)S(1)}, f32[2,64,128]{2,1,0:T(8,128)S(1)}, u32[]{:S(2)}, u32[]{:S(2)}) collective-permute-start(f32[2,64,128]{2,1,0:T(8,128)S(1)} %slice.150), channel_id=1, source_target_pairs={{0,2},{1,3},{2,0},{3,1},{4,6},{5,7},{6,4},{7,5},{8,10},{9,11},{10,... | collective-permute-start | bytes 196616 | tf_op jit(solution)/shard_map/ppermute | solution.py:33
  157.8 4.3 %collective-permute-start.16 = (f32[2,64,128]{2,1,0:T(8,128)S(1)}, f32[2,64,128]{2,1,0:T(8,128)S(1)}, u32[]{:S(2)}, u32[]{:S(2)}) collective-permute-start(f32[2,64,128]{2,1,0:T(8,128)S(1)} %slice.148), channel_id=1, source_target_pairs={{0,4},{1,5},{2,6},{3,7},{4,0},{5,1},{6,2},{7,3},{8,12},{9,13},{10,... | collective-permute-start | bytes 196616 | tf_op jit(solution)/shard_map/ppermute | solution.py:33
  162.1 5.7 %collective-permute-start.19 = (f32[1,128,128]{2,1,0:T(8,128)S(1)}, f32[1,128,128]{2,1,0:T(8,128)S(1)}, u32[]{:S(2)}, u32[]{:S(2)}) collective-permute-start(f32[1,128,128]{2,1,0:T(8,128)S(1)} %pad_maximum_fusion.8), channel_id=1, source_target_pairs={{0,8},{1,9},{2,10},{3,11},{4,12},{5,13},{6,14},{7,15},{8,0},{9,1},... | collective-permute-start | bytes 196616 | tf_op jit(solution)/shard_map/ppermute | solution.py:33
  170.3 0.6 copy-start.8
